TPU v7x, 512 devices: a whole 4x4x16 slice. The times are simulated.
512 devices in a mesh: pool: 16 (over z), row: 8 (over y, core), head: 4 (over x).
Axes of the slice: x: 4, y: 4, z: 16, core: 2. Of those that a mesh axis runs over, the one named last changes fastest.
Arguments:
- queries: bfloat16 [2048, 64, 128], P(('pool', 'row'), 'head'), may hold values from -24 to 24
- prefix_keys: bfloat16 [16, 8192, 8, 128], P('pool', 'row', 'head'), may hold values from -18 to 18
- prefix_values: bfloat16 [16, 8192, 8, 128], P('pool', 'row', 'head'), may hold values from -6 to 6
- suffix_keys: bfloat16 [2048, 64, 8, 128], P(('pool', 'row'), None, 'head'), may hold values from -18 to 18
- suffix_values: bfloat16 [2048, 64, 8, 128], P(('pool', 'row'), None, 'head'), may hold values from -6 to 6
- row_prefix: int32 [2048, 1], P(('pool', 'row')), may hold values from 0 to 15; in each aligned block of 16 rows (0 to 15, 16 to 31, ...) at most 3 rows name the same one
- owner_map: int32 [16], replicated, may hold values from 0 to 15, each once
- prefix_lengths: int32 [16], replicated, may hold values from 2048 to 8192, as said below
- suffix_lengths: int32 [2048], P(('pool', 'row')), may hold values from 1 to 64, as said below
- out_weight: bfloat16 [8192, 5120], P('head', 'row'), may hold values from -2 to 2
Outputs:
- projected: bfloat16 [2048, 5120], P(('pool', 'head'), 'row')
Inputs may be any that keep to these rules, and one draw needn't show every extreme that they name: `row_prefix`: among the rows of one index of pool and row, no prefix id is named more than 3 times, a bound that some block reaches. `owner_map`: each index of pool owns exactly one prefix id. `prefix_lengths`: every prefix holds at least a quarter of 8192 positions; the longest holds exactly 8192. `suffix_lengths`: some row has exactly 64 suffix positions.
All inputs are finite; a program needn't handle non-finite values.
Results may differ from a plain program's by a relative error of at most 0.019.
Values may be sent and summed in bfloat16 or wider, within the bound.
No kernel may reach another device: no remote copies, remote signals or barrier semaphores. Data moves between devices by JAX's collectives and lax.ppermute only.
A program may use at most 128 MiB of HBM per device.

v0:
```python
import math

import jax
import jax.numpy as jnp
from jax import lax
from jax.sharding import PartitionSpec as P

LOWEST = -1e30


def attend_block(grouped, key_rows, value_rows, visible, score_scale):
    length = key_rows.shape[0]
    block_size = math.gcd(256, length)
    head_shape = grouped.shape[:3]
    start_state = (
        jnp.zeros(grouped.shape, jnp.float32),
        jnp.full(head_shape, LOWEST, jnp.float32),
        jnp.zeros(head_shape, jnp.float32),
    )

    def advance(state, number):
        weighted, running, denominator = state
        offset = number * block_size
        key_block = lax.dynamic_slice_in_dim(key_rows, offset, block_size, 0)
        value_block = lax.dynamic_slice_in_dim(value_rows, offset, block_size, 0)
        visible_block = lax.dynamic_slice_in_dim(visible, offset, block_size, 0)
        scores = (
            jnp.einsum("nkgd,tkd->nkgt", grouped, key_block, preferred_element_type=jnp.float32)
            * score_scale
        )
        scores = jnp.where(visible_block, scores, -jnp.inf)
        updated = jnp.maximum(running, jnp.max(scores, axis=-1))
        factor = jnp.exp(running - updated)
        powers = jnp.exp(scores - updated[..., None])
        denominator = denominator * factor + jnp.sum(powers, axis=-1)
        weighted = weighted * factor[..., None] + jnp.einsum(
            "nkgt,tkd->nkgd",
            powers.astype(jnp.bfloat16),
            value_block,
            preferred_element_type=jnp.float32,
        )
        return ((weighted, updated, denominator), None)

    finished, unused = lax.scan(advance, start_state, jnp.arange(length // block_size))
    return finished


def normalize(weighted, running, denominator):
    live = denominator > 0
    safe_total = jnp.where(live, denominator, 1.0)
    block_out = jnp.where(live[..., None], weighted / safe_total[..., None], 0.0).astype(
        jnp.bfloat16
    )
    block_lse = jnp.where(live, running + jnp.log(safe_total), LOWEST)
    return (block_out, block_lse)


def reduce_parts(block_out, block_lse, along):
    top = jnp.max(block_lse, axis=along, keepdims=True)
    share = jnp.exp(block_lse - top)
    share_total = jnp.sum(share, axis=along)
    merged = jnp.sum(block_out * share[..., None], axis=along) / share_total[..., None]
    return (merged, jnp.squeeze(top, along) + jnp.log(share_total))


def body(
    queries,
    prefix_keys,
    prefix_values,
    suffix_keys,
    suffix_values,
    row_prefix,
    owner_map,
    prefix_lengths,
    suffix_lengths,
    out_weight,
):
    row_count, qheads, hdim = queries.shape
    kvheads = prefix_keys.shape[2]
    groups = qheads // kvheads
    plen_local = prefix_keys.shape[1]
    pool_count = lax.axis_size("pool")
    row_axis_count = lax.axis_size("row")
    capacity = max(2, row_count * 3 // pool_count)
    score_scale = hdim ** (-0.5)
    pool_index = lax.axis_index("pool")
    row_index = lax.axis_index("row")
    prefix_count = owner_map.shape[0]
    prefix_ids = row_prefix[:, 0]
    id_table = (prefix_ids[:, None] == jnp.arange(prefix_count, dtype=jnp.int32)[None, :]).astype(
        jnp.int32
    )
    owner_of = jnp.sum(id_table * owner_map[None, :], axis=1)
    positions = jnp.arange(row_count, dtype=jnp.int32)
    earlier_same = (owner_of[:, None] == owner_of[None, :]) & (
        positions[:, None] > positions[None, :]
    )
    position = jnp.sum(earlier_same.astype(jnp.int32), axis=1)
    slot_index = owner_of * capacity + position
    own_length = jnp.sum(jnp.where(owner_map == pool_index, prefix_lengths, 0))
    token_index = row_index * plen_local + jnp.arange(plen_local, dtype=jnp.int32)
    visible = token_index < own_length
    key_rows = prefix_keys[0]
    value_rows = prefix_values[0]
    slot_table = (
        slot_index[:, None] == jnp.arange(pool_count * capacity, dtype=jnp.int32)[None, :]
    ).astype(jnp.bfloat16)
    outgoing = jnp.einsum(
        "rs,rhd->shd", slot_table, queries, preferred_element_type=jnp.float32
    ).astype(jnp.bfloat16)
    outgoing = outgoing.reshape(pool_count, capacity, qheads, hdim)
    arrived = lax.all_to_all(outgoing, "pool", split_axis=0, concat_axis=0, tiled=True)
    flat_arrived = arrived.reshape(pool_count * capacity, qheads, hdim)
    block = lax.all_gather(flat_arrived, "row", axis=0, tiled=True)
    leading = block.shape[:-2]
    grouped = block.reshape((-1, kvheads, groups, hdim))
    weighted, running, denominator = attend_block(
        grouped, key_rows, value_rows, visible, score_scale
    )
    block_out, block_lse = normalize(weighted, running, denominator)
    block_out, block_lse = (
        block_out.reshape(leading + (qheads, hdim)),
        block_lse.reshape(leading + (qheads,)),
    )
    block_out = block_out.reshape(row_axis_count, pool_count, capacity, qheads, hdim)
    block_lse = block_lse.reshape(row_axis_count, pool_count, capacity, qheads)
    pool_dim = 1
    row_dim = 0
    block_out, block_lse = (
        lax.all_to_all(
            lax.all_to_all(
                block_out.astype(jnp.float32),
                "pool",
                split_axis=pool_dim,
                concat_axis=pool_dim,
                tiled=True,
            ),
            "row",
            split_axis=row_dim,
            concat_axis=row_dim,
            tiled=True,
        ),
        lax.all_to_all(
            lax.all_to_all(
                block_lse, "pool", split_axis=pool_dim, concat_axis=pool_dim, tiled=True
            ),
            "row",
            split_axis=row_dim,
            concat_axis=row_dim,
            tiled=True,
        ),
    )
    prefix_out, prefix_lse = reduce_parts(block_out, block_lse, row_dim)
    prefix_out = jnp.take(
        prefix_out.reshape(pool_count * capacity, qheads, hdim), slot_index, axis=0
    )
    prefix_lse = jnp.take(prefix_lse.reshape(pool_count * capacity, qheads), slot_index, axis=0)
    grouped = queries.reshape(row_count, kvheads, groups, hdim)
    suffix_scores = (
        jnp.einsum("rkgd,rtkd->rkgt", grouped, suffix_keys, preferred_element_type=jnp.float32)
        * score_scale
    )
    suffix_visible = (
        jnp.arange(suffix_keys.shape[1], dtype=jnp.int32)[None, :] < suffix_lengths[:, None]
    )
    suffix_scores = jnp.where(suffix_visible[:, None, None, :], suffix_scores, -jnp.inf)
    suffix_peak = jnp.max(suffix_scores, axis=-1)
    suffix_powers = jnp.exp(suffix_scores - suffix_peak[..., None])
    suffix_total = jnp.sum(suffix_powers, axis=-1)
    suffix_weighted = jnp.einsum(
        "rkgt,rtkd->rkgd",
        suffix_powers.astype(jnp.bfloat16),
        suffix_values,
        preferred_element_type=jnp.float32,
    )
    suffix_out = (suffix_weighted / suffix_total[..., None]).reshape(row_count, qheads, hdim)
    suffix_lse = (suffix_peak + jnp.log(suffix_total)).reshape(row_count, qheads)
    highest = jnp.maximum(prefix_lse, suffix_lse)
    prefix_share = jnp.exp(prefix_lse - highest)
    suffix_share = jnp.exp(suffix_lse - highest)
    mixed = (prefix_share[..., None] * prefix_out + suffix_share[..., None] * suffix_out) / (
        prefix_share + suffix_share
    )[..., None]
    attended = mixed.reshape(row_count, qheads * hdim).astype(jnp.bfloat16)
    terms = jnp.dot(
        lax.all_gather(attended, "row", axis=0, tiled=True),
        out_weight,
        preferred_element_type=jnp.float32,
    )
    summed = lax.psum_scatter(terms.astype(jnp.bfloat16), "head", scatter_dimension=0, tiled=True)
    return summed


def solution(mesh):
    return jax.shard_map(
        body,
        mesh=mesh,
        in_specs=(
            P(("pool", "row"), "head", None),
            P("pool", "row", "head", None),
            P("pool", "row", "head", None),
            P(("pool", "row"), None, "head", None),
            P(("pool", "row"), None, "head", None),
            P(("pool", "row"), None),
            P(),
            P(),
            P(("pool", "row")),
            P("head", "row"),
        ),
        out_specs=P(("pool", "head"), "row"),
        check_vma=False,
    )
```

profile of v0, /device:TPU:1, one launch (start us, length us, event | category | flops | bytes accessed | tf_op | source)
XLA Modules:
  0.0 410.5 jit_solution(751602916665314384)
XLA Ops:
  6.5 1.0 select_reduce_fusion
  7.6 0.2 convert_reduce_fusion
  7.7 1.2 convolution_convert_fusion
  9.0 28.2 %all_to_all.25 = bf16[16,3,16,128]{3,2,1,0:T(8,128)(2,1)} all-to-all(bf16[16,3,16,128]{3,2,1,0:T(8,128)(2,1)S(1)} %bitcast.114), channel_id=1, replica_groups=mesh['pool'=16,'row'=8,'head'=4] {'pool'}, dimensions={0} | all-to-all | bytes 393216 | tf_op jit(solution)/shard_map/all_to_all | solution.py:112
  37.2 1.3 copy.102
  38.6 1.9 copy.145
  40.5 0.7 fusion.39
  41.2 0.7 add_compare_fusion
  41.9 26.3 %all-gather.2.cloned.1.call-done = bf16[384,16,128]{2,1,0:T(8,128)(2,1)} async-done(((bf16[48,16,128]{2,1,0:T(8,128)(2,1)}), bf16[384,16,128]{2,1,0:T(8,128)(2,1)}) %all-gather.2.cloned.1.call-update) | async-done | bytes 1572880 | tf_op jit(solution)/shard_map/all_gather | solution.py:114
  68.1 3.0 copy.103
  71.1 64.7 %while.15 = (s32[]{:T(128)}, f32[384,2,8,128]{0,3,2,1:T(8,128)}, f32[384,2,8]{0,2,1:T(8,128)S(1)}, f32[384,2,8]{0,2,1:T(8,128)S(1)}, s32[4]{0:T(128)S(1)}, /*ind...) while((s32[]{:T(128)}, f32[384,2,8,128]{0,3,2,1:T(8,128)}, ...), condition=%wide.region_6.7_spmd.clone, body=%wide.region_3.6_spmd.clone.sunk | while | flops 824997888 | bytes 52561640 | solution.py:44
  71.1 0.7 dynamic_slice.33
  72.6 5.1 %bitcast_reduce_fusion.3 = (f32[384,2,8]{0,2,1:T(8,128)S(1)}, f32[2,256,384,8]{2,1,3,0:T(8,128)}) fusion(pred[256]{0:T(512)(128)(4,1)S(1)} %dynamic_slice.34, bf16[384,2,8,128]{3,0,2,1:T(8,128)(2,1)} %get-tuple-element.261, bf16[1024,2,128]{2,0,1:T(8,128)(2,1)} %get-tuple-element.260, s32[]{:T(128)S(6)} %select_n.123), kind=kOutput, calls=%fused_computation.3.clone.1 | convolution fusion | flops 407365632 | bytes 8020228 | tf_op jit(solution)/shard_map/while/body/eval_jaxpr/nkgd,tkd->nkgt/dot_general | solution.py:28
  77.7 4.3 %fusion.57 = f32[384,2,8]{0,2,1:T(8,128)S(1)} fusion(f32[2,256,384,8]{2,1,3,0:T(8,128)} %get-tuple-element.224, f32[384,2,8]{0,2,1:T(8,128)S(1)} %select_maximum_fusion.2, pred[256]{0:T(512)(128)(4,1)S(1)} %dynamic_slice.34), kind=kLoop, calls=%fused_computation.6.clone.1 | loop fusion | flops 6285312 | bytes 6340864 | tf_op jit(solution)/shard_map/while/body/eval_jaxpr/reduce_sum | solution.py:35
  82.1 0.3 copy-done.1
  82.3 3.6 bitcast_add_fusion.2
  85.9 0.7 dynamic_slice.33
  87.3 5.1 %bitcast_reduce_fusion.3 = (f32[384,2,8]{0,2,1:T(8,128)S(1)}, f32[2,256,384,8]{2,1,3,0:T(8,128)}) fusion(pred[256]{0:T(512)(128)(4,1)S(1)} %dynamic_slice.34, bf16[384,2,8,128]{3,0,2,1:T(8,128)(2,1)} %get-tuple-element.261, bf16[1024,2,128]{2,0,1:T(8,128)(2,1)} %get-tuple-element.260, s32[]{:T(128)S(6)} %select_n.123), kind=kOutput, calls=%fused_computation.3.clone.1 | convolution fusion | flops 407365632 | bytes 8020228 | tf_op jit(solution)/shard_map/while/body/eval_jaxpr/nkgd,tkd->nkgt/dot_general | solution.py:28
  92.5 4.3 %fusion.57 = f32[384,2,8]{0,2,1:T(8,128)S(1)} fusion(f32[2,256,384,8]{2,1,3,0:T(8,128)} %get-tuple-element.224, f32[384,2,8]{0,2,1:T(8,128)S(1)} %select_maximum_fusion.2, pred[256]{0:T(512)(128)(4,1)S(1)} %dynamic_slice.34), kind=kLoop, calls=%fused_computation.6.clone.1 | loop fusion | flops 6285312 | bytes 6340864 | tf_op jit(solution)/shard_map/while/body/eval_jaxpr/reduce_sum | solution.py:35
  96.8 0.3 copy-done.1
  97.1 5.5 %bitcast_add_fusion.2 = f32[384,2,8,128]{0,3,2,1:T(8,128)} fusion(f32[384,2,8,128]{0,3,2,1:T(8,128)} %get-tuple-element.242, f32[384,2,8]{0,2,1:T(8,128)S(1)} %get-tuple-element.226, pred[]{:T(512)S(6)} %compare.3, f32[2,256,384,8]{2,1,3,0:T(8,128)S(1)} %copy-done.1, f32[384,2,8]{0,2,1:T(8,128)S(1)} %select_maximum_fusion.2, ...), kind=kOutput, calls=%fused_computation.9.clone.1 | convolution fusion | flops 411303936 | bytes 12763653 | tf_op jit(solution)/shard_map/while/body/eval_jaxpr/nkgt,tkd->nkgd/dot_general | solution.py:36
  102.5 0.7 dynamic_slice.33
  104.0 5.1 %bitcast_reduce_fusion.3 = (f32[384,2,8]{0,2,1:T(8,128)S(1)}, f32[2,256,384,8]{2,1,3,0:T(8,128)}) fusion(pred[256]{0:T(512)(128)(4,1)S(1)} %dynamic_slice.34, bf16[384,2,8,128]{3,0,2,1:T(8,128)(2,1)} %get-tuple-element.261, bf16[1024,2,128]{2,0,1:T(8,128)(2,1)} %get-tuple-element.260, s32[]{:T(128)S(6)} %select_n.123), kind=kOutput, calls=%fused_computation.3.clone.1 | convolution fusion | flops 407365632 | bytes 8020228 | tf_op jit(solution)/shard_map/while/body/eval_jaxpr/nkgd,tkd->nkgt/dot_general | solution.py:28
  109.1 4.3 %fusion.57 = f32[384,2,8]{0,2,1:T(8,128)S(1)} fusion(f32[2,256,384,8]{2,1,3,0:T(8,128)} %get-tuple-element.224, f32[384,2,8]{0,2,1:T(8,128)S(1)} %select_maximum_fusion.2, pred[256]{0:T(512)(128)(4,1)S(1)} %dynamic_slice.34), kind=kLoop, calls=%fused_computation.6.clone.1 | loop fusion | flops 6285312 | bytes 6340864 | tf_op jit(solution)/shard_map/while/body/eval_jaxpr/reduce_sum | solution.py:35
  113.4 0.3 copy-done.1
  113.7 5.5 %bitcast_add_fusion.2 = f32[384,2,8,128]{0,3,2,1:T(8,128)} fusion(f32[384,2,8,128]{0,3,2,1:T(8,128)} %get-tuple-element.242, f32[384,2,8]{0,2,1:T(8,128)S(1)} %get-tuple-element.226, pred[]{:T(512)S(6)} %compare.3, f32[2,256,384,8]{2,1,3,0:T(8,128)S(1)} %copy-done.1, f32[384,2,8]{0,2,1:T(8,128)S(1)} %select_maximum_fusion.2, ...), kind=kOutput, calls=%fused_computation.9.clone.1 | convolution fusion | flops 411303936 | bytes 12763653 | tf_op jit(solution)/shard_map/while/body/eval_jaxpr/nkgt,tkd->nkgd/dot_general | solution.py:36
  119.2 0.7 dynamic_slice.33
  120.6 5.1 %bitcast_reduce_fusion.3 = (f32[384,2,8]{0,2,1:T(8,128)S(1)}, f32[2,256,384,8]{2,1,3,0:T(8,128)}) fusion(pred[256]{0:T(512)(128)(4,1)S(1)} %dynamic_slice.34, bf16[384,2,8,128]{3,0,2,1:T(8,128)(2,1)} %get-tuple-element.261, bf16[1024,2,128]{2,0,1:T(8,128)(2,1)} %get-tuple-element.260, s32[]{:T(128)S(6)} %select_n.123), kind=kOutput, calls=%fused_computation.3.clone.1 | convolution fusion | flops 407365632 | bytes 8020228 | tf_op jit(solution)/shard_map/while/body/eval_jaxpr/nkgd,tkd->nkgt/dot_general | solution.py:28
  125.8 4.3 %fusion.57 = f32[384,2,8]{0,2,1:T(8,128)S(1)} fusion(f32[2,256,384,8]{2,1,3,0:T(8,128)} %get-tuple-element.224, f32[384,2,8]{0,2,1:T(8,128)S(1)} %select_maximum_fusion.2, pred[256]{0:T(512)(128)(4,1)S(1)} %dynamic_slice.34), kind=kLoop, calls=%fused_computation.6.clone.1 | loop fusion | flops 6285312 | bytes 6340864 | tf_op jit(solution)/shard_map/while/body/eval_jaxpr/reduce_sum | solution.py:35
  130.1 0.3 copy-done.1
  130.4 5.5 %bitcast_add_fusion.2 = f32[384,2,8,128]{0,3,2,1:T(8,128)} fusion(f32[384,2,8,128]{0,3,2,1:T(8,128)} %get-tuple-element.242, f32[384,2,8]{0,2,1:T(8,128)S(1)} %get-tuple-element.226, pred[]{:T(512)S(6)} %compare.3, f32[2,256,384,8]{2,1,3,0:T(8,128)S(1)} %copy-done.1, f32[384,2,8]{0,2,1:T(8,128)S(1)} %select_maximum_fusion.2, ...), kind=kOutput, calls=%fused_computation.9.clone.1 | convolution fusion | flops 411303936 | bytes 12763653 | tf_op jit(solution)/shard_map/while/body/eval_jaxpr/nkgt,tkd->nkgd/dot_general | solution.py:36
  135.8 0.3 copy.113
  136.2 0.2 copy.104
  136.4 0.4 reshape_reshape.4
  136.8 0.1 copy.147
  136.9 0.7 reshape.201
  137.6 12.0 %all-to-all-start.1 = ((f32[16,1,384]{2,1,0:T(1,128)}), f32[16,1,384]{2,1,0:T(1,128)S(1)}, u32[]{:S(2)}, u32[]{:S(2)}) async-start(f32[16,1,384]{2,1,0:T(1,128)} %reshape.201), calls=%async_computation.1 | async-start | bytes 49152 | tf_op jit(solution)/shard_map/all_to_all | solution.py:144
  149.6 0.2 copy.114
  149.8 3.5 copy.115
  153.4 5.4 %select_convert_fusion = bf16[384,2,8,128]{3,2,1,0:T(8,128)(2,1)S(1)} fusion(f32[384,2,8,128]{3,2,1,0:T(8,128)} %copy.115, f32[384,2,8]{2,1,0:T(2,128)S(1)} %copy.114, pred[384,2,8]{2,1,0:T(4,128)(4,1)S(1)} %copy.113), kind=kLoop, calls=%fused_computation.29 | loop fusion | flops 2359296 | bytes 4749312 | tf_op jit(solution)/shard_map/convert_element_type | solution.py:51
  158.8 2.0 copy.116
  160.8 0.3 all-to-all-done.1
  161.1 11.2 %all-to-all-start.3 = ((f32[8,16,3,16,128]{4,3,2,0,1:T(8,128)}), f32[8,16,3,16,128]{4,3,2,0,1:T(8,128)}, u32[]{:S(2)}, u32[]{:S(2)}) async-start(f32[8,16,3,16,128]{4,3,2,0,1:T(8,128)} %copy.116), calls=%async_computation.3 | async-start | bytes 6291456 | tf_op jit(solution)/shard_map/all_to_all | solution.py:131
  172.3 0.5 broadcast.186
  172.8 0.6 reduce
  173.6 0.7 reshape.203
  174.4 134.8 %all-to-all-done.3 = f32[8,16,3,16,128]{4,3,2,0,1:T(8,128)} async-done(((f32[8,16,3,16,128]{4,3,2,0,1:T(8,128)}), f32[8,16,3,16,128]{4,3,2,0,1:T(8,128)}, u32[]{:S(2)}, u32[]{:S(2)}) %all-to-all-start.3) | async-done | bytes 3145760 | tf_op jit(solution)/shard_map/all_to_all | solution.py:131
  309.2 7.3 %all-to-all-start.2 = ((f32[8,1,768]{2,1,0:T(1,128)}), f32[8,1,768]{2,1,0:T(1,128)S(1)}, u32[]{:S(2)}, u32[]{:S(2)}) async-start(f32[8,1,768]{2,1,0:T(1,128)} %reshape.203), calls=%async_computation.2 | async-start | bytes 49152 | tf_op jit(solution)/shard_map/all_to_all | solution.py:143
  316.4 3.9 copy.117
  320.4 0.8 all-to-all-done.2
  321.2 5.0 %all-to-all-start.4 = ((f32[8,16,3,16,128]{4,3,2,1,0:T(8,128)}), f32[8,16,3,16,128]{4,3,2,1,0:T(8,128)}, u32[]{:S(2)}, u32[]{:S(2)}) async-start(f32[8,16,3,16,128]{4,3,2,1,0:T(8,128)} %copy.117), calls=%async_computation.4 | async-start | bytes 6291456 | tf_op jit(solution)/shard_map/all_to_all | solution.py:130
  326.3 0.5 fusion.45
  326.8 0.2 fusion.28
  327.2 1.4 convolution_divide_fusion
  328.6 0.6 reduce.1
  329.6 0.6 gather_fusion
  330.3 33.6 %all-to-all-done.4 = f32[8,16,3,16,128]{4,3,2,1,0:T(8,128)} async-done(((f32[8,16,3,16,128]{4,3,2,1,0:T(8,128)}), f32[8,16,3,16,128]{4,3,2,1,0:T(8,128)}, u32[]{:S(2)}, u32[]{:S(2)}) %all-to-all-start.4) | async-done | bytes 3145760 | tf_op jit(solution)/shard_map/all_to_all | solution.py:130
  363.9 2.4 multiply_reduce_fusion
  366.3 0.2 bitcast_divide_fusion
  366.5 0.6 gather_fusion.1
  367.3 0.2 fusion.24
  367.6 13.8 %all_gather.7 = bf16[128,2048]{1,0:T(8,128)(2,1)S(1)} all-gather(bf16[16,2048]{1,0:T(8,128)(2,1)S(1)} %fusion.24), channel_id=1, replica_groups=mesh['pool'=16,'row'=8,'head'=4] {'row'}, dimensions={0}, use_global_device_ids=true | all-gather | bytes 589824 | tf_op jit(solution)/shard_map/all_gather | solution.py:186
  381.4 1.2 convolution_convert_fusion.1
  382.6 21.0 %reduce-scatter.2.cloned.1.call-done = bf16[32,640]{1,0:T(8,128)(2,1)} async-done(((bf16[128,640]{1,0:T(8,128)(2,1)}), bf16[32,640]{1,0:T(8,128)(2,1)}) %reduce-scatter.2.cloned.1.call-update) | async-done | bytes 40976 | tf_op jit(solution)/shard_map/reduce_scatter | solution.py:190
  (66 shorter events, 1.8 us)
Async XLA Ops:
  6.5 374.8 %copy-start = (bf16[2048,640]{1,0:T(8,128)(2,1)S(1)}, bf16[2048,640]{1,0:T(8,128)(2,1)}, u32[]{:S(2)}) copy-start(bf16[2048,640]{1,0:T(8,128)(2,1)} %param.21) | copy-start | bytes 7864324
  6.5 34.0 %copy-start.5 = (s32[16]{0:T(128)S(1)}, s32[16]{0:T(128)}, u32[]{:S(2)}) copy-start(s32[16]{0:T(128)} %param.18) | copy-start | bytes 196
  6.5 34.0 %copy-start.6 = (s32[16]{0:T(128)S(1)}, s32[16]{0:T(128)}, u32[]{:S(2)}) copy-start(s32[16]{0:T(128)} %param.19) | copy-start | bytes 196
  6.5 61.6 %all-gather.2.cloned.1.call-start = ((), (), s32[]{:S(2)}) async-start(), calls=%async_computation.6 | async-start | bytes 1769472 | tf_op jit(solution)/shard_map/all_gather | solution.py:114
  77.7 4.6 %copy-start.1 = (f32[2,256,384,8]{2,1,3,0:T(8,128)S(1)}, f32[2,256,384,8]{2,1,3,0:T(8,128)}, u32[]{:S(2)}) copy-start(f32[2,256,384,8]{2,1,3,0:T(8,128)} %get-tuple-element.224) | copy-start | bytes 18874372 | tf_op jit(solution)/shard_map/while
  92.5 4.6 %copy-start.1 = (f32[2,256,384,8]{2,1,3,0:T(8,128)S(1)}, f32[2,256,384,8]{2,1,3,0:T(8,128)}, u32[]{:S(2)}) copy-start(f32[2,256,384,8]{2,1,3,0:T(8,128)} %get-tuple-element.224) | copy-start | bytes 18874372 | tf_op jit(solution)/shard_map/while
  109.1 4.6 %copy-start.1 = (f32[2,256,384,8]{2,1,3,0:T(8,128)S(1)}, f32[2,256,384,8]{2,1,3,0:T(8,128)}, u32[]{:S(2)}) copy-start(f32[2,256,384,8]{2,1,3,0:T(8,128)} %get-tuple-element.224) | copy-start | bytes 18874372 | tf_op jit(solution)/shard_map/while
  125.8 4.6 %copy-start.1 = (f32[2,256,384,8]{2,1,3,0:T(8,128)S(1)}, f32[2,256,384,8]{2,1,3,0:T(8,128)}, u32[]{:S(2)}) copy-start(f32[2,256,384,8]{2,1,3,0:T(8,128)} %get-tuple-element.224) | copy-start | bytes 18874372 | tf_op jit(solution)/shard_map/while
  137.6 23.4 %all-to-all-start.1 = ((f32[16,1,384]{2,1,0:T(1,128)}), f32[16,1,384]{2,1,0:T(1,128)S(1)}, u32[]{:S(2)}, u32[]{:S(2)}) async-start(f32[16,1,384]{2,1,0:T(1,128)} %reshape.201), calls=%async_computation.1 | async-start | bytes 49152 | tf_op jit(solution)/shard_map/all_to_all | solution.py:144
  161.1 148.1 %all-to-all-start.3 = ((f32[8,16,3,16,128]{4,3,2,0,1:T(8,128)}), f32[8,16,3,16,128]{4,3,2,0,1:T(8,128)}, u32[]{:S(2)}, u32[]{:S(2)}) async-start(f32[8,16,3,16,128]{4,3,2,0,1:T(8,128)} %copy.116), calls=%async_computation.3 | async-start | bytes 6291456 | tf_op jit(solution)/shard_map/all_to_all | solution.py:131
  309.2 12.0 %all-to-all-start.2 = ((f32[8,1,768]{2,1,0:T(1,128)}), f32[8,1,768]{2,1,0:T(1,128)S(1)}, u32[]{:S(2)}, u32[]{:S(2)}) async-start(f32[8,1,768]{2,1,0:T(1,128)} %reshape.203), calls=%async_computation.2 | async-start | bytes 49152 | tf_op jit(solution)/shard_map/all_to_all | solution.py:143
  320.3 5.8 %copy-start.4 = (s32[16]{0:T(128)S(1)}, s32[16]{0:T(128)}, u32[]{:S(2)}) copy-start(s32[16]{0:T(128)} %param.20) | copy-start | bytes 196
  320.3 5.9 %copy-start.2 = (bf16[16,64,2,128]{3,2,1,0:T(2,128)(2,1)S(1)}, bf16[16,64,2,128]{3,2,1,0:T(2,128)(2,1)}, u32[]{:S(2)}) copy-start(bf16[16,64,2,128]{3,2,1,0:T(2,128)(2,1)} %param.15) | copy-start | bytes 1572868
  320.3 5.9 %copy-start.3 = (bf16[16,16,128]{2,1,0:T(8,128)(2,1)S(1)}, bf16[16,16,128]{2,1,0:T(8,128)(2,1)}, u32[]{:S(2)}) copy-start(bf16[16,16,128]{2,1,0:T(8,128)(2,1)} %param.12) | copy-start | bytes 196612
  321.2 42.7 %all-to-all-start.4 = ((f32[8,16,3,16,128]{4,3,2,1,0:T(8,128)}), f32[8,16,3,16,128]{4,3,2,1,0:T(8,128)}, u32[]{:S(2)}, u32[]{:S(2)}) async-start(f32[8,16,3,16,128]{4,3,2,1,0:T(8,128)} %copy.117), calls=%async_computation.4 | async-start | bytes 6291456 | tf_op jit(solution)/shard_map/all_to_all | solution.py:130
  326.2 77.4 %reduce-scatter.2.cloned.1.call-start = ((), (), s32[]{:S(2)}) async-start(), calls=%async_computation.7 | async-start | bytes 204800 | tf_op jit(solution)/shard_map/reduce_scatter | solution.py:190
Sparse Core Ops, SparseCore 0:
  37.3 30.7 all-gather.1
  382.8 20.8 reduce-scatter.1
where the time goes:
time: 413 us; the launch traced here: 410 us
  waiting for transfers between devices  217 us (53%)
  matrix products  44.7 us (11%)
  blocking collectives  42 us (10%)
  starting transfers between devices  35.6 us (9%)
  other arithmetic  29.8 us (7%)
  local copies, waits for them, and re-layouts  25.1 us (6%)
  between operations  13.7 us (3%)
    all_to_all x1, waiting for transfers between devices, body(): lax.all_to_all(block_out.astype(jnp.float32), 'pool', split_axis=pool_dim...  135 us
    all_to_all x1, waiting for transfers between devices, body(): lax.all_to_all(lax.all_to_all(block_out.astype(jnp.float32), 'pool', spli...  33.6 us
    all_to_all x1, blocking collectives, body(): lax.all_to_all(outgoing, 'pool', split_axis=0, concat_axis=0, tiled=True)  28.2 us
    all_gather x1, waiting for transfers between devices, body(): block = lax.all_gather(flat_arrived, 'row', axis=0, tiled=True)  26.3 us
    reduce_scatter x1, waiting for transfers between devices, body(): lax.psum_scatter(terms.astype(jnp.bfloat16), 'head', scatter_dimension=0,...  21 us
    dot_general x4, matrix products, advance(): jnp.einsum('nkgd,tkd->nkgt', grouped, key_block, preferred_element_type=j...  20.5 us
    dot_general x4, matrix products, advance(): jnp.einsum('nkgt,tkd->nkgd', powers.astype(jnp.bfloat16), value_block, pr...  19.9 us
    reduce_sum x4, other arithmetic, advance(): denominator = denominator * factor + jnp.sum(powers, axis=-1)  17.2 us
  transfers between devices with their start and end apart: 6, of which 6 were waited for; matrix products, arithmetic and copies ran while one was open for 6% of the time, Pallas kernels for 0%

commit v1 on v0

v1 whole, which is shorter than its diff:
```python
import functools
import math

import jax
import jax.numpy as jnp
from jax import lax
from jax.experimental import pallas as pl
from jax.experimental.pallas import tpu as pltpu
from jax.sharding import Mesh, PartitionSpec as P

LOWEST = -1e30
CAP = 3
GROUP = 8
HD = 128
SCALE = HD**-0.5
LOG2E = math.log2(math.e)
F32 = jnp.float32
BF16 = jnp.bfloat16

VMEM = pl.BlockSpec(memory_space=pltpu.VMEM)
SMEM = pl.BlockSpec(memory_space=pltpu.SMEM)


def params(mib):
    return pltpu.CompilerParams(vmem_limit_bytes=mib * 1024 * 1024)


def split3(value):
    high = value.astype(BF16).astype(F32)
    rest = value - high
    middle = rest.astype(BF16).astype(F32)
    return high, middle, (rest - middle).astype(BF16).astype(F32)


def slot_of(row, row_prefix_ref, owner_ref, count_ref):
    owner = owner_ref[row_prefix_ref[row]]
    place = count_ref[owner]
    count_ref[owner] = place + 1
    return owner, place


def dispatch_kernel(row_prefix_ref, owner_ref, q_ref, out_ref, count_ref):
    for p in range(owner_ref.shape[0]):
        count_ref[p] = 0
    out_ref[...] = jnp.zeros_like(out_ref)
    for r in range(q_ref.shape[0]):
        owner, place = slot_of(r, row_prefix_ref, owner_ref, count_ref)
        out_ref[owner * CAP + place] = q_ref[r]


def unmix_kernel(k0_ref, k1_ref, v0_ref, v1_ref, k_ref, v_ref, scratch):
    length = k0_ref.shape[0] // 2
    for i, (sources, target) in enumerate((((k0_ref, k1_ref), k_ref), ((v0_ref, v1_ref), v_ref))):
        for n, source in enumerate(sources):
            held = scratch.at[2 * i + n]
            held[...] = source[...].astype(F32)
            for g in range(2):
                target[g, n * length : (n + 1) * length, :] = held[
                    pl.ds(g, length, stride=2), :
                ].astype(BF16)


def attend_kernel(owner_ref, lengths_ref, q_ref, k_ref, v_ref, out_ref):
    slots = q_ref.shape[0]
    step_slots = math.gcd(24, slots)
    span = k_ref.shape[1]
    part = span // 2
    pool = lax.axis_index("pool")
    core = lax.axis_index("core")
    first = lax.axis_index("y") * 2
    own_length = jnp.int32(0)
    for p in range(owner_ref.shape[0]):
        own_length += jnp.where(owner_ref[p] == pool, lengths_ref[p], 0)
    column = lax.broadcasted_iota(jnp.int32, (1, span), 1)
    token = jnp.where(
        column < part, column + (first + core) * part, column + (first - core) * part
    )
    bias = jnp.where(token < own_length, 0.0, LOWEST).astype(F32)
    lane = lax.broadcasted_iota(jnp.int32, (GROUP, 128), 1)

    def step(j, packed):
        start = j * step_slots
        q_all = q_ref[pl.ds(start, step_slots)].astype(F32)
        outs = []
        filled = []
        for g in range(2):
            q = q_all[:, g * GROUP : (g + 1) * GROUP, :].reshape(step_slots * GROUP, HD)
            scores = (
                lax.dot_general(
                    q.astype(BF16), k_ref[g], (((1,), (1,)), ((), ())), preferred_element_type=F32
                )
                + bias
            )
            peak = jnp.maximum(jnp.max(scores, axis=1, keepdims=True), 0.1 * LOWEST)
            weights = jnp.exp2((scores - peak) * (SCALE * LOG2E)).astype(BF16)
            values = jnp.concatenate([v_ref[g], jnp.ones((span, HD), BF16)], axis=1)
            both = jnp.dot(weights, values, preferred_element_type=F32)
            total = both[:, HD:]
            live = total > 0
            safe = jnp.where(live, total, 1.0)
            outs.append((both[:, :HD] / safe).reshape(step_slots, GROUP, HD))
            lse = jnp.where(live, peak * SCALE + jnp.log(safe), LOWEST)
            lse = lse.reshape(step_slots, GROUP, HD)
            kept = packed[g]
            for i in range(step_slots):
                kept = jnp.where(lane == start + i, lse[i], kept)
            filled.append(kept)
        out_ref[pl.ds(start, step_slots)] = jnp.concatenate(outs, axis=1).astype(BF16)
        return tuple(filled)

    empty = jnp.zeros((GROUP, 128), F32)
    packed = lax.fori_loop(0, slots // step_slots, step, (empty, empty))
    for i, plane in enumerate(split3(jnp.concatenate(packed, axis=0))):
        out_ref[slots + i] = plane.astype(BF16)


def merge_kernel(a_ref, b_ref, c_ref, d_ref, out_ref):
    blocks = (a_ref, b_ref, c_ref, d_ref)
    slots = a_ref.shape[0] - 3
    pools = slots // CAP
    lses = [
        (ref[slots + 2].astype(F32) + ref[slots + 1].astype(F32)) + ref[slots].astype(F32)
        for ref in blocks
    ]
    top = functools.reduce(jnp.maximum, lses)
    shares = [jnp.exp(lse - top) for lse in lses]
    total = functools.reduce(jnp.add, shares)
    weights = [share / total for share in shares]
    planes = split3(top + jnp.log(total))
    lane = lax.broadcasted_iota(jnp.int32, (GROUP, 128), 1)
    for pair in range(0, pools, 2):
        rows = []
        for p in (pair, pair + 1):
            for s in range(p * CAP, (p + 1) * CAP):
                terms = [
                    weight[:, s : s + 1] * ref[s].astype(F32) for weight, ref in zip(weights, blocks)
                ]
                rows.append(functools.reduce(jnp.add, terms))
            tile = jnp.zeros((GROUP, 128), F32)
            for i, plane in enumerate(planes):
                for g in range(2):
                    at = i * 16 + g * 8
                    moved = plane[g * GROUP : (g + 1) * GROUP]
                    shift = (at - p * CAP) % 128
                    if shift:
                        moved = pltpu.roll(moved, shift, 1)
                    tile = jnp.where((lane >= at) & (lane < at + CAP), moved, tile)
            rows.append(tile)
        height = CAP * 16 + GROUP
        out_ref[pl.ds(pair * height, 2 * height), :] = jnp.concatenate(rows, axis=0).astype(BF16)


def suffix_kernel(length_ref, q_ref, k_ref, v_ref, out_ref, lse_ref):
    span = k_ref.shape[1]
    column = lax.broadcasted_iota(jnp.int32, (2 * GROUP, span), 1)
    head = lax.broadcasted_iota(jnp.int32, (2 * GROUP, span), 0)
    same = (column & 1) == head // GROUP
    for r in range(q_ref.shape[0]):
        scores = lax.dot_general(
            q_ref[r], k_ref[r], (((1,), (1,)), ((), ())), preferred_element_type=F32
        )
        visible = same & (column < 2 * length_ref[r])
        scores = jnp.where(visible, scores * SCALE, LOWEST)
        peak = jnp.max(scores, axis=1, keepdims=True)
        powers = jnp.exp(scores - peak)
        total = jnp.sum(powers, axis=1, keepdims=True)
        summed = jnp.dot(powers.astype(BF16), v_ref[r], preferred_element_type=F32)
        out_ref[r] = summed / total
        lse_ref[r] = jnp.broadcast_to(peak + jnp.log(total), (2 * GROUP, HD))


def combine_kernel(
    row_prefix_ref, owner_ref, got_ref, suffix_ref, suffix_lse_ref, out_ref, wide, mixed, count_ref
):
    rows = suffix_ref.shape[0]
    height = CAP * 16 + GROUP
    for p in range(owner_ref.shape[0]):
        count_ref[p] = 0
    wide[...] = got_ref[...].astype(F32)
    lane = lax.broadcasted_iota(jnp.int32, (GROUP, 128), 1)
    for r in range(rows):
        owner, place = slot_of(r, row_prefix_ref, owner_ref, count_ref)
        base = owner * height
        prefix = wide[pl.ds(pl.multiple_of(base + place * 16, 8), 16), :]
        tile = wide[pl.ds(pl.multiple_of(base + CAP * 16, 8), GROUP), :]
        lses = []
        for g in range(2):
            chosen = ((lane & 15) == place + g * 8) & (lane < 48)
            lses.append(jnp.sum(jnp.where(chosen, tile, 0.0), axis=1, keepdims=True))
        prefix_lse = jnp.broadcast_to(jnp.concatenate(lses, axis=0), (2 * GROUP, HD))
        suffix_lse = suffix_lse_ref[r]
        highest = jnp.maximum(prefix_lse, suffix_lse)
        a = jnp.exp(prefix_lse - highest)
        b = jnp.exp(suffix_lse - highest)
        mixed[r * 16 : (r + 1) * 16, :] = (a * prefix + b * suffix_ref[r]) / (a + b)
    for h in range(2 * GROUP):
        piece = mixed[pl.ds(h, rows, stride=16), :].astype(BF16)
        for n in range(out_ref.shape[0]):
            out_ref[n, :, h * HD : (h + 1) * HD] = piece


def project_kernel(own_ref, other_ref, w_ref, out_ref):
    count, rows, depth = own_ref.shape
    core = lax.axis_index("core")
    both = jnp.concatenate(
        [own_ref[...].reshape(count * rows, depth), other_ref[...].reshape(count * rows, depth)],
        axis=0,
    )
    terms = jnp.dot(both, w_ref[...], preferred_element_type=F32).astype(BF16)
    terms = terms.reshape(2, count, rows, -1)
    for n in range(count):
        out_ref[n, core] = terms[0, n]
        out_ref[n, 1 - core] = terms[1, n]


def body(
    queries,
    prefix_keys,
    prefix_values,
    suffix_keys,
    suffix_values,
    row_prefix,
    owner_map,
    prefix_lengths,
    suffix_lengths,
    out_weight,
):
    rows, heads, hdim = queries.shape
    row_prefix = row_prefix.reshape(-1)
    pools = lax.axis_size("pool")
    ring = lax.axis_size("y")
    slots = pools * CAP
    columns = out_weight.shape[1]
    shape = jax.ShapeDtypeStruct

    def turn(value, by):
        return lax.ppermute(value, "y", [(i, (i + by) % ring) for i in range(ring)])

    def swap(value):
        return lax.ppermute(value, "core", [(0, 1), (1, 0)])

    outgoing = pl.pallas_call(
        dispatch_kernel,
        out_shape=shape((slots, heads, hdim), BF16),
        in_specs=[SMEM, SMEM, VMEM],
        out_specs=VMEM,
        scratch_shapes=[pltpu.SMEM((pools,), jnp.int32)],
        compiler_params=params(8),
        cost_estimate=pl.CostEstimate(flops=0, bytes_accessed=300_000, transcendentals=0),
        name="dispatch",
    )(row_prefix, owner_map, queries)

    own_keys = prefix_keys.reshape(-1, hdim)
    own_values = prefix_values.reshape(-1, hdim)
    other_keys = swap(prefix_keys).reshape(-1, hdim)
    other_values = swap(prefix_values).reshape(-1, hdim)

    arrived = lax.all_to_all(
        outgoing.reshape(pools, CAP, heads, hdim), "pool", split_axis=0, concat_axis=0, tiled=True
    ).reshape(slots, heads, hdim)
    asked = {by: turn(arrived, by) for by in (1, ring - 1, 2)}
    asked[0] = arrived

    span = own_keys.shape[0]
    keys, values = pl.pallas_call(
        unmix_kernel,
        out_shape=[shape((2, span, hdim), BF16)] * 2,
        in_specs=[VMEM] * 4,
        out_specs=[VMEM] * 2,
        scratch_shapes=[pltpu.VMEM((4, span, hdim), F32)],
        compiler_params=params(16),
        cost_estimate=pl.CostEstimate(flops=0, bytes_accessed=4_000_000, transcendentals=0),
        name="unmix",
    )(own_keys, other_keys, own_values, other_values)

    suffix_out, suffix_lse = pl.pallas_call(
        suffix_kernel,
        out_shape=[shape((rows, heads, hdim), F32)] * 2,
        in_specs=[SMEM, VMEM, VMEM, VMEM],
        out_specs=[VMEM] * 2,
        compiler_params=params(8),
        cost_estimate=pl.CostEstimate(
            flops=4 * rows * heads * 128 * 128, bytes_accessed=2_000_000, transcendentals=0
        ),
        name="suffix",
    )(
        suffix_lengths,
        queries,
        suffix_keys.reshape(rows, -1, hdim),
        suffix_values.reshape(rows, -1, hdim),
    )

    attend = pl.pallas_call(
        attend_kernel,
        out_shape=shape((slots + 3, heads, hdim), BF16),
        in_specs=[SMEM, SMEM, VMEM, VMEM, VMEM],
        out_specs=VMEM,
        compiler_params=params(24),
        cost_estimate=pl.CostEstimate(
            flops=6 * slots * heads * span * hdim,
            bytes_accessed=3_000_000,
            transcendentals=slots * heads * span,
        ),
        name="attend",
    )
    parts = {by: attend(owner_map, prefix_lengths, q, keys, values) for by, q in asked.items()}
    merged = pl.pallas_call(
        merge_kernel,
        out_shape=shape((pools * (CAP * heads + GROUP), hdim), BF16),
        in_specs=[VMEM] * 4,
        out_specs=VMEM,
        compiler_params=params(8),
        cost_estimate=pl.CostEstimate(flops=0, bytes_accessed=1_000_000, transcendentals=0),
        name="merge",
    )(parts[0], *(turn(parts[by], -by) for by in (1, ring - 1, 2)))
    returned = lax.all_to_all(
        merged.reshape(pools, CAP * heads + GROUP, hdim),
        "pool",
        split_axis=0,
        concat_axis=0,
        tiled=True,
    ).reshape(-1, hdim)

    attended = pl.pallas_call(
        combine_kernel,
        out_shape=shape((ring, rows, heads * hdim), BF16),
        in_specs=[SMEM, SMEM, VMEM, VMEM, VMEM],
        out_specs=VMEM,
        scratch_shapes=[
            pltpu.VMEM((pools * (CAP * heads + GROUP), hdim), F32),
            pltpu.VMEM((rows * heads, hdim), F32),
            pltpu.SMEM((pools,), jnp.int32),
        ],
        compiler_params=params(8),
        cost_estimate=pl.CostEstimate(flops=0, bytes_accessed=1_000_000, transcendentals=0),
        name="combine",
    )(row_prefix, owner_map, returned, suffix_out, suffix_lse)
    gathered = lax.all_to_all(attended, "y", split_axis=0, concat_axis=0, tiled=True)
    terms = pl.pallas_call(
        project_kernel,
        out_shape=shape((ring, 2, rows, columns), BF16),
        in_specs=[VMEM] * 3,
        out_specs=VMEM,
        compiler_params=params(16),
        cost_estimate=pl.CostEstimate(
            flops=4 * ring * rows * heads * hdim * columns,
            bytes_accessed=4_000_000,
            transcendentals=0,
        ),
        name="project",
    )(gathered, swap(gathered), out_weight)
    shared = lax.all_to_all(
        terms.reshape(lax.axis_size("head"), -1, columns), "head", split_axis=0, concat_axis=0, tiled=True
    )
    return jnp.sum(shared.astype(F32), axis=0).astype(BF16)


def solution(mesh):
    pools, across, groups = mesh.devices.shape
    fine = Mesh(
        mesh.devices.reshape(pools, across // 2, 2, groups), ("pool", "y", "core", "head")
    )
    row = ("y", "core")
    every = ("pool", "y", "core")
    return jax.shard_map(
        body,
        mesh=fine,
        in_specs=(
            P(every, "head", None),
            P("pool", row, "head", None),
            P("pool", row, "head", None),
            P(every, None, "head", None),
            P(every, None, "head", None),
            P(every, None),
            P(),
            P(),
            P(every),
            P("head", row),
        ),
        out_specs=P(("pool", "head"), row),
        check_vma=False,
    )
```

time: 413 us -> 125 us (0.30)
  waiting for transfers between devices: 217 us -> 14.7 us
  matrix products: 44.7 us -> 0 us
  other arithmetic: 29.8 us -> 0.64 us
  blocking collectives: 42 us -> 17.4 us
  Pallas kernels: 0 us -> 24.1 us
  starting transfers between devices: 35.6 us -> 58.1 us
  local copies, waits for them, and re-layouts: 25.1 us -> 8.43 us
  between operations: 13.7 us -> 0.3 us
    all_to_all x4 -> x2, waiting for transfers between devices: 169 us -> 13.5 us  [the longest x1 7.75 us: body(): lax.all_to_all(outgoing.reshape(pools, CAP, heads, hdim), 'pool', split_a...]
    dot_general x12 -> x0, matrix products: 44.7 us -> none  [the longest x4 20.5 us: advance(): jnp.einsum('nkgd,tkd->nkgt', grouped, key_block, preferred_element_type=j...]
    ppermute x0 -> x9, starting transfers between devices: none -> 33.6 us  [the longest x6 19.4 us: turn(): return lax.ppermute(value, 'y', [(i, (i + by) % ring) for i in range(ring)])]
    all_gather x1 -> x0, waiting for transfers between devices: 26.3 us -> none  [body(): block = lax.all_gather(flat_arrived, 'row', axis=0, tiled=True)]
    pallas_call x0 -> x10, Pallas kernels: none -> 24.1 us  [the longest x4 15.1 us: body(): attend(owner_map, prefix_lengths, q, keys, values)]
    reduce_sum x10 -> x1, other arithmetic: 21.7 us -> 0.64 us  [body(): return jnp.sum(shared.astype(F32), axis=0).astype(BF16)]
    reduce_scatter x1 -> x0, waiting for transfers between devices: 21 us -> none  [body(): lax.psum_scatter(terms.astype(jnp.bfloat16), 'head', scatter_dimension=0,...]
    all_gather x1 -> x0, blocking collectives: 13.8 us -> none  [body(): lax.all_gather(attended, 'row', axis=0, tiled=True)]
  transfers between devices with their start and end apart: 6 -> 11, of which waited for: 6 -> 3; matrix products, arithmetic and copies ran while one was open for 6% -> 0% of each run, Pallas kernels for 0% -> 16%
where the time goes in v1:
time: 125 us; the launch traced here: 124 us
  starting transfers between devices  58.1 us (46%)
  Pallas kernels  24.1 us (19%)
  blocking collectives  17.4 us (14%)
  waiting for transfers between devices  14.7 us (12%)
  local copies, waits for them, and re-layouts  8.43 us (7%)
    ppermute x6, starting transfers between devices, turn(): return lax.ppermute(value, 'y', [(i, (i + by) % ring) for i in range(ring)])  19.4 us
    all_to_all x1, starting transfers between devices, body(): lax.all_to_all(outgoing.reshape(pools, CAP, heads, hdim), 'pool', split_a...  15.7 us
    pallas_call x4, Pallas kernels, body(): attend(owner_map, prefix_lengths, q, keys, values)  15.1 us
    ppermute x3, starting transfers between devices, swap(): return lax.ppermute(value, 'core', [(0, 1), (1, 0)])  14.2 us
    all_to_all x1, blocking collectives, body(): lax.all_to_all(terms.reshape(lax.axis_size('head'), -1, columns), 'head',...  8.82 us
    all_to_all x1, starting transfers between devices, body(): lax.all_to_all(merged.reshape(pools, CAP * heads + GROUP, hdim), 'pool',...  8.81 us
    all_to_all x1, blocking collectives, body(): lax.all_to_all(attended, 'y', split_axis=0, concat_axis=0, tiled=True)  8.62 us
    unnamed x34, local copies, waits for them, and re-layouts  8.43 us
  transfers between devices with their start and end apart: 11, of which 3 were waited for; matrix products, arithmetic and copies ran while one was open for 0% of the time, Pallas kernels for 16%

profile of v1, /device:TPU:1, one launch (start us, length us, event | category | flops | bytes accessed | tf_op | source)
XLA Modules:
  0.0 123.8 jit_solution(13097867094419300554)
XLA Ops:
  0.0 0.0 copy-start.14
  0.0 0.0 copy-start.16
  0.0 0.9 copy-done.5
  0.9 0.0 copy-start.11
  0.9 0.7 copy-done.11
  1.5 0.0 copy-start.13
  1.5 0.7 copy-done.13
  2.2 1.3 %dispatch.1 = bf16[48,16,128]{2,1,0:T(8,128)(2,1)} custom-call(s32[16]{0:T(128)S(1)} %bitcast.24, s32[16]{0:T(128)S(1)} %copy-done.13, bf16[16,16,128]{2,1,0:T(8,128)(2,1)S(1)} %copy-done.5), custom_call_target="tpu_custom_call" | custom-call | bytes 300000 | tf_op jit(solution)/shard_map/dispatch/pallas_call | solution.py:242
  3.5 15.7 %all-to-all-start = ((bf16[16,3,16,128]{3,2,1,0:T(8,128)(2,1)}), bf16[16,3,16,128]{3,2,1,0:T(8,128)(2,1)S(1)}, u32[]{:S(2)}, u32[]{:S(2)}) async-start(bf16[16,3,16,128]{3,2,1,0:T(8,128)(2,1)} %bitcast.1), calls=%async_computation | async-start | bytes 393216 | tf_op jit(solution)/shard_map/all_to_all | solution.py:258
  19.2 2.9 %collective-permute-start = (bf16[1,1024,2,128]{3,2,1,0:T(2,128)(2,1)}, bf16[1,1024,2,128]{3,2,1,0:T(2,128)(2,1)S(1)}, u32[]{:S(2)}, u32[]{:S(2)}) collective-permute-start(bf16[1,1024,2,128]{3,2,1,0:T(2,128)(2,1)} %param.11), channel_id=1, source_target_pairs={{0,4},{4,0},{1,5},{5,1},{2,6},{6,2},{3,7},{7,3},{8,12},{12,8},{9,1... | collective-permute-start | bytes 1572872 | tf_op jit(solution)/shard_map/ppermute | solution.py:240
  22.1 1.9 %collective-permute-start.1 = (bf16[1,1024,2,128]{3,2,1,0:T(2,128)(2,1)}, bf16[1,1024,2,128]{3,2,1,0:T(2,128)(2,1)S(1)}, u32[]{:S(2)}, u32[]{:S(2)}) collective-permute-start(bf16[1,1024,2,128]{3,2,1,0:T(2,128)(2,1)} %param.12), channel_id=1, source_target_pairs={{0,4},{4,0},{1,5},{5,1},{2,6},{6,2},{3,7},{7,3},{8,12},{12,8},{9,1... | collective-permute-start | bytes 1572872 | tf_op jit(solution)/shard_map/ppermute | solution.py:240
  24.0 7.8 %all-to-all-done = bf16[16,3,16,128]{3,2,1,0:T(8,128)(2,1)S(1)} async-done(((bf16[16,3,16,128]{3,2,1,0:T(8,128)(2,1)}), bf16[16,3,16,128]{3,2,1,0:T(8,128)(2,1)S(1)}, u32[]{:S(2)}, u32[]{:S(2)}) %all-to-all-start) | async-done | bytes 196640 | tf_op jit(solution)/shard_map/all_to_all | solution.py:258
  31.8 4.8 %collective-permute-start.6 = (bf16[48,16,128]{2,1,0:T(8,128)(2,1)S(1)}, bf16[48,16,128]{2,1,0:T(8,128)(2,1)S(1)}, u32[]{:S(2)}, u32[]{:S(2)}) collective-permute-start(bf16[48,16,128]{2,1,0:T(8,128)(2,1)S(1)} %bitcast.20), channel_id=1, source_target_pairs={{0,16},{8,24},{16,0},{24,8},{1,17},{9,25},{17,1},{25,9},{2,18},{10... | collective-permute-start | bytes 589832 | tf_op jit(solution)/shard_map/ppermute | solution.py:237
  36.6 2.7 %collective-permute-start.4 = (bf16[48,16,128]{2,1,0:T(8,128)(2,1)S(1)}, bf16[48,16,128]{2,1,0:T(8,128)(2,1)S(1)}, u32[]{:S(2)}, u32[]{:S(2)}) collective-permute-start(bf16[48,16,128]{2,1,0:T(8,128)(2,1)S(1)} %bitcast.21), channel_id=1, source_target_pairs={{0,24},{8,0},{16,8},{24,16},{1,25},{9,1},{17,9},{25,17},{2,26},{10... | collective-permute-start | bytes 589832 | tf_op jit(solution)/shard_map/ppermute | solution.py:237
  39.3 0.0 collective-permute-done
  39.3 0.0 collective-permute-done.1
  39.3 0.0 copy-start.3
  39.3 1.0 copy-done.3
  40.4 0.0 copy-start.4
  40.4 1.0 copy-done.4
  41.4 0.5 unmix.1
  41.9 2.6 %collective-permute-start.2 = (bf16[48,16,128]{2,1,0:T(8,128)(2,1)S(1)}, bf16[48,16,128]{2,1,0:T(8,128)(2,1)S(1)}, u32[]{:S(2)}, u32[]{:S(2)}) collective-permute-start(bf16[48,16,128]{2,1,0:T(8,128)(2,1)S(1)} %bitcast.22), channel_id=1, source_target_pairs={{0,8},{8,16},{16,24},{24,0},{1,9},{9,17},{17,25},{25,1},{2,10},{10... | collective-permute-start | bytes 589832 | tf_op jit(solution)/shard_map/ppermute | solution.py:237
  44.5 0.0 collective-permute-done.6.q_ref
  44.5 0.0 copy-done.14
  44.5 0.0 copy-done.16
  44.5 3.8 %attend.7 = bf16[51,16,128]{2,1,0:T(8,128)(2,1)S(1)} custom-call(s32[16]{0:T(128)S(1)} %copy-done.14, s32[16]{0:T(128)S(1)} %copy-done.16, bf16[48,16,128]{2,1,0:T(8,128)(2,1)S(1)} %collective-permute-done.6.q_ref, bf16[2,2048,128]{2,1,0:T(8,128)(2,1)S(1)} %get-tuple-element.9.k_ref, bf16[2,2048,128]{2,1,0:T(8,128)(2,1)S(1)} %get-tuple-element.10.v_ref), custom_call_target="tpu_custom_call" | custom-call | flops 1207959552 | bytes 3000000 | tf_op jit(solution)/shard_map/attend/pallas_call | solution.py:306
  48.3 2.6 %collective-permute-start.7 = (bf16[51,16,128]{2,1,0:T(8,128)(2,1)S(1)}, bf16[51,16,128]{2,1,0:T(8,128)(2,1)S(1)}, u32[]{:S(2)}, u32[]{:S(2)}) collective-permute-start(bf16[51,16,128]{2,1,0:T(8,128)(2,1)S(1)} %attend.7), channel_id=1, source_target_pairs={{0,16},{8,24},{16,0},{24,8},{1,17},{9,25},{17,1},{25,9},{2,18},{10... | collective-permute-start | bytes 626696 | tf_op jit(solution)/shard_map/ppermute | solution.py:237
  51.0 0.0 collective-permute-done.4.q_ref
  51.0 3.8 %attend.6 = bf16[51,16,128]{2,1,0:T(8,128)(2,1)S(1)} custom-call(s32[16]{0:T(128)S(1)} %copy-done.14, s32[16]{0:T(128)S(1)} %copy-done.16, bf16[48,16,128]{2,1,0:T(8,128)(2,1)S(1)} %collective-permute-done.4.q_ref, bf16[2,2048,128]{2,1,0:T(8,128)(2,1)S(1)} %get-tuple-element.9.k_ref, bf16[2,2048,128]{2,1,0:T(8,128)(2,1)S(1)} %get-tuple-element.10.v_ref), custom_call_target="tpu_custom_call" | custom-call | flops 1207959552 | bytes 3000000 | tf_op jit(solution)/shard_map/attend/pallas_call | solution.py:306
  54.8 3.7 %collective-permute-start.5 = (bf16[51,16,128]{2,1,0:T(8,128)(2,1)S(1)}, bf16[51,16,128]{2,1,0:T(8,128)(2,1)S(1)}, u32[]{:S(2)}, u32[]{:S(2)}) collective-permute-start(bf16[51,16,128]{2,1,0:T(8,128)(2,1)S(1)} %attend.6), channel_id=1, source_target_pairs={{0,8},{8,16},{16,24},{24,0},{1,9},{9,17},{17,25},{25,1},{2,10},{10... | collective-permute-start | bytes 626696 | tf_op jit(solution)/shard_map/ppermute | solution.py:237
  58.5 0.0 collective-permute-done.2.q_ref
  58.5 3.8 %attend.5 = bf16[51,16,128]{2,1,0:T(8,128)(2,1)S(1)} custom-call(s32[16]{0:T(128)S(1)} %copy-done.14, s32[16]{0:T(128)S(1)} %copy-done.16, bf16[48,16,128]{2,1,0:T(8,128)(2,1)S(1)} %collective-permute-done.2.q_ref, bf16[2,2048,128]{2,1,0:T(8,128)(2,1)S(1)} %get-tuple-element.9.k_ref, bf16[2,2048,128]{2,1,0:T(8,128)(2,1)S(1)} %get-tuple-element.10.v_ref), custom_call_target="tpu_custom_call" | custom-call | flops 1207959552 | bytes 3000000 | tf_op jit(solution)/shard_map/attend/pallas_call | solution.py:306
  62.3 0.0 copy-start.1
  62.3 0.0 copy-start.6
  62.3 0.0 copy-start.15
  62.4 0.0 copy-start.12
  62.4 2.9 %collective-permute-start.3 = (bf16[51,16,128]{2,1,0:T(8,128)(2,1)S(1)}, bf16[51,16,128]{2,1,0:T(8,128)(2,1)S(1)}, u32[]{:S(2)}, u32[]{:S(2)}) collective-permute-start(bf16[51,16,128]{2,1,0:T(8,128)(2,1)S(1)} %attend.5), channel_id=1, source_target_pairs={{0,24},{8,0},{16,8},{24,16},{1,25},{9,1},{17,9},{25,17},{2,26},{10... | collective-permute-start | bytes 626696 | tf_op jit(solution)/shard_map/ppermute | solution.py:237
  65.3 3.8 %attend.4.a_ref = bf16[51,16,128]{2,1,0:T(8,128)(2,1)S(1)} custom-call(s32[16]{0:T(128)S(1)} %copy-done.14, s32[16]{0:T(128)S(1)} %copy-done.16, bf16[48,16,128]{2,1,0:T(8,128)(2,1)S(1)} %bitcast.23, bf16[2,2048,128]{2,1,0:T(8,128)(2,1)S(1)} %get-tuple-element.9.k_ref, bf16[2,2048,128]{2,1,0:T(8,128)(2,1)S(1)} %get-tuple-element.10.v_ref), custom_call_target="tpu_custom_call" | custom-call | flops 1207959552 | bytes 3000000 | tf_op jit(solution)/shard_map/attend/pallas_call | solution.py:306
  69.0 0.0 copy-start
  69.0 0.0 collective-permute-done.7.d_ref
  69.1 0.0 collective-permute-done.5.c_ref
  69.1 0.0 collective-permute-done.3.b_ref
  69.1 1.4 %merge.1 = bf16[896,128]{1,0:T(8,128)(2,1)} custom-call(bf16[51,16,128]{2,1,0:T(8,128)(2,1)S(1)} %attend.4.a_ref, bf16[51,16,128]{2,1,0:T(8,128)(2,1)S(1)} %collective-permute-done.3.b_ref, bf16[51,16,128]{2,1,0:T(8,128)(2,1)S(1)} %collective-permute-done.5.c_ref, bf16[51,16,128]{2,1,0:T(8,128)(2,1)S(1)} %collective-permute-done.7.d_ref), custom_call_target="tpu_custom_call" | custom-call | bytes 1000000 | tf_op jit(solution)/shard_map/merge/pallas_call | solution.py:307
  70.5 8.8 %all-to-all-start.1 = ((bf16[16,56,128]{2,1,0:T(8,128)(2,1)}), bf16[16,56,128]{2,1,0:T(8,128)(2,1)S(1)}, u32[]{:S(2)}, u32[]{:S(2)}) async-start(bf16[16,56,128]{2,1,0:T(8,128)(2,1)} %bitcast.7), calls=%async_computation.1 | async-start | bytes 458752 | tf_op jit(solution)/shard_map/all_to_all | solution.py:316
  79.3 0.0 copy-done.1
  79.3 0.0 copy-done.6
  79.3 0.0 copy-done.15
  79.3 0.0 copy-start.2
  79.3 1.0 copy-done.2
  80.3 4.4 %suffix.1 = (f32[16,16,128]{2,1,0:T(8,128)S(1)}, f32[16,16,128]{2,1,0:T(8,128)S(1)}) custom-call(s32[16]{0:T(128)S(1)} %copy-done.15, bf16[16,16,128]{2,1,0:T(8,128)(2,1)S(1)} %copy-done.6, bf16[16,128,128]{2,1,0:T(8,128)(2,1)S(1)} %bitcast.14, bf16[16,128,128]{2,1,0:T(8,128)(2,1)S(1)} %bitcast.15), custom_call_target="tpu_custom_call" | custom-call | flops 16777216 | bytes 2000000 | tf_op jit(solution)/shard_map/suffix/pallas_call | solution.py:276
  84.7 0.6 copy-done.7
  85.4 0.6 copy-done.9
  86.0 5.8 %all-to-all-done.1 = bf16[16,56,128]{2,1,0:T(8,128)(2,1)S(1)} async-done(((bf16[16,56,128]{2,1,0:T(8,128)(2,1)}), bf16[16,56,128]{2,1,0:T(8,128)(2,1)S(1)}, u32[]{:S(2)}, u32[]{:S(2)}) %all-to-all-start.1) | async-done | bytes 229408 | tf_op jit(solution)/shard_map/all_to_all | solution.py:316
  91.8 0.0 copy-done.12
  91.8 0.9 copy-done.8
  92.7 0.9 copy-done.10
  93.6 0.9 combine.1
  94.5 8.6 %all_to_all.20.own_ref = bf16[4,16,2048]{2,1,0:T(8,128)(2,1)S(1)} all-to-all(bf16[4,16,2048]{2,1,0:T(8,128)(2,1)S(1)} %combine.1), channel_id=1, replica_groups=mesh['pool'=16,'y'=4,'core'=2,'head'=4] {'y'}, dimensions={0} | all-to-all | bytes 524288 | tf_op jit(solution)/shard_map/all_to_all | solution.py:338
  103.1 9.4 %collective-permute-start.8 = (bf16[4,16,2048]{2,1,0:T(8,128)(2,1)S(1)}, bf16[4,16,2048]{2,1,0:T(8,128)(2,1)S(1)}, u32[]{:S(2)}, u32[]{:S(2)}) collective-permute-start(bf16[4,16,2048]{2,1,0:T(8,128)(2,1)S(1)} %all_to_all.20.own_ref), channel_id=1, source_target_pairs={{0,4},{4,0},{1,5},{5,1},{2,6},{6,2},{3,7},{7,3},{8,12},{12,8},{9,1... | collective-permute-start | bytes 786440 | tf_op jit(solution)/shard_map/ppermute | solution.py:240
  112.6 1.1 collective-permute-done.8.other_ref
  113.7 0.0 copy-done
  113.7 0.6 project.1
  114.3 8.8 %all_to_all.21 = bf16[4,32,640]{2,1,0:T(8,128)(2,1)S(1)} all-to-all(bf16[4,32,640]{2,1,0:T(8,128)(2,1)S(1)} %bitcast.13), channel_id=1, replica_groups=mesh['pool'=16,'y'=4,'core'=2,'head'=4] {'head'}, dimensions={0} | all-to-all | bytes 327680 | tf_op jit(solution)/shard_map/all_to_all | solution.py:352
  123.1 0.6 reduce_sum.12
  (5 shorter events, 0.0 us)
Async XLA Ops:
  0.0 44.5 %copy-start.14 = (s32[16]{0:T(128)S(1)}, s32[16]{0:T(128)}, u32[]{:S(2)}) copy-start(s32[16]{0:T(128)} %owner_ref.11) | copy-start | bytes 196
  0.0 44.5 %copy-start.16 = (s32[16]{0:T(128)S(1)}, s32[16]{0:T(128)}, u32[]{:S(2)}) copy-start(s32[16]{0:T(128)} %lengths_ref.7) | copy-start | bytes 196
  0.0 0.9 copy-start.5
  0.9 0.7 copy-start.11
  1.5 0.7 copy-start.13
  3.5 28.3 %all-to-all-start = ((bf16[16,3,16,128]{3,2,1,0:T(8,128)(2,1)}), bf16[16,3,16,128]{3,2,1,0:T(8,128)(2,1)S(1)}, u32[]{:S(2)}, u32[]{:S(2)}) async-start(bf16[16,3,16,128]{3,2,1,0:T(8,128)(2,1)} %bitcast.1), calls=%async_computation | async-start | bytes 393216 | tf_op jit(solution)/shard_map/all_to_all | solution.py:258
  19.2 20.1 %collective-permute-start = (bf16[1,1024,2,128]{3,2,1,0:T(2,128)(2,1)}, bf16[1,1024,2,128]{3,2,1,0:T(2,128)(2,1)S(1)}, u32[]{:S(2)}, u32[]{:S(2)}) collective-permute-start(bf16[1,1024,2,128]{3,2,1,0:T(2,128)(2,1)} %param.11), channel_id=1, source_target_pairs={{0,4},{4,0},{1,5},{5,1},{2,6},{6,2},{3,7},{7,3},{8,12},{12,8},{9,1... | collective-permute-start | bytes 1572872 | tf_op jit(solution)/shard_map/ppermute | solution.py:240
  22.1 17.2 %collective-permute-start.1 = (bf16[1,1024,2,128]{3,2,1,0:T(2,128)(2,1)}, bf16[1,1024,2,128]{3,2,1,0:T(2,128)(2,1)S(1)}, u32[]{:S(2)}, u32[]{:S(2)}) collective-permute-start(bf16[1,1024,2,128]{3,2,1,0:T(2,128)(2,1)} %param.12), channel_id=1, source_target_pairs={{0,4},{4,0},{1,5},{5,1},{2,6},{6,2},{3,7},{7,3},{8,12},{12,8},{9,1... | collective-permute-start | bytes 1572872 | tf_op jit(solution)/shard_map/ppermute | solution.py:240
  31.8 12.7 %collective-permute-start.6 = (bf16[48,16,128]{2,1,0:T(8,128)(2,1)S(1)}, bf16[48,16,128]{2,1,0:T(8,128)(2,1)S(1)}, u32[]{:S(2)}, u32[]{:S(2)}) collective-permute-start(bf16[48,16,128]{2,1,0:T(8,128)(2,1)S(1)} %bitcast.20), channel_id=1, source_target_pairs={{0,16},{8,24},{16,0},{24,8},{1,17},{9,25},{17,1},{25,9},{2,18},{10... | collective-permute-start | bytes 589832 | tf_op jit(solution)/shard_map/ppermute | solution.py:237
  36.6 14.4 %collective-permute-start.4 = (bf16[48,16,128]{2,1,0:T(8,128)(2,1)S(1)}, bf16[48,16,128]{2,1,0:T(8,128)(2,1)S(1)}, u32[]{:S(2)}, u32[]{:S(2)}) collective-permute-start(bf16[48,16,128]{2,1,0:T(8,128)(2,1)S(1)} %bitcast.21), channel_id=1, source_target_pairs={{0,24},{8,0},{16,8},{24,16},{1,25},{9,1},{17,9},{25,17},{2,26},{10... | collective-permute-start | bytes 589832 | tf_op jit(solution)/shard_map/ppermute | solution.py:237
  39.3 1.0 copy-start.3
  40.4 1.0 copy-start.4
  41.9 16.6 %collective-permute-start.2 = (bf16[48,16,128]{2,1,0:T(8,128)(2,1)S(1)}, bf16[48,16,128]{2,1,0:T(8,128)(2,1)S(1)}, u32[]{:S(2)}, u32[]{:S(2)}) collective-permute-start(bf16[48,16,128]{2,1,0:T(8,128)(2,1)S(1)} %bitcast.22), channel_id=1, source_target_pairs={{0,8},{8,16},{16,24},{24,0},{1,9},{9,17},{17,25},{25,1},{2,10},{10... | collective-permute-start | bytes 589832 | tf_op jit(solution)/shard_map/ppermute | solution.py:237
  48.3 20.7 %collective-permute-start.7 = (bf16[51,16,128]{2,1,0:T(8,128)(2,1)S(1)}, bf16[51,16,128]{2,1,0:T(8,128)(2,1)S(1)}, u32[]{:S(2)}, u32[]{:S(2)}) collective-permute-start(bf16[51,16,128]{2,1,0:T(8,128)(2,1)S(1)} %attend.7), channel_id=1, source_target_pairs={{0,16},{8,24},{16,0},{24,8},{1,17},{9,25},{17,1},{25,9},{2,18},{10... | collective-permute-start | bytes 626696 | tf_op jit(solution)/shard_map/ppermute | solution.py:237
  54.8 14.3 %collective-permute-start.5 = (bf16[51,16,128]{2,1,0:T(8,128)(2,1)S(1)}, bf16[51,16,128]{2,1,0:T(8,128)(2,1)S(1)}, u32[]{:S(2)}, u32[]{:S(2)}) collective-permute-start(bf16[51,16,128]{2,1,0:T(8,128)(2,1)S(1)} %attend.6), channel_id=1, source_target_pairs={{0,8},{8,16},{16,24},{24,0},{1,9},{9,17},{17,25},{25,1},{2,10},{10... | collective-permute-start | bytes 626696 | tf_op jit(solution)/shard_map/ppermute | solution.py:237
  62.3 16.9 %copy-start.1 = (bf16[16,64,2,128]{3,2,1,0:T(2,128)(2,1)S(1)}, bf16[16,64,2,128]{3,2,1,0:T(2,128)(2,1)}, u32[]{:S(2)}) copy-start(bf16[16,64,2,128]{3,2,1,0:T(2,128)(2,1)} %param.13) | copy-start | bytes 1572868
  62.3 16.9 %copy-start.6 = (bf16[16,16,128]{2,1,0:T(8,128)(2,1)S(1)}, bf16[16,16,128]{2,1,0:T(8,128)(2,1)}, u32[]{:S(2)}) copy-start(bf16[16,16,128]{2,1,0:T(8,128)(2,1)} %q_ref.3) | copy-start | bytes 196612
  62.3 16.9 %copy-start.15 = (s32[16]{0:T(128)S(1)}, s32[16]{0:T(128)}, u32[]{:S(2)}) copy-start(s32[16]{0:T(128)} %length_ref.1) | copy-start | bytes 196
  62.4 29.5 %copy-start.12 = (s32[16,1]{0,1:T(1,128)S(1)}, s32[16,1]{0,1:T(1,128)}, u32[]{:S(2)}) copy-start(s32[16,1]{0,1:T(1,128)} %param.15) | copy-start | bytes 196
  62.4 6.7 %collective-permute-start.3 = (bf16[51,16,128]{2,1,0:T(8,128)(2,1)S(1)}, bf16[51,16,128]{2,1,0:T(8,128)(2,1)S(1)}, u32[]{:S(2)}, u32[]{:S(2)}) collective-permute-start(bf16[51,16,128]{2,1,0:T(8,128)(2,1)S(1)} %attend.5), channel_id=1, source_target_pairs={{0,24},{8,0},{16,8},{24,16},{1,25},{9,1},{17,9},{25,17},{2,26},{10... | collective-permute-start | bytes 626696 | tf_op jit(solution)/shard_map/ppermute | solution.py:237
  69.0 44.7 %copy-start = (bf16[2048,640]{1,0:T(8,128)(2,1)S(1)}, bf16[2048,640]{1,0:T(8,128)(2,1)}, u32[]{:S(2)}) copy-start(bf16[2048,640]{1,0:T(8,128)(2,1)} %w_ref.1) | copy-start | bytes 7864324
  70.5 21.4 %all-to-all-start.1 = ((bf16[16,56,128]{2,1,0:T(8,128)(2,1)}), bf16[16,56,128]{2,1,0:T(8,128)(2,1)S(1)}, u32[]{:S(2)}, u32[]{:S(2)}) async-start(bf16[16,56,128]{2,1,0:T(8,128)(2,1)} %bitcast.7), calls=%async_computation.1 | async-start | bytes 458752 | tf_op jit(solution)/shard_map/all_to_all | solution.py:316
  79.3 1.0 copy-start.2
  84.7 0.7 copy-start.7
  85.4 0.6 copy-start.9
  91.8 0.9 copy-start.8
  92.7 0.9 copy-start.10
  103.1 10.6 %collective-permute-start.8 = (bf16[4,16,2048]{2,1,0:T(8,128)(2,1)S(1)}, bf16[4,16,2048]{2,1,0:T(8,128)(2,1)S(1)}, u32[]{:S(2)}, u32[]{:S(2)}) collective-permute-start(bf16[4,16,2048]{2,1,0:T(8,128)(2,1)S(1)} %all_to_all.20.own_ref), channel_id=1, source_target_pairs={{0,4},{4,0},{1,5},{5,1},{2,6},{6,2},{3,7},{7,3},{8,12},{12,8},{9,1... | collective-permute-start | bytes 786440 | tf_op jit(solution)/shard_map/ppermute | solution.py:240

commit v2 on v1

--- a/solution.py
+++ b/solution.py
@@ -39,43 +39,39 @@
     return owner, place
 
 
-def dispatch_kernel(row_prefix_ref, owner_ref, q_ref, out_ref, count_ref):
+def dispatch_kernel(
+    row_prefix_ref, owner_ref, q_ref, k_ref, v_ref, out_ref, packed_ref, held, count_ref
+):
     for p in range(owner_ref.shape[0]):
         count_ref[p] = 0
     out_ref[...] = jnp.zeros_like(out_ref)
     for r in range(q_ref.shape[0]):
         owner, place = slot_of(r, row_prefix_ref, owner_ref, count_ref)
         out_ref[owner * CAP + place] = q_ref[r]
-
-
-def unmix_kernel(k0_ref, k1_ref, v0_ref, v1_ref, k_ref, v_ref, scratch):
-    length = k0_ref.shape[0] // 2
-    for i, (sources, target) in enumerate((((k0_ref, k1_ref), k_ref), ((v0_ref, v1_ref), v_ref))):
-        for n, source in enumerate(sources):
-            held = scratch.at[2 * i + n]
-            held[...] = source[...].astype(F32)
-            for g in range(2):
-                target[g, n * length : (n + 1) * length, :] = held[
-                    pl.ds(g, length, stride=2), :
-                ].astype(BF16)
-
-
-def attend_kernel(owner_ref, lengths_ref, q_ref, k_ref, v_ref, out_ref):
+    length = packed_ref.shape[1]
+    for n, source in enumerate((k_ref, v_ref)):
+        held[n] = source[...].astype(F32)
+        for g in range(2):
+            packed_ref[2 * n + g] = held[n, pl.ds(g, length, stride=2), :].astype(BF16)
+
+
+def attend_kernel(sources, owner_ref, lengths_ref, q_ref, *refs):
+    blocks, out_ref = refs[:-1], refs[-1]
     slots = q_ref.shape[0]
     step_slots = math.gcd(24, slots)
-    span = k_ref.shape[1]
-    part = span // 2
+    span = blocks[0].shape[1]
     pool = lax.axis_index("pool")
     core = lax.axis_index("core")
-    first = lax.axis_index("y") * 2
+    across = lax.axis_index("y")
     own_length = jnp.int32(0)
     for p in range(owner_ref.shape[0]):
         own_length += jnp.where(owner_ref[p] == pool, lengths_ref[p], 0)
     column = lax.broadcasted_iota(jnp.int32, (1, span), 1)
-    token = jnp.where(
-        column < part, column + (first + core) * part, column + (first - core) * part
-    )
-    bias = jnp.where(token < own_length, 0.0, LOWEST).astype(F32)
+    biases = []
+    for dy, dc in sources:
+        at = (across + dy * (1 - 2 * (across & 1))) * 2 + core + dc * (1 - 2 * core)
+        biases.append(jnp.where(column + at * span < own_length, 0.0, LOWEST).astype(F32))
+    ones = jnp.ones((span, HD), BF16)
     lane = lax.broadcasted_iota(jnp.int32, (GROUP, 128), 1)
 
     def step(j, packed):
@@ -85,16 +81,29 @@
         filled = []
         for g in range(2):
             q = q_all[:, g * GROUP : (g + 1) * GROUP, :].reshape(step_slots * GROUP, HD)
-            scores = (
+            q = q.astype(BF16)
+            scores = [
                 lax.dot_general(
-                    q.astype(BF16), k_ref[g], (((1,), (1,)), ((), ())), preferred_element_type=F32
+                    q, block[g], (((1,), (1,)), ((), ())), preferred_element_type=F32
                 )
                 + bias
+                for block, bias in zip(blocks, biases)
+            ]
+            peak = functools.reduce(
+                jnp.maximum, [jnp.max(part, axis=1, keepdims=True) for part in scores]
             )
-            peak = jnp.maximum(jnp.max(scores, axis=1, keepdims=True), 0.1 * LOWEST)
-            weights = jnp.exp2((scores - peak) * (SCALE * LOG2E)).astype(BF16)
-            values = jnp.concatenate([v_ref[g], jnp.ones((span, HD), BF16)], axis=1)
-            both = jnp.dot(weights, values, preferred_element_type=F32)
+            peak = jnp.maximum(peak, 0.1 * LOWEST)
+            both = functools.reduce(
+                jnp.add,
+                [
+                    jnp.dot(
+                        jnp.exp2((part - peak) * (SCALE * LOG2E)).astype(BF16),
+                        jnp.concatenate([block[2 + g], ones], axis=1),
+                        preferred_element_type=F32,
+                    )
+                    for part, block in zip(scores, blocks)
+                ],
+            )
             total = both[:, HD:]
             live = total > 0
             safe = jnp.where(live, total, 1.0)
@@ -114,8 +123,8 @@
         out_ref[slots + i] = plane.astype(BF16)
 
 
-def merge_kernel(a_ref, b_ref, c_ref, d_ref, out_ref):
-    blocks = (a_ref, b_ref, c_ref, d_ref)
+def merge_kernel(a_ref, b_ref, c_ref, out_ref):
+    blocks = (a_ref, b_ref, c_ref)
     slots = a_ref.shape[0] - 3
     pools = slots // CAP
     lses = [
@@ -199,18 +208,10 @@
             out_ref[n, :, h * HD : (h + 1) * HD] = piece
 
 
-def project_kernel(own_ref, other_ref, w_ref, out_ref):
-    count, rows, depth = own_ref.shape
-    core = lax.axis_index("core")
-    both = jnp.concatenate(
-        [own_ref[...].reshape(count * rows, depth), other_ref[...].reshape(count * rows, depth)],
-        axis=0,
-    )
-    terms = jnp.dot(both, w_ref[...], preferred_element_type=F32).astype(BF16)
-    terms = terms.reshape(2, count, rows, -1)
-    for n in range(count):
-        out_ref[n, core] = terms[0, n]
-        out_ref[n, 1 - core] = terms[1, n]
+def project_kernel(attended_ref, w_ref, out_ref):
+    out_ref[...] = jnp.dot(
+        attended_ref[...], w_ref[...], preferred_element_type=F32
+    ).astype(BF16)
 
 
 def body(
@@ -233,45 +234,73 @@
     columns = out_weight.shape[1]
     shape = jax.ShapeDtypeStruct
 
-    def turn(value, by):
-        return lax.ppermute(value, "y", [(i, (i + by) % ring) for i in range(ring)])
-
-    def swap(value):
-        return lax.ppermute(value, "core", [(0, 1), (1, 0)])
-
-    outgoing = pl.pallas_call(
+    def meet(value, axis, partner):
+        return lax.ppermute(value, axis, list(enumerate(partner)))
+
+    length = prefix_keys.shape[1]
+    outgoing, own = pl.pallas_call(
         dispatch_kernel,
-        out_shape=shape((slots, heads, hdim), BF16),
-        in_specs=[SMEM, SMEM, VMEM],
-        out_specs=VMEM,
-        scratch_shapes=[pltpu.SMEM((pools,), jnp.int32)],
-        compiler_params=params(8),
-        cost_estimate=pl.CostEstimate(flops=0, bytes_accessed=300_000, transcendentals=0),
+        out_shape=[shape((slots, heads, hdim), BF16), shape((4, length, hdim), BF16)],
+        in_specs=[SMEM, SMEM, VMEM, VMEM, VMEM],
+        out_specs=[VMEM] * 2,
+        scratch_shapes=[pltpu.VMEM((2, 2 * length, hdim), F32), pltpu.SMEM((pools,), jnp.int32)],
+        compiler_params=params(60),
+        cost_estimate=pl.CostEstimate(flops=0, bytes_accessed=3_000_000, transcendentals=0),
         name="dispatch",
-    )(row_prefix, owner_map, queries)
-
-    own_keys = prefix_keys.reshape(-1, hdim)
-    own_values = prefix_values.reshape(-1, hdim)
-    other_keys = swap(prefix_keys).reshape(-1, hdim)
-    other_values = swap(prefix_values).reshape(-1, hdim)
+    )(row_prefix, owner_map, queries, prefix_keys.reshape(-1, hdim), prefix_values.reshape(-1, hdim))
 
     arrived = lax.all_to_all(
         outgoing.reshape(pools, CAP, heads, hdim), "pool", split_axis=0, concat_axis=0, tiled=True
     ).reshape(slots, heads, hdim)
-    asked = {by: turn(arrived, by) for by in (1, ring - 1, 2)}
-    asked[0] = arrived
-
-    span = own_keys.shape[0]
-    keys, values = pl.pallas_call(
-        unmix_kernel,
-        out_shape=[shape((2, span, hdim), BF16)] * 2,
-        in_specs=[VMEM] * 4,
-        out_specs=[VMEM] * 2,
-        scratch_shapes=[pltpu.VMEM((4, span, hdim), F32)],
-        compiler_params=params(16),
-        cost_estimate=pl.CostEstimate(flops=0, bytes_accessed=4_000_000, transcendentals=0),
-        name="unmix",
-    )(own_keys, other_keys, own_values, other_values)
+    mirror = [ring - 1 - i for i in range(ring)]
+    asked = meet(arrived, "y", mirror)
+
+    pair = meet(own, "y", [i ^ 1 for i in range(ring)])
+    pair, arrived_later = lax.optimization_barrier((pair, arrived))
+    blocks = {
+        (0, 0): own,
+        (0, 1): meet(own, "core", [1, 0]),
+        (1, 0): pair,
+        (1, 1): meet(pair, "core", [1, 0]),
+    }
+
+    def attend(q, *sources):
+        span = len(sources) * length
+        return pl.pallas_call(
+            functools.partial(attend_kernel, sources),
+            out_shape=shape((slots + 3, heads, hdim), BF16),
+            in_specs=[SMEM, SMEM, VMEM] + [VMEM] * len(sources),
+            out_specs=VMEM,
+            compiler_params=params(30),
+            cost_estimate=pl.CostEstimate(
+                flops=6 * slots * heads * span * hdim,
+                bytes_accessed=3_000_000,
+                transcendentals=slots * heads * span,
+            ),
+            name="attend",
+        )(owner_map, prefix_lengths, q, *(blocks[source] for source in sources))
+
+    near, far = ((0, 0), (0, 1)), ((1, 0), (1, 1))
+    near_part, asked = lax.optimization_barrier((attend(arrived, *near), asked))
+    answer = meet(attend(asked, *near, *far), "y", mirror)
+    far_part = attend(arrived_later, *far)
+    merged = pl.pallas_call(
+        merge_kernel,
+        out_shape=shape((pools * (CAP * heads + GROUP), hdim), BF16),
+        in_specs=[VMEM] * 3,
+        out_specs=VMEM,
+        compiler_params=params(8),
+        cost_estimate=pl.CostEstimate(flops=0, bytes_accessed=1_000_000, transcendentals=0),
+        name="merge",
+    )(near_part, far_part, answer)
+    merged, queries_later = lax.optimization_barrier((merged, queries))
+    returned = lax.all_to_all(
+        merged.reshape(pools, CAP * heads + GROUP, hdim),
+        "pool",
+        split_axis=0,
+        concat_axis=0,
+        tiled=True,
+    ).reshape(-1, hdim)
 
     suffix_out, suffix_lse = pl.pallas_call(
         suffix_kernel,
@@ -285,45 +314,14 @@
         name="suffix",
     )(
         suffix_lengths,
-        queries,
+        queries_later,
         suffix_keys.reshape(rows, -1, hdim),
         suffix_values.reshape(rows, -1, hdim),
     )
 
-    attend = pl.pallas_call(
-        attend_kernel,
-        out_shape=shape((slots + 3, heads, hdim), BF16),
-        in_specs=[SMEM, SMEM, VMEM, VMEM, VMEM],
-        out_specs=VMEM,
-        compiler_params=params(24),
-        cost_estimate=pl.CostEstimate(
-            flops=6 * slots * heads * span * hdim,
-            bytes_accessed=3_000_000,
-            transcendentals=slots * heads * span,
-        ),
-        name="attend",
-    )
-    parts = {by: attend(owner_map, prefix_lengths, q, keys, values) for by, q in asked.items()}
-    merged = pl.pallas_call(
-        merge_kernel,
-        out_shape=shape((pools * (CAP * heads + GROUP), hdim), BF16),
-        in_specs=[VMEM] * 4,
-        out_specs=VMEM,
-        compiler_params=params(8),
-        cost_estimate=pl.CostEstimate(flops=0, bytes_accessed=1_000_000, transcendentals=0),
-        name="merge",
-    )(parts[0], *(turn(parts[by], -by) for by in (1, ring - 1, 2)))
-    returned = lax.all_to_all(
-        merged.reshape(pools, CAP * heads + GROUP, hdim),
-        "pool",
-        split_axis=0,
-        concat_axis=0,
-        tiled=True,
-    ).reshape(-1, hdim)
-
     attended = pl.pallas_call(
         combine_kernel,
-        out_shape=shape((ring, rows, heads * hdim), BF16),
+        out_shape=shape((2 * ring, rows, heads * hdim), BF16),
         in_specs=[SMEM, SMEM, VMEM, VMEM, VMEM],
         out_specs=VMEM,
         scratch_shapes=[
@@ -331,15 +329,15 @@
             pltpu.VMEM((rows * heads, hdim), F32),
             pltpu.SMEM((pools,), jnp.int32),
         ],
-        compiler_params=params(8),
+        compiler_params=params(60),
         cost_estimate=pl.CostEstimate(flops=0, bytes_accessed=1_000_000, transcendentals=0),
         name="combine",
     )(row_prefix, owner_map, returned, suffix_out, suffix_lse)
-    gathered = lax.all_to_all(attended, "y", split_axis=0, concat_axis=0, tiled=True)
+    gathered = lax.all_to_all(attended, ("y", "core"), split_axis=0, concat_axis=0, tiled=True)
     terms = pl.pallas_call(
         project_kernel,
-        out_shape=shape((ring, 2, rows, columns), BF16),
-        in_specs=[VMEM] * 3,
+        out_shape=shape((2 * ring * rows, columns), BF16),
+        in_specs=[VMEM] * 2,
         out_specs=VMEM,
         compiler_params=params(16),
         cost_estimate=pl.CostEstimate(
@@ -348,7 +346,7 @@
             transcendentals=0,
         ),
         name="project",
-    )(gathered, swap(gathered), out_weight)
+    )(gathered.reshape(-1, heads * hdim), out_weight)
     shared = lax.all_to_all(
         terms.reshape(lax.axis_size("head"), -1, columns), "head", split_axis=0, concat_axis=0, tiled=True
     )

time: 125 us -> 122 us (0.976)
  starting transfers between devices: 58.1 us -> 44 us
  blocking collectives: 17.4 us -> 27.4 us
  waiting for transfers between devices: 14.7 us -> 17.6 us
  local copies, waits for them, and re-layouts: 8.43 us -> 5.58 us
  Pallas kernels: 24.1 us -> 25.6 us
    ppermute x9 -> x5, starting transfers between devices: 33.6 us -> 21.3 us  [meet(): return lax.ppermute(value, axis, list(enumerate(partner)))]
    all_to_all x1, blocking collectives: 8.62 us -> 18.6 us  [body(): lax.all_to_all(attended, ('y', 'core'), split_axis=0, concat_axis=0, tile...]
    unnamed x34 -> x22, local copies, waits for them, and re-layouts: 8.43 us -> 5.58 us
    pallas_call x8 -> x6, Pallas kernels: 18.3 us -> 19.9 us  [the longest x3 14.6 us: attend(): pl.pallas_call(functools.partial(attend_kernel, sources), out_shape=shape...]
    all_to_all x1, waiting for transfers between devices: 7.75 us -> 9.22 us  [body(): lax.all_to_all(outgoing.reshape(pools, CAP, heads, hdim), 'pool', split_a...]
    ppermute x9 -> x5, waiting for transfers between devices: 1.16 us -> 2.56 us  [meet(): return lax.ppermute(value, axis, list(enumerate(partner)))]
  transfers between devices with their start and end apart: 11 -> 7, of which waited for: 3 -> 3; matrix products, arithmetic and copies ran while one was open for 0% -> 0% of each run, Pallas kernels for 16% -> 10%
where the time goes in v2:
time: 122 us; the launch traced here: 121 us
  starting transfers between devices  44 us (36%)
  blocking collectives  27.4 us (22%)
  Pallas kernels  25.6 us (21%)
  waiting for transfers between devices  17.6 us (14%)
  local copies, waits for them, and re-layouts  5.58 us (5%)
    ppermute x5, starting transfers between devices, meet(): return lax.ppermute(value, axis, list(enumerate(partner)))  21.3 us
    all_to_all x1, blocking collectives, body(): lax.all_to_all(attended, ('y', 'core'), split_axis=0, concat_axis=0, tile...  18.6 us
    all_to_all x1, starting transfers between devices, body(): lax.all_to_all(outgoing.reshape(pools, CAP, heads, hdim), 'pool', split_a...  14.9 us
    pallas_call x3, Pallas kernels, attend(): pl.pallas_call(functools.partial(attend_kernel, sources), out_shape=shape...  14.6 us
    all_to_all x1, waiting for transfers between devices, body(): lax.all_to_all(outgoing.reshape(pools, CAP, heads, hdim), 'pool', split_a...  9.22 us
    all_to_all x1, blocking collectives, body(): lax.all_to_all(terms.reshape(lax.axis_size('head'), -1, columns), 'head',...  8.82 us
    all_to_all x1, starting transfers between devices, body(): lax.all_to_all(merged.reshape(pools, CAP * heads + GROUP, hdim), 'pool',...  7.84 us
    all_to_all x1, waiting for transfers between devices, body(): lax.all_to_all(merged.reshape(pools, CAP * heads + GROUP, hdim), 'pool',...  5.82 us
  transfers between devices with their start and end apart: 7, of which 3 were waited for; matrix products, arithmetic and copies ran while one was open for 0% of the time, Pallas kernels for 10%

profile of v2, /device:TPU:1, one launch (start us, length us, event | category | flops | bytes accessed | tf_op | source)
XLA Modules:
  0.0 121.0 jit_solution(13559966454585543809)
XLA Ops:
  0.0 2.5 %dispatch.1 = (bf16[48,16,128]{2,1,0:T(8,128)(2,1)}, bf16[4,1024,128]{2,1,0:T(8,128)(2,1)}) custom-call(s32[16]{0:T(128)} %bitcast.22, s32[16]{0:T(128)} %owner_ref.9, bf16[16,16,128]{2,1,0:T(8,128)(2,1)} %q_ref.2, bf16[2048,128]{1,0:T(8,128)(2,1)} %bitcast.19, bf16[2048,128]{1,0:T(8,128)(2,1)} %bitcast.20), custom_call_target="tpu_custom_call" | custom-call | bytes 3000000 | tf_op jit(solution)/shard_map/dispatch/pallas_call | solution.py:241
  2.5 4.0 %collective-permute-start.2 = (bf16[4,1024,128]{2,1,0:T(8,128)(2,1)}, bf16[4,1024,128]{2,1,0:T(8,128)(2,1)S(1)}, u32[]{:S(2)}, u32[]{:S(2)}) collective-permute-start(bf16[4,1024,128]{2,1,0:T(8,128)(2,1)} %get-tuple-element.16.refs_0_), channel_id=1, source_target_pairs={{0,8},{8,0},{16,24},{24,16},{1,9},{9,1},{17,25},{25,17},{2,10},{10... | collective-permute-start | bytes 3145736 | tf_op jit(solution)/shard_map/ppermute | solution.py:238
  6.5 14.9 %all-to-all-start = ((bf16[16,3,16,128]{3,2,1,0:T(8,128)(2,1)}), bf16[16,3,16,128]{3,2,1,0:T(8,128)(2,1)S(1)}, u32[]{:S(2)}, u32[]{:S(2)}) async-start(bf16[16,3,16,128]{3,2,1,0:T(8,128)(2,1)} %bitcast.21), calls=%async_computation | async-start | bytes 393216 | tf_op jit(solution)/shard_map/all_to_all | solution.py:252
  21.4 3.1 %collective-permute-start = (bf16[4,1024,128]{2,1,0:T(8,128)(2,1)}, bf16[4,1024,128]{2,1,0:T(8,128)(2,1)S(1)}, u32[]{:S(2)}, u32[]{:S(2)}) collective-permute-start(bf16[4,1024,128]{2,1,0:T(8,128)(2,1)} %get-tuple-element.16.refs_0_), channel_id=1, source_target_pairs={{0,4},{4,0},{1,5},{5,1},{2,6},{6,2},{3,7},{7,3},{8,12},{12,8},{9,1... | collective-permute-start | bytes 3145736 | tf_op jit(solution)/shard_map/ppermute | solution.py:238
  24.6 9.2 %all-to-all-done = bf16[16,3,16,128]{3,2,1,0:T(8,128)(2,1)S(1)} async-done(((bf16[16,3,16,128]{3,2,1,0:T(8,128)(2,1)}), bf16[16,3,16,128]{3,2,1,0:T(8,128)(2,1)S(1)}, u32[]{:S(2)}, u32[]{:S(2)}) %all-to-all-start) | async-done | bytes 196640 | tf_op jit(solution)/shard_map/all_to_all | solution.py:252
  33.8 0.0 collective-permute-done.2.refs_0_.refs_2_
  33.8 7.0 %collective-permute-start.3 = (bf16[4,1024,128]{2,1,0:T(8,128)(2,1)S(1)}, bf16[4,1024,128]{2,1,0:T(8,128)(2,1)S(1)}, u32[]{:S(2)}, u32[]{:S(2)}) collective-permute-start(bf16[4,1024,128]{2,1,0:T(8,128)(2,1)S(1)} %collective-permute-done.2.refs_0_.refs_2_), channel_id=1, source_target_pairs={{0,4},{4,0},{1,5},{5,1},{2,6},{6,2},{3,7},{7,3},{8,12},{12,8},{9,1... | collective-permute-start | bytes 3145736 | tf_op jit(solution)/shard_map/ppermute | solution.py:238
  40.8 3.8 %collective-permute-start.1 = (bf16[48,16,128]{2,1,0:T(8,128)(2,1)S(1)}, bf16[48,16,128]{2,1,0:T(8,128)(2,1)S(1)}, u32[]{:S(2)}, u32[]{:S(2)}) collective-permute-start(bf16[48,16,128]{2,1,0:T(8,128)(2,1)S(1)} %bitcast.15), channel_id=1, source_target_pairs={{0,24},{8,16},{16,8},{24,0},{1,25},{9,17},{17,9},{25,1},{2,26},{10... | collective-permute-start | bytes 589832 | tf_op jit(solution)/shard_map/ppermute | solution.py:238
  44.6 0.0 collective-permute-done.refs_1_
  44.6 0.0 copy-start.6
  44.6 0.6 copy-done.6
  45.3 0.0 copy-start.8
  45.3 1.2 %copy-done.8 = bf16[4,1024,128]{2,1,0:T(8,128)(2,1)S(1)} copy-done((bf16[4,1024,128]{2,1,0:T(8,128)(2,1)S(1)}, bf16[4,1024,128]{2,1,0:T(8,128)(2,1)}, u32[]{:S(2)}) %copy-start.8) | copy-done | bytes 1048600
  46.5 0.0 copy-start.9
  46.5 0.7 copy-done.9
  47.2 3.9 %attend.3.a_ref = bf16[51,16,128]{2,1,0:T(8,128)(2,1)S(1)} custom-call(s32[16]{0:T(128)S(1)} %copy-done.6, s32[16]{0:T(128)S(1)} %copy-done.9, bf16[48,16,128]{2,1,0:T(8,128)(2,1)S(1)} %bitcast.16, bf16[4,1024,128]{2,1,0:T(8,128)(2,1)S(1)} %copy-done.8, bf16[4,1024,128]{2,1,0:T(8,128)(2,1)S(1)} %collective-permute-done.refs_1_), custom_call_target="tpu_custom_call" | custom-call | flops 1207959552 | bytes 3000000 | tf_op jit(solution)/shard_map/attend/pallas_call | solution.py:269
  51.0 0.0 collective-permute-done.1.q_ref
  51.0 0.0 collective-permute-done.3.refs_1_.refs_3_
  51.0 6.9 %attend.5 = bf16[51,16,128]{2,1,0:T(8,128)(2,1)S(1)} custom-call(s32[16]{0:T(128)S(1)} %copy-done.6, s32[16]{0:T(128)S(1)} %copy-done.9, bf16[48,16,128]{2,1,0:T(8,128)(2,1)S(1)} %collective-permute-done.1.q_ref, bf16[4,1024,128]{2,1,0:T(8,128)(2,1)S(1)} %copy-done.8, bf16[4,1024,128]{2,1,0:T(8,128)(2,1)S(1)} %collective-permute-done.refs_1_, ...), custom_call_target="tpu_custom_call" | custom-call | flops 2415919104 | bytes 3000000 | tf_op jit(solution)/shard_map/attend/pallas_call | solution.py:269
  58.0 0.0 copy-start.1
  58.0 0.0 copy-start.3
  58.0 0.0 copy-start.7
  58.0 3.3 %collective-permute-start.4 = (bf16[51,16,128]{2,1,0:T(8,128)(2,1)S(1)}, bf16[51,16,128]{2,1,0:T(8,128)(2,1)S(1)}, u32[]{:S(2)}, u32[]{:S(2)}) collective-permute-start(bf16[51,16,128]{2,1,0:T(8,128)(2,1)S(1)} %attend.5), channel_id=1, source_target_pairs={{0,24},{8,16},{16,8},{24,0},{1,25},{9,17},{17,9},{25,1},{2,26},{10... | collective-permute-start | bytes 626696 | tf_op jit(solution)/shard_map/ppermute | solution.py:238
  61.3 3.8 %attend.4.b_ref = bf16[51,16,128]{2,1,0:T(8,128)(2,1)S(1)} custom-call(s32[16]{0:T(128)S(1)} %copy-done.6, s32[16]{0:T(128)S(1)} %copy-done.9, bf16[48,16,128]{2,1,0:T(8,128)(2,1)S(1)} %bitcast.17, bf16[4,1024,128]{2,1,0:T(8,128)(2,1)S(1)} %collective-permute-done.2.refs_0_.refs_2_, bf16[4,1024,128]{2,1,0:T(8,128)(2,1)S(1)} %collective-permute-done.3.refs_1_.refs_3_), custom_call_target="tpu_custom_call" | custom-call | flops 1207959552 | bytes 3000000 | tf_op jit(solution)/shard_map/attend/pallas_call | solution.py:269
  65.2 0.0 copy-start
  65.2 2.5 %collective-permute-done.4.c_ref = bf16[51,16,128]{2,1,0:T(8,128)(2,1)S(1)} collective-permute-done((bf16[51,16,128]{2,1,0:T(8,128)(2,1)S(1)}, bf16[51,16,128]{2,1,0:T(8,128)(2,1)S(1)}, u32[]{:S(2)}, u32[]{:S(2)}) %collective-permute-start.4) | collective-permute-done | bytes 208928 | tf_op jit(solution)/shard_map/ppermute | solution.py:238
  67.7 1.3 %merge.1 = bf16[896,128]{1,0:T(8,128)(2,1)} custom-call(bf16[51,16,128]{2,1,0:T(8,128)(2,1)S(1)} %attend.3.a_ref, bf16[51,16,128]{2,1,0:T(8,128)(2,1)S(1)} %attend.4.b_ref, bf16[51,16,128]{2,1,0:T(8,128)(2,1)S(1)} %collective-permute-done.4.c_ref), custom_call_target="tpu_custom_call" | custom-call | bytes 1000000 | tf_op jit(solution)/shard_map/merge/pallas_call | solution.py:287
  69.0 7.8 %all-to-all-start.1 = ((bf16[16,56,128]{2,1,0:T(8,128)(2,1)}), bf16[16,56,128]{2,1,0:T(8,128)(2,1)S(1)}, u32[]{:S(2)}, u32[]{:S(2)}) async-start(bf16[16,56,128]{2,1,0:T(8,128)(2,1)} %bitcast.5), calls=%async_computation.1 | async-start | bytes 458752 | tf_op jit(solution)/shard_map/all_to_all | solution.py:297
  76.8 0.0 copy-done.1
  76.8 0.0 copy-done.3
  76.8 0.0 copy-done.7
  76.9 0.0 copy-start.2
  76.9 1.0 copy-done.2
  77.9 4.4 %suffix.1 = (f32[16,16,128]{2,1,0:T(8,128)S(1)}, f32[16,16,128]{2,1,0:T(8,128)S(1)}) custom-call(s32[16]{0:T(128)S(1)} %copy-done.7, bf16[16,16,128]{2,1,0:T(8,128)(2,1)S(1)} %copy-done.3, bf16[16,128,128]{2,1,0:T(8,128)(2,1)S(1)} %bitcast.13, bf16[16,128,128]{2,1,0:T(8,128)(2,1)S(1)} %bitcast.14), custom_call_target="tpu_custom_call" | custom-call | flops 16777216 | bytes 2000000 | tf_op jit(solution)/shard_map/suffix/pallas_call | solution.py:305
  82.3 0.0 copy-start.4
  82.3 0.7 copy-done.4
  82.9 0.0 copy-start.5
  82.9 0.7 copy-done.5
  83.6 5.8 %all-to-all-done.1 = bf16[16,56,128]{2,1,0:T(8,128)(2,1)S(1)} async-done(((bf16[16,56,128]{2,1,0:T(8,128)(2,1)}), bf16[16,56,128]{2,1,0:T(8,128)(2,1)S(1)}, u32[]{:S(2)}, u32[]{:S(2)}) %all-to-all-start.1) | async-done | bytes 229408 | tf_op jit(solution)/shard_map/all_to_all | solution.py:297
  89.4 0.0 copy-start.10
  89.4 0.7 copy-done.10
  90.1 2.2 %combine.1 = bf16[8,16,2048]{2,1,0:T(8,128)(2,1)} custom-call(s32[16]{0:T(128)} %bitcast.23, s32[16]{0:T(128)} %owner_ref.9, bf16[896,128]{1,0:T(8,128)(2,1)} %bitcast.18, f32[16,16,128]{2,1,0:T(8,128)} %copy-done.4, f32[16,16,128]{2,1,0:T(8,128)} %copy-done.5), custom_call_target="tpu_custom_call" | custom-call | bytes 1000000 | tf_op jit(solution)/shard_map/combine/pallas_call | solution.py:322
  92.3 18.6 %all_to_all.20 = bf16[8,16,2048]{2,1,0:T(8,128)(2,1)S(1)} all-to-all(bf16[8,16,2048]{2,1,0:T(8,128)(2,1)} %combine.1), channel_id=1, replica_groups=mesh['pool'=16,'y'=4,'core'=2,'head'=4] {'y','core'}, dimensions={0} | all-to-all | bytes 1048576 | tf_op jit(solution)/shard_map/all_to_all | solution.py:336
  110.9 0.0 copy-done
  110.9 0.6 project.1
  111.5 8.8 %all_to_all.21 = bf16[4,32,640]{2,1,0:T(8,128)(2,1)S(1)} all-to-all(bf16[4,32,640]{2,1,0:T(8,128)(2,1)S(1)} %bitcast.12), channel_id=1, replica_groups=mesh['pool'=16,'y'=4,'core'=2,'head'=4] {'head'}, dimensions={0} | all-to-all | bytes 327680 | tf_op jit(solution)/shard_map/all_to_all | solution.py:350
  120.3 0.6 reduce_sum.12
Async XLA Ops:
  2.5 31.3 %collective-permute-start.2 = (bf16[4,1024,128]{2,1,0:T(8,128)(2,1)}, bf16[4,1024,128]{2,1,0:T(8,128)(2,1)S(1)}, u32[]{:S(2)}, u32[]{:S(2)}) collective-permute-start(bf16[4,1024,128]{2,1,0:T(8,128)(2,1)} %get-tuple-element.16.refs_0_), channel_id=1, source_target_pairs={{0,8},{8,0},{16,24},{24,16},{1,9},{9,1},{17,25},{25,17},{2,10},{10... | collective-permute-start | bytes 3145736 | tf_op jit(solution)/shard_map/ppermute | solution.py:238
  6.5 27.3 %all-to-all-start = ((bf16[16,3,16,128]{3,2,1,0:T(8,128)(2,1)}), bf16[16,3,16,128]{3,2,1,0:T(8,128)(2,1)S(1)}, u32[]{:S(2)}, u32[]{:S(2)}) async-start(bf16[16,3,16,128]{3,2,1,0:T(8,128)(2,1)} %bitcast.21), calls=%async_computation | async-start | bytes 393216 | tf_op jit(solution)/shard_map/all_to_all | solution.py:252
  21.4 23.2 %collective-permute-start = (bf16[4,1024,128]{2,1,0:T(8,128)(2,1)}, bf16[4,1024,128]{2,1,0:T(8,128)(2,1)S(1)}, u32[]{:S(2)}, u32[]{:S(2)}) collective-permute-start(bf16[4,1024,128]{2,1,0:T(8,128)(2,1)} %get-tuple-element.16.refs_0_), channel_id=1, source_target_pairs={{0,4},{4,0},{1,5},{5,1},{2,6},{6,2},{3,7},{7,3},{8,12},{12,8},{9,1... | collective-permute-start | bytes 3145736 | tf_op jit(solution)/shard_map/ppermute | solution.py:238
  33.8 17.2 %collective-permute-start.3 = (bf16[4,1024,128]{2,1,0:T(8,128)(2,1)S(1)}, bf16[4,1024,128]{2,1,0:T(8,128)(2,1)S(1)}, u32[]{:S(2)}, u32[]{:S(2)}) collective-permute-start(bf16[4,1024,128]{2,1,0:T(8,128)(2,1)S(1)} %collective-permute-done.2.refs_0_.refs_2_), channel_id=1, source_target_pairs={{0,4},{4,0},{1,5},{5,1},{2,6},{6,2},{3,7},{7,3},{8,12},{12,8},{9,1... | collective-permute-start | bytes 3145736 | tf_op jit(solution)/shard_map/ppermute | solution.py:238
  40.8 10.2 %collective-permute-start.1 = (bf16[48,16,128]{2,1,0:T(8,128)(2,1)S(1)}, bf16[48,16,128]{2,1,0:T(8,128)(2,1)S(1)}, u32[]{:S(2)}, u32[]{:S(2)}) collective-permute-start(bf16[48,16,128]{2,1,0:T(8,128)(2,1)S(1)} %bitcast.15), channel_id=1, source_target_pairs={{0,24},{8,16},{16,8},{24,0},{1,25},{9,17},{17,9},{25,1},{2,26},{10... | collective-permute-start | bytes 589832 | tf_op jit(solution)/shard_map/ppermute | solution.py:238
  44.6 0.7 copy-start.6
  45.3 1.2 %copy-start.8 = (bf16[4,1024,128]{2,1,0:T(8,128)(2,1)S(1)}, bf16[4,1024,128]{2,1,0:T(8,128)(2,1)}, u32[]{:S(2)}) copy-start(bf16[4,1024,128]{2,1,0:T(8,128)(2,1)} %get-tuple-element.16.refs_0_) | copy-start | bytes 3145732
  46.5 0.7 copy-start.9
  58.0 18.8 %copy-start.1 = (bf16[16,64,2,128]{3,2,1,0:T(2,128)(2,1)S(1)}, bf16[16,64,2,128]{3,2,1,0:T(2,128)(2,1)}, u32[]{:S(2)}) copy-start(bf16[16,64,2,128]{3,2,1,0:T(2,128)(2,1)} %param.13) | copy-start | bytes 1572868
  58.0 18.8 %copy-start.3 = (bf16[16,16,128]{2,1,0:T(8,128)(2,1)S(1)}, bf16[16,16,128]{2,1,0:T(8,128)(2,1)}, u32[]{:S(2)}) copy-start(bf16[16,16,128]{2,1,0:T(8,128)(2,1)} %q_ref.2) | copy-start | bytes 196612
  58.0 18.8 %copy-start.7 = (s32[16]{0:T(128)S(1)}, s32[16]{0:T(128)}, u32[]{:S(2)}) copy-start(s32[16]{0:T(128)} %length_ref.1) | copy-start | bytes 196
  58.0 9.7 %collective-permute-start.4 = (bf16[51,16,128]{2,1,0:T(8,128)(2,1)S(1)}, bf16[51,16,128]{2,1,0:T(8,128)(2,1)S(1)}, u32[]{:S(2)}, u32[]{:S(2)}) collective-permute-start(bf16[51,16,128]{2,1,0:T(8,128)(2,1)S(1)} %attend.5), channel_id=1, source_target_pairs={{0,24},{8,16},{16,8},{24,0},{1,25},{9,17},{17,9},{25,1},{2,26},{10... | collective-permute-start | bytes 626696 | tf_op jit(solution)/shard_map/ppermute | solution.py:238
  65.2 45.8 %copy-start = (bf16[2048,640]{1,0:T(8,128)(2,1)S(1)}, bf16[2048,640]{1,0:T(8,128)(2,1)}, u32[]{:S(2)}) copy-start(bf16[2048,640]{1,0:T(8,128)(2,1)} %w_ref.1) | copy-start | bytes 7864324
  69.0 20.4 %all-to-all-start.1 = ((bf16[16,56,128]{2,1,0:T(8,128)(2,1)}), bf16[16,56,128]{2,1,0:T(8,128)(2,1)S(1)}, u32[]{:S(2)}, u32[]{:S(2)}) async-start(bf16[16,56,128]{2,1,0:T(8,128)(2,1)} %bitcast.5), calls=%async_computation.1 | async-start | bytes 458752 | tf_op jit(solution)/shard_map/all_to_all | solution.py:297
  76.9 1.0 copy-start.2
  82.3 0.7 copy-start.4
  82.9 0.7 copy-start.5
  89.4 0.7 copy-start.10

commit v3 on v2

--- a/solution.py
+++ b/solution.py
@@ -18,7 +18,8 @@
 BF16 = jnp.bfloat16
 
 VMEM = pl.BlockSpec(memory_space=pltpu.VMEM)
-SMEM = pl.BlockSpec(memory_space=pltpu.SMEM)
+HBM = pl.BlockSpec(memory_space=pltpu.HBM)
+TAIL = 16
 
 
 def params(mib):
@@ -39,86 +40,121 @@
     return owner, place
 
 
+def fetch(pairs, sems):
+    copies = [pltpu.make_async_copy(*pair, sems.at[i]) for i, pair in enumerate(pairs)]
+    for copy in copies:
+        copy.start()
+    return copies
+
+
 def dispatch_kernel(
-    row_prefix_ref, owner_ref, q_ref, k_ref, v_ref, out_ref, packed_ref, held, count_ref
+    row_prefix_hbm, owner_hbm, lengths_hbm, q_hbm, k_hbm, v_hbm, out_ref, block_ref,
+    row_prefix_ref, owner_ref, lengths_ref, q_ref, mixed, held, count_ref, sems,
 ):
-    for p in range(owner_ref.shape[0]):
+    copies = fetch(
+        (
+            (row_prefix_hbm, row_prefix_ref),
+            (owner_hbm, owner_ref),
+            (lengths_hbm, lengths_ref),
+            (q_hbm, q_ref),
+            (k_hbm, mixed.at[0]),
+            (v_hbm, mixed.at[1]),
+        ),
+        sems,
+    )
+    pools = owner_ref.shape[0]
+    length = mixed.shape[1] // 2
+    for p in range(pools):
         count_ref[p] = 0
     out_ref[...] = jnp.zeros_like(out_ref)
+    for copy in copies[:4]:
+        copy.wait()
     for r in range(q_ref.shape[0]):
         owner, place = slot_of(r, row_prefix_ref, owner_ref, count_ref)
         out_ref[owner * CAP + place] = q_ref[r]
-    length = packed_ref.shape[1]
-    for n, source in enumerate((k_ref, v_ref)):
-        held[n] = source[...].astype(F32)
+    pool = lax.axis_index("pool")
+    seen = -(lax.axis_index("y") * 2 + lax.axis_index("core")) * length
+    for p in range(pools):
+        seen += jnp.where(owner_ref[p] == pool, lengths_ref[p], 0)
+    tail = (TAIL, HD)
+    token = lax.broadcasted_iota(jnp.int32, tail, 0) * HD + lax.broadcasted_iota(jnp.int32, tail, 1)
+    block_ref[pl.ds(4 * length, TAIL), :] = jnp.where(token < seen, 0.0, LOWEST).astype(BF16)
+    for n in range(2):
+        copies[4 + n].wait()
+        held[n] = mixed[n].astype(F32)
         for g in range(2):
-            packed_ref[2 * n + g] = held[n, pl.ds(g, length, stride=2), :].astype(BF16)
-
-
-def attend_kernel(sources, owner_ref, lengths_ref, q_ref, *refs):
+            block_ref[pl.ds((2 * n + g) * length, length), :] = held[
+                n, pl.ds(g, length, stride=2), :
+            ].astype(BF16)
+
+
+def attend_kernel(q_ref, *refs):
     blocks, out_ref = refs[:-1], refs[-1]
     slots = q_ref.shape[0]
     step_slots = math.gcd(24, slots)
-    span = blocks[0].shape[1]
-    pool = lax.axis_index("pool")
-    core = lax.axis_index("core")
-    across = lax.axis_index("y")
-    own_length = jnp.int32(0)
-    for p in range(owner_ref.shape[0]):
-        own_length += jnp.where(owner_ref[p] == pool, lengths_ref[p], 0)
-    column = lax.broadcasted_iota(jnp.int32, (1, span), 1)
-    biases = []
-    for dy, dc in sources:
-        at = (across + dy * (1 - 2 * (across & 1))) * 2 + core + dc * (1 - 2 * core)
-        biases.append(jnp.where(column + at * span < own_length, 0.0, LOWEST).astype(F32))
-    ones = jnp.ones((span, HD), BF16)
+    length = (blocks[0].shape[0] - TAIL) // 4
+    width = min(512, length)
+    units = [(start, g) for start in range(0, slots, step_slots) for g in range(2)]
+    pieces = [(block, at) for block in blocks for at in range(0, length, width)]
     lane = lax.broadcasted_iota(jnp.int32, (GROUP, 128), 1)
-
-    def step(j, packed):
-        start = j * step_slots
-        q_all = q_ref[pl.ds(start, step_slots)].astype(F32)
-        outs = []
-        filled = []
-        for g in range(2):
-            q = q_all[:, g * GROUP : (g + 1) * GROUP, :].reshape(step_slots * GROUP, HD)
-            q = q.astype(BF16)
-            scores = [
-                lax.dot_general(
-                    q, block[g], (((1,), (1,)), ((), ())), preferred_element_type=F32
-                )
-                + bias
-                for block, bias in zip(blocks, biases)
-            ]
-            peak = functools.reduce(
-                jnp.maximum, [jnp.max(part, axis=1, keepdims=True) for part in scores]
+    ones = jnp.ones((width, HD), BF16)
+    tails = [block[pl.ds(4 * length, TAIL), :].astype(F32) for block in blocks]
+    biases = [
+        jnp.concatenate(
+            [tail[row : row + 1] for row in range(at // HD, (at + width) // HD)], axis=1
+        )
+        for tail in tails
+        for at in range(0, length, width)
+    ]
+
+    def query(unit):
+        start, g = unit
+        held = q_ref[pl.ds(start, step_slots)].astype(F32)[:, g * GROUP : (g + 1) * GROUP, :]
+        return held.reshape(step_slots * GROUP, HD).astype(BF16)
+
+    def score(q, g, n):
+        block, at = pieces[n]
+        keys = block[pl.ds(g * length + at, width), :]
+        return (
+            lax.dot_general(q, keys, (((1,), (1,)), ((), ())), preferred_element_type=F32)
+            + biases[n]
+        )
+
+    packed = [jnp.zeros((GROUP, 128), F32)] * 2
+    kept = {}
+    q = query(units[0])
+    scores = [score(q, units[0][1], n) for n in range(len(pieces))]
+    for i, (start, g) in enumerate(units):
+        peak = functools.reduce(
+            jnp.maximum, [jnp.max(part, axis=1, keepdims=True) for part in scores]
+        )
+        peak = jnp.maximum(peak, 0.1 * LOWEST)
+        coming = []
+        both = None
+        if i + 1 < len(units):
+            q = query(units[i + 1])
+        for n, (block, at) in enumerate(pieces):
+            weights = jnp.exp2((scores[n] - peak) * (SCALE * LOG2E)).astype(BF16)
+            if i + 1 < len(units):
+                coming.append(score(q, units[i + 1][1], n))
+            values = jnp.concatenate(
+                [block[pl.ds((2 + g) * length + at, width), :], ones], axis=1
             )
-            peak = jnp.maximum(peak, 0.1 * LOWEST)
-            both = functools.reduce(
-                jnp.add,
-                [
-                    jnp.dot(
-                        jnp.exp2((part - peak) * (SCALE * LOG2E)).astype(BF16),
-                        jnp.concatenate([block[2 + g], ones], axis=1),
-                        preferred_element_type=F32,
-                    )
-                    for part, block in zip(scores, blocks)
-                ],
-            )
-            total = both[:, HD:]
-            live = total > 0
-            safe = jnp.where(live, total, 1.0)
-            outs.append((both[:, :HD] / safe).reshape(step_slots, GROUP, HD))
-            lse = jnp.where(live, peak * SCALE + jnp.log(safe), LOWEST)
-            lse = lse.reshape(step_slots, GROUP, HD)
-            kept = packed[g]
-            for i in range(step_slots):
-                kept = jnp.where(lane == start + i, lse[i], kept)
-            filled.append(kept)
-        out_ref[pl.ds(start, step_slots)] = jnp.concatenate(outs, axis=1).astype(BF16)
-        return tuple(filled)
-
-    empty = jnp.zeros((GROUP, 128), F32)
-    packed = lax.fori_loop(0, slots // step_slots, step, (empty, empty))
+            term = jnp.dot(weights, values, preferred_element_type=F32)
+            both = term if both is None else both + term
+        scores = coming
+        total = both[:, HD:]
+        live = total > 0
+        safe = jnp.where(live, total, 1.0)
+        kept[g] = (both[:, :HD] / safe).reshape(step_slots, GROUP, HD)
+        lse = jnp.where(live, peak * SCALE + jnp.log(safe), LOWEST)
+        lse = lse.reshape(step_slots, GROUP, HD)
+        for s in range(step_slots):
+            packed[g] = jnp.where(lane == start + s, lse[s], packed[g])
+        if g == 1:
+            out_ref[pl.ds(start, step_slots)] = jnp.concatenate(
+                [kept[0], kept[1]], axis=1
+            ).astype(BF16)
     for i, plane in enumerate(split3(jnp.concatenate(packed, axis=0))):
         out_ref[slots + i] = plane.astype(BF16)
 
@@ -159,7 +195,8 @@
         out_ref[pl.ds(pair * height, 2 * height), :] = jnp.concatenate(rows, axis=0).astype(BF16)
 
 
-def suffix_kernel(length_ref, q_ref, k_ref, v_ref, out_ref, lse_ref):
+def suffix_kernel(length_hbm, q_ref, k_ref, v_ref, out_ref, lse_ref, length_ref, sems):
+    fetch(((length_hbm, length_ref),), sems)[0].wait()
     span = k_ref.shape[1]
     column = lax.broadcasted_iota(jnp.int32, (2 * GROUP, span), 1)
     head = lax.broadcasted_iota(jnp.int32, (2 * GROUP, span), 0)
@@ -179,13 +216,25 @@
 
 
 def combine_kernel(
-    row_prefix_ref, owner_ref, got_ref, suffix_ref, suffix_lse_ref, out_ref, wide, mixed, count_ref
+    row_prefix_hbm, owner_hbm, got_ref, suffix_hbm, suffix_lse_hbm, out_ref,
+    row_prefix_ref, owner_ref, suffix_ref, suffix_lse_ref, wide, mixed, count_ref, sems,
 ):
+    copies = fetch(
+        (
+            (row_prefix_hbm, row_prefix_ref),
+            (owner_hbm, owner_ref),
+            (suffix_hbm, suffix_ref),
+            (suffix_lse_hbm, suffix_lse_ref),
+        ),
+        sems,
+    )
     rows = suffix_ref.shape[0]
     height = CAP * 16 + GROUP
     for p in range(owner_ref.shape[0]):
         count_ref[p] = 0
     wide[...] = got_ref[...].astype(F32)
+    for copy in copies:
+        copy.wait()
     lane = lax.broadcasted_iota(jnp.int32, (GROUP, 128), 1)
     for r in range(rows):
         owner, place = slot_of(r, row_prefix_ref, owner_ref, count_ref)
@@ -208,10 +257,18 @@
             out_ref[n, :, h * HD : (h + 1) * HD] = piece
 
 
-def project_kernel(attended_ref, w_ref, out_ref):
-    out_ref[...] = jnp.dot(
-        attended_ref[...], w_ref[...], preferred_element_type=F32
-    ).astype(BF16)
+def project_kernel(own_ref, other_ref, w_ref, out_ref):
+    count, rows, depth = own_ref.shape
+    core = lax.axis_index("core")
+    both = jnp.concatenate(
+        [own_ref[...].reshape(count * rows, depth), other_ref[...].reshape(count * rows, depth)],
+        axis=0,
+    )
+    terms = jnp.dot(both, w_ref[...], preferred_element_type=F32).astype(BF16)
+    terms = terms.reshape(2, count, rows, -1)
+    for n in range(count):
+        out_ref[n, core] = terms[0, n]
+        out_ref[n, 1 - core] = terms[1, n]
 
 
 def body(
@@ -234,42 +291,54 @@
     columns = out_weight.shape[1]
     shape = jax.ShapeDtypeStruct
 
-    def meet(value, axis, partner):
-        return lax.ppermute(value, axis, list(enumerate(partner)))
+    def meet(value, axis, apart):
+        pairs = [(i, i ^ apart) for i in range(lax.axis_size(axis))]
+        return lax.ppermute(value, axis, pairs)
+
+    def ints(count):
+        return pltpu.SMEM((count,), jnp.int32)
 
     length = prefix_keys.shape[1]
     outgoing, own = pl.pallas_call(
         dispatch_kernel,
-        out_shape=[shape((slots, heads, hdim), BF16), shape((4, length, hdim), BF16)],
-        in_specs=[SMEM, SMEM, VMEM, VMEM, VMEM],
+        out_shape=[shape((slots, heads, hdim), BF16), shape((4 * length + TAIL, hdim), BF16)],
+        in_specs=[HBM] * 6,
         out_specs=[VMEM] * 2,
-        scratch_shapes=[pltpu.VMEM((2, 2 * length, hdim), F32), pltpu.SMEM((pools,), jnp.int32)],
+        scratch_shapes=[
+            ints(rows),
+            ints(pools),
+            ints(pools),
+            pltpu.VMEM((rows, heads, hdim), BF16),
+            pltpu.VMEM((2, 2 * length, hdim), BF16),
+            pltpu.VMEM((2, 2 * length, hdim), F32),
+            ints(pools),
+            pltpu.SemaphoreType.DMA((6,)),
+        ],
         compiler_params=params(60),
         cost_estimate=pl.CostEstimate(flops=0, bytes_accessed=3_000_000, transcendentals=0),
         name="dispatch",
-    )(row_prefix, owner_map, queries, prefix_keys.reshape(-1, hdim), prefix_values.reshape(-1, hdim))
+    )(
+        row_prefix,
+        owner_map,
+        prefix_lengths,
+        queries,
+        prefix_keys.reshape(-1, hdim),
+        prefix_values.reshape(-1, hdim),
+    )
 
     arrived = lax.all_to_all(
         outgoing.reshape(pools, CAP, heads, hdim), "pool", split_axis=0, concat_axis=0, tiled=True
     ).reshape(slots, heads, hdim)
-    mirror = [ring - 1 - i for i in range(ring)]
-    asked = meet(arrived, "y", mirror)
-
-    pair = meet(own, "y", [i ^ 1 for i in range(ring)])
-    pair, arrived_later = lax.optimization_barrier((pair, arrived))
-    blocks = {
-        (0, 0): own,
-        (0, 1): meet(own, "core", [1, 0]),
-        (1, 0): pair,
-        (1, 1): meet(pair, "core", [1, 0]),
-    }
+    asked = meet(arrived, "y", 3)
+
+    blocks = {(0, 0): own, (0, 1): meet(own, "core", 1), (1, 0): meet(own, "y", 1)}
 
     def attend(q, *sources):
         span = len(sources) * length
         return pl.pallas_call(
-            functools.partial(attend_kernel, sources),
+            attend_kernel,
             out_shape=shape((slots + 3, heads, hdim), BF16),
-            in_specs=[SMEM, SMEM, VMEM] + [VMEM] * len(sources),
+            in_specs=[VMEM] * (1 + len(sources)),
             out_specs=VMEM,
             compiler_params=params(30),
             cost_estimate=pl.CostEstimate(
@@ -278,12 +347,15 @@
                 transcendentals=slots * heads * span,
             ),
             name="attend",
-        )(owner_map, prefix_lengths, q, *(blocks[source] for source in sources))
+        )(q, *(blocks[source] for source in sources))
 
     near, far = ((0, 0), (0, 1)), ((1, 0), (1, 1))
-    near_part, asked = lax.optimization_barrier((attend(arrived, *near), asked))
-    answer = meet(attend(asked, *near, *far), "y", mirror)
-    far_part = attend(arrived_later, *far)
+    near_part, blocks[1, 0] = lax.optimization_barrier(
+        (attend(arrived, *near), blocks[1, 0])
+    )
+    blocks[1, 1] = meet(blocks[1, 0], "core", 1)
+    answer = meet(attend(asked, *near, *far), "y", 3)
+    far_part = attend(arrived, *far)
     merged = pl.pallas_call(
         merge_kernel,
         out_shape=shape((pools * (CAP * heads + GROUP), hdim), BF16),
@@ -305,8 +377,9 @@
     suffix_out, suffix_lse = pl.pallas_call(
         suffix_kernel,
         out_shape=[shape((rows, heads, hdim), F32)] * 2,
-        in_specs=[SMEM, VMEM, VMEM, VMEM],
+        in_specs=[HBM, VMEM, VMEM, VMEM],
         out_specs=[VMEM] * 2,
+        scratch_shapes=[ints(rows), pltpu.SemaphoreType.DMA((1,))],
         compiler_params=params(8),
         cost_estimate=pl.CostEstimate(
             flops=4 * rows * heads * 128 * 128, bytes_accessed=2_000_000, transcendentals=0
@@ -321,23 +394,28 @@
 
     attended = pl.pallas_call(
         combine_kernel,
-        out_shape=shape((2 * ring, rows, heads * hdim), BF16),
-        in_specs=[SMEM, SMEM, VMEM, VMEM, VMEM],
+        out_shape=shape((ring, rows, heads * hdim), BF16),
+        in_specs=[HBM, HBM, VMEM, HBM, HBM],
         out_specs=VMEM,
         scratch_shapes=[
+            ints(rows),
+            ints(pools),
+            pltpu.VMEM((rows, heads, hdim), F32),
+            pltpu.VMEM((rows, heads, hdim), F32),
             pltpu.VMEM((pools * (CAP * heads + GROUP), hdim), F32),
             pltpu.VMEM((rows * heads, hdim), F32),
-            pltpu.SMEM((pools,), jnp.int32),
+            ints(pools),
+            pltpu.SemaphoreType.DMA((4,)),
         ],
-        compiler_params=params(60),
+        compiler_params=params(8),
         cost_estimate=pl.CostEstimate(flops=0, bytes_accessed=1_000_000, transcendentals=0),
         name="combine",
     )(row_prefix, owner_map, returned, suffix_out, suffix_lse)
-    gathered = lax.all_to_all(attended, ("y", "core"), split_axis=0, concat_axis=0, tiled=True)
+    gathered = lax.all_to_all(attended, "y", split_axis=0, concat_axis=0, tiled=True)
     terms = pl.pallas_call(
         project_kernel,
-        out_shape=shape((2 * ring * rows, columns), BF16),
-        in_specs=[VMEM] * 2,
+        out_shape=shape((ring, 2, rows, columns), BF16),
+        in_specs=[VMEM] * 3,
         out_specs=VMEM,
         compiler_params=params(16),
         cost_estimate=pl.CostEstimate(
@@ -346,9 +424,13 @@
             transcendentals=0,
         ),
         name="project",
-    )(gathered.reshape(-1, heads * hdim), out_weight)
+    )(gathered, meet(gathered, "core", 1), out_weight)
     shared = lax.all_to_all(
-        terms.reshape(lax.axis_size("head"), -1, columns), "head", split_axis=0, concat_axis=0, tiled=True
+        terms.reshape(lax.axis_size("head"), -1, columns),
+        "head",
+        split_axis=0,
+        concat_axis=0,
+        tiled=True,
     )
     return jnp.sum(shared.astype(F32), axis=0).astype(BF16)
 

time: 122 us -> 121 us (level)
  blocking collectives: 27.4 us -> 41.1 us
  Pallas kernels: 25.6 us -> 18.3 us
  starting transfers between devices: 44 us -> 39 us
  waiting for transfers between devices: 17.6 us -> 15.7 us
    all_to_all x1 -> x0, starting transfers between devices: 14.9 us -> none  [body(): lax.all_to_all(outgoing.reshape(pools, CAP, heads, hdim), 'pool', split_a...]
    all_to_all x1 -> x2, blocking collectives: 18.6 us -> 32.3 us  [the longest x1 23.8 us: body(): lax.all_to_all(outgoing.reshape(pools, CAP, heads, hdim), 'pool', split_a...]
    ppermute x5 -> x6, starting transfers between devices: 21.3 us -> 33 us  [meet(): return lax.ppermute(value, axis, pairs)]
    all_to_all x1 -> x0, waiting for transfers between devices: 9.22 us -> none  [body(): lax.all_to_all(outgoing.reshape(pools, CAP, heads, hdim), 'pool', split_a...]
    ppermute x5 -> x6, waiting for transfers between devices: 2.56 us -> 9.93 us  [meet(): return lax.ppermute(value, axis, pairs)]
    pallas_call x5, Pallas kernels: 17.4 us -> 10.2 us  [the longest x3 8.77 us: attend(): pl.pallas_call(attend_kernel, out_shape=shape((slots + 3, heads, hdim), B...]
    all_to_all x1, starting transfers between devices: 7.84 us -> 6.03 us  [body(): lax.all_to_all(merged.reshape(pools, CAP * heads + GROUP, hdim), 'pool',...]
    unnamed x22 -> x24, local copies, waits for them, and re-layouts: 5.58 us -> 5.4 us
  transfers between devices with their start and end apart: 7 -> 7, of which waited for: 3 -> 4; matrix products, arithmetic and copies ran while one was open for 0% -> 0% of each run, Pallas kernels for 10% -> 7%
where the time goes in v3:
time: 121 us; the launch traced here: 120 us
  blocking collectives  41.1 us (34%)
  starting transfers between devices  39 us (32%)
  Pallas kernels  18.3 us (15%)
  waiting for transfers between devices  15.7 us (13%)
  local copies, waits for them, and re-layouts  5.4 us (4%)
    ppermute x6, starting transfers between devices, meet(): return lax.ppermute(value, axis, pairs)  33 us
    all_to_all x1, blocking collectives, body(): lax.all_to_all(outgoing.reshape(pools, CAP, heads, hdim), 'pool', split_a...  23.8 us
    ppermute x6, waiting for transfers between devices, meet(): return lax.ppermute(value, axis, pairs)  9.93 us
    all_to_all x1, blocking collectives, body(): lax.all_to_all(terms.reshape(lax.axis_size('head'), -1, columns), 'head',...  8.81 us
    pallas_call x3, Pallas kernels, attend(): pl.pallas_call(attend_kernel, out_shape=shape((slots + 3, heads, hdim), B...  8.77 us
    all_to_all x1, blocking collectives, body(): lax.all_to_all(attended, 'y', split_axis=0, concat_axis=0, tiled=True)  8.49 us
    all_to_all x1, starting transfers between devices, body(): lax.all_to_all(merged.reshape(pools, CAP * heads + GROUP, hdim), 'pool',...  6.03 us
    all_to_all x1, waiting for transfers between devices, body(): lax.all_to_all(merged.reshape(pools, CAP * heads + GROUP, hdim), 'pool',...  5.81 us
  transfers between devices with their start and end apart: 7, of which 4 were waited for; matrix products, arithmetic and copies ran while one was open for 0% of the time, Pallas kernels for 7%

profile of v3, /device:TPU:1, one launch (start us, length us, event | category | flops | bytes accessed | tf_op | source)
XLA Modules:
  0.0 120.4 jit_solution(16973844961546136771)
XLA Ops:
  0.0 2.4 %dispatch.1 = (bf16[48,16,128]{2,1,0:T(8,128)(2,1)}, bf16[4112,128]{1,0:T(8,128)(2,1)}) custom-call(s32[16]{0:T(128)} %bitcast.17, s32[16]{0:T(128)} %owner_hbm.3, s32[16]{0:T(128)} %lengths_hbm.1, bf16[16,16,128]{2,1,0:T(8,128)(2,1)} %q_ref, bf16[2048,128]{1,0:T(8,128)(2,1)} %bitcast.19, bf16[2048,128]{1,0:T(8,128)(2,1)} %bitcast.20), custom_call_target="tpu_custom_call" | custom-call | bytes 3000000 | tf_op jit(solution)/shard_map/dispatch/pallas_call | solution.py:302
  2.4 8.8 %collective-permute-start = (bf16[4112,128]{1,0:T(8,128)(2,1)}, bf16[4112,128]{1,0:T(8,128)(2,1)S(1)}, u32[]{:S(2)}, u32[]{:S(2)}) collective-permute-start(bf16[4112,128]{1,0:T(8,128)(2,1)} %get-tuple-element.14.refs_0_), channel_id=1, source_target_pairs={{0,4},{4,0},{1,5},{5,1},{2,6},{6,2},{3,7},{7,3},{8,12},{12,8},{9,1... | collective-permute-start | bytes 3158024 | tf_op jit(solution)/shard_map/ppermute | solution.py:296
  11.2 1.9 %collective-permute-start.1 = (bf16[4112,128]{1,0:T(8,128)(2,1)}, bf16[4112,128]{1,0:T(8,128)(2,1)S(1)}, u32[]{:S(2)}, u32[]{:S(2)}) collective-permute-start(bf16[4112,128]{1,0:T(8,128)(2,1)} %get-tuple-element.14.refs_0_), channel_id=1, source_target_pairs={{0,8},{8,0},{16,24},{24,16},{1,9},{9,1},{17,25},{25,17},{2,10},{10... | collective-permute-start | bytes 3158024 | tf_op jit(solution)/shard_map/ppermute | solution.py:296
  13.1 23.8 %all_to_all.20 = bf16[16,3,16,128]{3,2,1,0:T(8,128)(2,1)S(1)} all-to-all(bf16[16,3,16,128]{3,2,1,0:T(8,128)(2,1)} %bitcast.21), channel_id=1, replica_groups=mesh['pool'=16,'y'=4,'core'=2,'head'=4] {'pool'}, dimensions={0} | all-to-all | bytes 393216 | tf_op jit(solution)/shard_map/all_to_all | solution.py:329
  37.0 0.0 collective-permute-done.refs_1_
  37.0 0.0 copy-start.11
  37.0 1.2 %copy-done.11 = bf16[4112,128]{1,0:T(8,128)(2,1)S(1)} copy-done((bf16[4112,128]{1,0:T(8,128)(2,1)S(1)}, bf16[4112,128]{1,0:T(8,128)(2,1)}, u32[]{:S(2)}) %copy-start.11) | copy-done | bytes 1052696
  38.2 2.2 %attend.3.a_ref = bf16[51,16,128]{2,1,0:T(8,128)(2,1)S(1)} custom-call(bf16[48,16,128]{2,1,0:T(8,128)(2,1)S(1)} %bitcast.14, bf16[4112,128]{1,0:T(8,128)(2,1)S(1)} %copy-done.11, bf16[4112,128]{1,0:T(8,128)(2,1)S(1)} %collective-permute-done.refs_1_), custom_call_target="tpu_custom_call" | custom-call | flops 1207959552 | bytes 3000000 | tf_op jit(solution)/shard_map/attend/pallas_call | solution.py:338
  40.4 0.0 collective-permute-done.1.refs_0_.refs_2_
  40.4 5.2 %collective-permute-start.2 = (bf16[4112,128]{1,0:T(8,128)(2,1)S(1)}, bf16[4112,128]{1,0:T(8,128)(2,1)S(1)}, u32[]{:S(2)}, u32[]{:S(2)}) collective-permute-start(bf16[4112,128]{1,0:T(8,128)(2,1)S(1)} %collective-permute-done.1.refs_0_.refs_2_), channel_id=1, source_target_pairs={{0,4},{4,0},{1,5},{5,1},{2,6},{6,2},{3,7},{7,3},{8,12},{12,8},{9,1... | collective-permute-start | bytes 3158024 | tf_op jit(solution)/shard_map/ppermute | solution.py:296
  45.5 3.8 %collective-permute-start.3 = (bf16[48,16,128]{2,1,0:T(8,128)(2,1)S(1)}, bf16[48,16,128]{2,1,0:T(8,128)(2,1)S(1)}, u32[]{:S(2)}, u32[]{:S(2)}) collective-permute-start(bf16[48,16,128]{2,1,0:T(8,128)(2,1)S(1)} %bitcast.15), channel_id=1, source_target_pairs={{0,24},{8,16},{16,8},{24,0},{1,25},{9,17},{17,9},{25,1},{2,26},{10... | collective-permute-start | bytes 589832 | tf_op jit(solution)/shard_map/ppermute | solution.py:296
  49.4 5.8 %collective-permute-done.3.q_ref = bf16[48,16,128]{2,1,0:T(8,128)(2,1)S(1)} collective-permute-done((bf16[48,16,128]{2,1,0:T(8,128)(2,1)S(1)}, bf16[48,16,128]{2,1,0:T(8,128)(2,1)S(1)}, u32[]{:S(2)}, u32[]{:S(2)}) %collective-permute-start.3) | collective-permute-done | bytes 196640 | tf_op jit(solution)/shard_map/ppermute | solution.py:296
  55.2 0.0 collective-permute-done.2.refs_1_.refs_3_
  55.2 4.5 %attend.5 = bf16[51,16,128]{2,1,0:T(8,128)(2,1)S(1)} custom-call(bf16[48,16,128]{2,1,0:T(8,128)(2,1)S(1)} %collective-permute-done.3.q_ref, bf16[4112,128]{1,0:T(8,128)(2,1)S(1)} %copy-done.11, bf16[4112,128]{1,0:T(8,128)(2,1)S(1)} %collective-permute-done.refs_1_, bf16[4112,128]{1,0:T(8,128)(2,1)S(1)} %collective-permute-done.1.refs_0_.refs_2_, ...), custom_call_target="tpu_custom_call" | custom-call | flops 2415919104 | bytes 3000000 | tf_op jit(solution)/shard_map/attend/pallas_call | solution.py:338
  59.6 3.8 %collective-permute-start.4 = (bf16[51,16,128]{2,1,0:T(8,128)(2,1)S(1)}, bf16[51,16,128]{2,1,0:T(8,128)(2,1)S(1)}, u32[]{:S(2)}, u32[]{:S(2)}) collective-permute-start(bf16[51,16,128]{2,1,0:T(8,128)(2,1)S(1)} %attend.5), channel_id=1, source_target_pairs={{0,24},{8,16},{16,8},{24,0},{1,25},{9,17},{17,9},{25,1},{2,26},{10... | collective-permute-start | bytes 626696 | tf_op jit(solution)/shard_map/ppermute | solution.py:296
  63.4 2.2 %attend.4.b_ref = bf16[51,16,128]{2,1,0:T(8,128)(2,1)S(1)} custom-call(bf16[48,16,128]{2,1,0:T(8,128)(2,1)S(1)} %bitcast.16, bf16[4112,128]{1,0:T(8,128)(2,1)S(1)} %collective-permute-done.1.refs_0_.refs_2_, bf16[4112,128]{1,0:T(8,128)(2,1)S(1)} %collective-permute-done.2.refs_1_.refs_3_), custom_call_target="tpu_custom_call" | custom-call | flops 1207959552 | bytes 3000000 | tf_op jit(solution)/shard_map/attend/pallas_call | solution.py:338
  65.6 0.0 copy-start.1
  65.6 0.0 copy-start.3
  65.6 0.0 copy-start.10
  65.6 0.0 copy-start.8
  65.6 0.0 copy-start.9
  65.7 3.0 %collective-permute-done.4.c_ref = bf16[51,16,128]{2,1,0:T(8,128)(2,1)S(1)} collective-permute-done((bf16[51,16,128]{2,1,0:T(8,128)(2,1)S(1)}, bf16[51,16,128]{2,1,0:T(8,128)(2,1)S(1)}, u32[]{:S(2)}, u32[]{:S(2)}) %collective-permute-start.4) | collective-permute-done | bytes 208928 | tf_op jit(solution)/shard_map/ppermute | solution.py:296
  68.6 1.3 %merge.1 = bf16[896,128]{1,0:T(8,128)(2,1)} custom-call(bf16[51,16,128]{2,1,0:T(8,128)(2,1)S(1)} %attend.3.a_ref, bf16[51,16,128]{2,1,0:T(8,128)(2,1)S(1)} %attend.4.b_ref, bf16[51,16,128]{2,1,0:T(8,128)(2,1)S(1)} %collective-permute-done.4.c_ref), custom_call_target="tpu_custom_call" | custom-call | bytes 1000000 | tf_op jit(solution)/shard_map/merge/pallas_call | solution.py:359
  69.9 0.0 copy-start
  69.9 6.0 %all-to-all-start.1 = ((bf16[16,56,128]{2,1,0:T(8,128)(2,1)}), bf16[16,56,128]{2,1,0:T(8,128)(2,1)S(1)}, u32[]{:S(2)}, u32[]{:S(2)}) async-start(bf16[16,56,128]{2,1,0:T(8,128)(2,1)} %bitcast.5), calls=%async_computation.1 | async-start | bytes 458752 | tf_op jit(solution)/shard_map/all_to_all | solution.py:369
  75.9 0.0 copy-done.1
  75.9 0.0 copy-done.3
  75.9 0.0 copy-done.10
  76.0 0.0 copy-start.2
  76.0 1.0 copy-done.2
  77.0 4.4 %suffix.1 = (f32[16,16,128]{2,1,0:T(8,128)S(1)}, f32[16,16,128]{2,1,0:T(8,128)S(1)}) custom-call(s32[16]{0:T(128)S(1)} %copy-done.10, bf16[16,16,128]{2,1,0:T(8,128)(2,1)S(1)} %copy-done.3, bf16[16,128,128]{2,1,0:T(8,128)(2,1)S(1)} %bitcast.12, bf16[16,128,128]{2,1,0:T(8,128)(2,1)S(1)} %bitcast.13), custom_call_target="tpu_custom_call" | custom-call | flops 16777216 | bytes 2000000 | tf_op jit(solution)/shard_map/suffix/pallas_call | solution.py:377
  81.4 0.0 copy-start.4
  81.4 0.6 copy-done.4
  82.1 0.0 copy-start.6
  82.1 0.6 copy-done.6
  82.7 5.8 %all-to-all-done.1 = bf16[16,56,128]{2,1,0:T(8,128)(2,1)S(1)} async-done(((bf16[16,56,128]{2,1,0:T(8,128)(2,1)}), bf16[16,56,128]{2,1,0:T(8,128)(2,1)S(1)}, u32[]{:S(2)}, u32[]{:S(2)}) %all-to-all-start.1) | async-done | bytes 229408 | tf_op jit(solution)/shard_map/all_to_all | solution.py:369
  88.5 0.0 copy-done.8
  88.5 0.0 copy-done.9
  88.5 0.0 copy-start.5
  88.5 0.9 copy-done.5
  89.4 0.0 copy-start.7
  89.4 0.9 copy-done.7
  90.3 0.9 combine.1
  91.2 8.5 %all_to_all.21.own_ref = bf16[4,16,2048]{2,1,0:T(8,128)(2,1)S(1)} all-to-all(bf16[4,16,2048]{2,1,0:T(8,128)(2,1)S(1)} %combine.1), channel_id=1, replica_groups=mesh['pool'=16,'y'=4,'core'=2,'head'=4] {'y'}, dimensions={0} | all-to-all | bytes 524288 | tf_op jit(solution)/shard_map/all_to_all | solution.py:414
  99.7 9.5 %collective-permute-start.5 = (bf16[4,16,2048]{2,1,0:T(8,128)(2,1)S(1)}, bf16[4,16,2048]{2,1,0:T(8,128)(2,1)S(1)}, u32[]{:S(2)}, u32[]{:S(2)}) collective-permute-start(bf16[4,16,2048]{2,1,0:T(8,128)(2,1)S(1)} %all_to_all.21.own_ref), channel_id=1, source_target_pairs={{0,4},{4,0},{1,5},{5,1},{2,6},{6,2},{3,7},{7,3},{8,12},{12,8},{9,1... | collective-permute-start | bytes 786440 | tf_op jit(solution)/shard_map/ppermute | solution.py:296
  109.2 1.1 collective-permute-done.5.other_ref
  110.3 0.0 copy-done
  110.3 0.6 project.1
  110.9 8.8 %all_to_all.22 = bf16[4,32,640]{2,1,0:T(8,128)(2,1)S(1)} all-to-all(bf16[4,32,640]{2,1,0:T(8,128)(2,1)S(1)} %bitcast.11), channel_id=1, replica_groups=mesh['pool'=16,'y'=4,'core'=2,'head'=4] {'head'}, dimensions={0} | all-to-all | bytes 327680 | tf_op jit(solution)/shard_map/all_to_all | solution.py:428
  119.8 0.6 reduce_sum.12
Async XLA Ops:
  2.4 34.6 %collective-permute-start = (bf16[4112,128]{1,0:T(8,128)(2,1)}, bf16[4112,128]{1,0:T(8,128)(2,1)S(1)}, u32[]{:S(2)}, u32[]{:S(2)}) collective-permute-start(bf16[4112,128]{1,0:T(8,128)(2,1)} %get-tuple-element.14.refs_0_), channel_id=1, source_target_pairs={{0,4},{4,0},{1,5},{5,1},{2,6},{6,2},{3,7},{7,3},{8,12},{12,8},{9,1... | collective-permute-start | bytes 3158024 | tf_op jit(solution)/shard_map/ppermute | solution.py:296
  11.2 29.2 %collective-permute-start.1 = (bf16[4112,128]{1,0:T(8,128)(2,1)}, bf16[4112,128]{1,0:T(8,128)(2,1)S(1)}, u32[]{:S(2)}, u32[]{:S(2)}) collective-permute-start(bf16[4112,128]{1,0:T(8,128)(2,1)} %get-tuple-element.14.refs_0_), channel_id=1, source_target_pairs={{0,8},{8,0},{16,24},{24,16},{1,9},{9,1},{17,25},{25,17},{2,10},{10... | collective-permute-start | bytes 3158024 | tf_op jit(solution)/shard_map/ppermute | solution.py:296
  37.0 1.2 %copy-start.11 = (bf16[4112,128]{1,0:T(8,128)(2,1)S(1)}, bf16[4112,128]{1,0:T(8,128)(2,1)}, u32[]{:S(2)}) copy-start(bf16[4112,128]{1,0:T(8,128)(2,1)} %get-tuple-element.14.refs_0_) | copy-start | bytes 3158020
  40.4 14.8 %collective-permute-start.2 = (bf16[4112,128]{1,0:T(8,128)(2,1)S(1)}, bf16[4112,128]{1,0:T(8,128)(2,1)S(1)}, u32[]{:S(2)}, u32[]{:S(2)}) collective-permute-start(bf16[4112,128]{1,0:T(8,128)(2,1)S(1)} %collective-permute-done.1.refs_0_.refs_2_), channel_id=1, source_target_pairs={{0,4},{4,0},{1,5},{5,1},{2,6},{6,2},{3,7},{7,3},{8,12},{12,8},{9,1... | collective-permute-start | bytes 3158024 | tf_op jit(solution)/shard_map/ppermute | solution.py:296
  45.5 9.6 %collective-permute-start.3 = (bf16[48,16,128]{2,1,0:T(8,128)(2,1)S(1)}, bf16[48,16,128]{2,1,0:T(8,128)(2,1)S(1)}, u32[]{:S(2)}, u32[]{:S(2)}) collective-permute-start(bf16[48,16,128]{2,1,0:T(8,128)(2,1)S(1)} %bitcast.15), channel_id=1, source_target_pairs={{0,24},{8,16},{16,8},{24,0},{1,25},{9,17},{17,9},{25,1},{2,26},{10... | collective-permute-start | bytes 589832 | tf_op jit(solution)/shard_map/ppermute | solution.py:296
  59.6 9.0 %collective-permute-start.4 = (bf16[51,16,128]{2,1,0:T(8,128)(2,1)S(1)}, bf16[51,16,128]{2,1,0:T(8,128)(2,1)S(1)}, u32[]{:S(2)}, u32[]{:S(2)}) collective-permute-start(bf16[51,16,128]{2,1,0:T(8,128)(2,1)S(1)} %attend.5), channel_id=1, source_target_pairs={{0,24},{8,16},{16,8},{24,0},{1,25},{9,17},{17,9},{25,1},{2,26},{10... | collective-permute-start | bytes 626696 | tf_op jit(solution)/shard_map/ppermute | solution.py:296
  65.6 10.3 %copy-start.1 = (bf16[16,64,2,128]{3,2,1,0:T(2,128)(2,1)S(1)}, bf16[16,64,2,128]{3,2,1,0:T(2,128)(2,1)}, u32[]{:S(2)}) copy-start(bf16[16,64,2,128]{3,2,1,0:T(2,128)(2,1)} %param.13) | copy-start | bytes 1572868
  65.6 10.3 %copy-start.3 = (bf16[16,16,128]{2,1,0:T(8,128)(2,1)S(1)}, bf16[16,16,128]{2,1,0:T(8,128)(2,1)}, u32[]{:S(2)}) copy-start(bf16[16,16,128]{2,1,0:T(8,128)(2,1)} %q_ref) | copy-start | bytes 196612
  65.6 10.3 %copy-start.10 = (s32[16]{0:T(128)S(1)}, s32[16]{0:T(128)}, u32[]{:S(2)}) copy-start(s32[16]{0:T(128)} %length_hbm.1) | copy-start | bytes 196
  65.6 22.9 %copy-start.8 = (s32[16,1]{0,1:T(1,128)S(1)}, s32[16,1]{0,1:T(1,128)}, u32[]{:S(2)}) copy-start(s32[16,1]{0,1:T(1,128)} %param.15) | copy-start | bytes 196
  65.6 22.9 %copy-start.9 = (s32[16]{0:T(128)S(1)}, s32[16]{0:T(128)}, u32[]{:S(2)}) copy-start(s32[16]{0:T(128)} %owner_hbm.3) | copy-start | bytes 196
  69.9 40.5 %copy-start = (bf16[2048,640]{1,0:T(8,128)(2,1)S(1)}, bf16[2048,640]{1,0:T(8,128)(2,1)}, u32[]{:S(2)}) copy-start(bf16[2048,640]{1,0:T(8,128)(2,1)} %w_ref.1) | copy-start | bytes 7864324
  69.9 18.6 %all-to-all-start.1 = ((bf16[16,56,128]{2,1,0:T(8,128)(2,1)}), bf16[16,56,128]{2,1,0:T(8,128)(2,1)S(1)}, u32[]{:S(2)}, u32[]{:S(2)}) async-start(bf16[16,56,128]{2,1,0:T(8,128)(2,1)} %bitcast.5), calls=%async_computation.1 | async-start | bytes 458752 | tf_op jit(solution)/shard_map/all_to_all | solution.py:369
  76.0 1.0 copy-start.2
  81.4 0.7 copy-start.4
  82.1 0.6 copy-start.6
  88.5 0.9 copy-start.5
  89.4 0.9 copy-start.7
  99.7 10.6 %collective-permute-start.5 = (bf16[4,16,2048]{2,1,0:T(8,128)(2,1)S(1)}, bf16[4,16,2048]{2,1,0:T(8,128)(2,1)S(1)}, u32[]{:S(2)}, u32[]{:S(2)}) collective-permute-start(bf16[4,16,2048]{2,1,0:T(8,128)(2,1)S(1)} %all_to_all.21.own_ref), channel_id=1, source_target_pairs={{0,4},{4,0},{1,5},{5,1},{2,6},{6,2},{3,7},{7,3},{8,12},{12,8},{9,1... | collective-permute-start | bytes 786440 | tf_op jit(solution)/shard_map/ppermute | solution.py:296

commit v4 on v3

--- a/solution.py
+++ b/solution.py
@@ -195,7 +195,7 @@
         out_ref[pl.ds(pair * height, 2 * height), :] = jnp.concatenate(rows, axis=0).astype(BF16)
 
 
-def suffix_kernel(length_hbm, q_ref, k_ref, v_ref, out_ref, lse_ref, length_ref, sems):
+def suffix_kernel(length_hbm, q_ref, k_ref, v_ref, out_ref, length_ref, sems):
     fetch(((length_hbm, length_ref),), sems)[0].wait()
     span = k_ref.shape[1]
     column = lax.broadcasted_iota(jnp.int32, (2 * GROUP, span), 1)
@@ -211,20 +211,19 @@
         powers = jnp.exp(scores - peak)
         total = jnp.sum(powers, axis=1, keepdims=True)
         summed = jnp.dot(powers.astype(BF16), v_ref[r], preferred_element_type=F32)
-        out_ref[r] = summed / total
-        lse_ref[r] = jnp.broadcast_to(peak + jnp.log(total), (2 * GROUP, HD))
+        out_ref[r, : 2 * GROUP] = summed / total
+        out_ref[r, 2 * GROUP :] = jnp.broadcast_to(peak + jnp.log(total), (2 * GROUP, HD))
 
 
 def combine_kernel(
-    row_prefix_hbm, owner_hbm, got_ref, suffix_hbm, suffix_lse_hbm, out_ref,
-    row_prefix_ref, owner_ref, suffix_ref, suffix_lse_ref, wide, mixed, count_ref, sems,
+    row_prefix_hbm, owner_hbm, got_ref, suffix_hbm, out_ref,
+    row_prefix_ref, owner_ref, suffix_ref, wide, mixed, count_ref, sems,
 ):
     copies = fetch(
         (
             (row_prefix_hbm, row_prefix_ref),
             (owner_hbm, owner_ref),
             (suffix_hbm, suffix_ref),
-            (suffix_lse_hbm, suffix_lse_ref),
         ),
         sems,
     )
@@ -246,11 +245,11 @@
             chosen = ((lane & 15) == place + g * 8) & (lane < 48)
             lses.append(jnp.sum(jnp.where(chosen, tile, 0.0), axis=1, keepdims=True))
         prefix_lse = jnp.broadcast_to(jnp.concatenate(lses, axis=0), (2 * GROUP, HD))
-        suffix_lse = suffix_lse_ref[r]
+        suffix_lse = suffix_ref[r, 2 * GROUP :]
         highest = jnp.maximum(prefix_lse, suffix_lse)
         a = jnp.exp(prefix_lse - highest)
         b = jnp.exp(suffix_lse - highest)
-        mixed[r * 16 : (r + 1) * 16, :] = (a * prefix + b * suffix_ref[r]) / (a + b)
+        mixed[r * 16 : (r + 1) * 16, :] = (a * prefix + b * suffix_ref[r, : 2 * GROUP]) / (a + b)
     for h in range(2 * GROUP):
         piece = mixed[pl.ds(h, rows, stride=16), :].astype(BF16)
         for n in range(out_ref.shape[0]):
@@ -329,9 +328,10 @@
     arrived = lax.all_to_all(
         outgoing.reshape(pools, CAP, heads, hdim), "pool", split_axis=0, concat_axis=0, tiled=True
     ).reshape(slots, heads, hdim)
-    asked = meet(arrived, "y", 3)
-
-    blocks = {(0, 0): own, (0, 1): meet(own, "core", 1), (1, 0): meet(own, "y", 1)}
+    asked = meet(arrived, "y", 1)
+
+    pair, arrived_later = lax.optimization_barrier((meet(own, "y", 3), arrived))
+    blocks = {(0, 0): own, (0, 1): meet(own, "core", 1), (1, 0): pair, (1, 1): meet(pair, "core", 1)}
 
     def attend(q, *sources):
         span = len(sources) * length
@@ -350,12 +350,9 @@
         )(q, *(blocks[source] for source in sources))
 
     near, far = ((0, 0), (0, 1)), ((1, 0), (1, 1))
-    near_part, blocks[1, 0] = lax.optimization_barrier(
-        (attend(arrived, *near), blocks[1, 0])
-    )
-    blocks[1, 1] = meet(blocks[1, 0], "core", 1)
-    answer = meet(attend(asked, *near, *far), "y", 3)
-    far_part = attend(arrived, *far)
+    near_part, asked = lax.optimization_barrier((attend(arrived, *near), asked))
+    answer = meet(attend(asked, *near, *far), "y", 1)
+    far_part = attend(arrived_later, *far)
     merged = pl.pallas_call(
         merge_kernel,
         out_shape=shape((pools * (CAP * heads + GROUP), hdim), BF16),
@@ -374,11 +371,11 @@
         tiled=True,
     ).reshape(-1, hdim)
 
-    suffix_out, suffix_lse = pl.pallas_call(
+    suffix = pl.pallas_call(
         suffix_kernel,
-        out_shape=[shape((rows, heads, hdim), F32)] * 2,
+        out_shape=shape((rows, 2 * heads, hdim), F32),
         in_specs=[HBM, VMEM, VMEM, VMEM],
-        out_specs=[VMEM] * 2,
+        out_specs=VMEM,
         scratch_shapes=[ints(rows), pltpu.SemaphoreType.DMA((1,))],
         compiler_params=params(8),
         cost_estimate=pl.CostEstimate(
@@ -395,22 +392,21 @@
     attended = pl.pallas_call(
         combine_kernel,
         out_shape=shape((ring, rows, heads * hdim), BF16),
-        in_specs=[HBM, HBM, VMEM, HBM, HBM],
+        in_specs=[HBM, HBM, VMEM, HBM],
         out_specs=VMEM,
         scratch_shapes=[
             ints(rows),
             ints(pools),
-            pltpu.VMEM((rows, heads, hdim), F32),
-            pltpu.VMEM((rows, heads, hdim), F32),
+            pltpu.VMEM((rows, 2 * heads, hdim), F32),
             pltpu.VMEM((pools * (CAP * heads + GROUP), hdim), F32),
             pltpu.VMEM((rows * heads, hdim), F32),
             ints(pools),
-            pltpu.SemaphoreType.DMA((4,)),
+            pltpu.SemaphoreType.DMA((3,)),
         ],
         compiler_params=params(8),
         cost_estimate=pl.CostEstimate(flops=0, bytes_accessed=1_000_000, transcendentals=0),
         name="combine",
-    )(row_prefix, owner_map, returned, suffix_out, suffix_lse)
+    )(row_prefix, owner_map, returned, suffix)
     gathered = lax.all_to_all(attended, "y", split_axis=0, concat_axis=0, tiled=True)
     terms = pl.pallas_call(
         project_kernel,

time: 121 us -> 116 us (0.959)
  blocking collectives: 41.1 us -> 18.2 us
  starting transfers between devices: 39 us -> 50.8 us
  waiting for transfers between devices: 15.7 us -> 23.2 us
  local copies, waits for them, and re-layouts: 5.4 us -> 3.32 us
    all_to_all x1 -> x0, blocking collectives: 23.8 us -> none  [body(): lax.all_to_all(outgoing.reshape(pools, CAP, heads, hdim), 'pool', split_a...]
    all_to_all x0 -> x1, starting transfers between devices: none -> 14.9 us  [body(): lax.all_to_all(outgoing.reshape(pools, CAP, heads, hdim), 'pool', split_a...]
    all_to_all x0 -> x1, waiting for transfers between devices: none -> 9.22 us  [body(): lax.all_to_all(outgoing.reshape(pools, CAP, heads, hdim), 'pool', split_a...]
    ppermute x6, starting transfers between devices: 33 us -> 28.8 us  [meet(): return lax.ppermute(value, axis, pairs)]
    unnamed x24 -> x16, local copies, waits for them, and re-layouts: 5.4 us -> 3.32 us
    ppermute x6, waiting for transfers between devices: 9.93 us -> 7.9 us  [meet(): return lax.ppermute(value, axis, pairs)]
  transfers between devices with their start and end apart: 7 -> 8, of which waited for: 4 -> 5; matrix products, arithmetic and copies ran while one was open for 0% -> 0% of each run, Pallas kernels for 7% -> 8%
where the time goes in v4:
time: 116 us; the launch traced here: 115 us
  starting transfers between devices  50.8 us (44%)
  waiting for transfers between devices  23.2 us (20%)
  Pallas kernels  18.2 us (16%)
  blocking collectives  18.2 us (16%)
  local copies, waits for them, and re-layouts  3.32 us (3%)
    ppermute x6, starting transfers between devices, meet(): return lax.ppermute(value, axis, pairs)  28.8 us
    all_to_all x1, starting transfers between devices, body(): lax.all_to_all(outgoing.reshape(pools, CAP, heads, hdim), 'pool', split_a...  14.9 us
    all_to_all x1, blocking collectives, body(): lax.all_to_all(attended, 'y', split_axis=0, concat_axis=0, tiled=True)  9.43 us
    all_to_all x1, waiting for transfers between devices, body(): lax.all_to_all(outgoing.reshape(pools, CAP, heads, hdim), 'pool', split_a...  9.22 us
    all_to_all x1, blocking collectives, body(): lax.all_to_all(terms.reshape(lax.axis_size('head'), -1, columns), 'head',...  8.82 us
    pallas_call x3, Pallas kernels, attend(): pl.pallas_call(attend_kernel, out_shape=shape((slots + 3, heads, hdim), B...  8.63 us
    ppermute x6, waiting for transfers between devices, meet(): return lax.ppermute(value, axis, pairs)  7.9 us
    all_to_all x1, starting transfers between devices, body(): lax.all_to_all(merged.reshape(pools, CAP * heads + GROUP, hdim), 'pool',...  7.05 us
  transfers between devices with their start and end apart: 8, of which 5 were waited for; matrix products, arithmetic and copies ran while one was open for 0% of the time, Pallas kernels for 8%

profile of v4, /device:TPU:1, one launch (start us, length us, event | category | flops | bytes accessed | tf_op | source)
XLA Modules:
  0.0 114.5 jit_solution(6277063800978724933)
XLA Ops:
  0.0 2.4 %dispatch.1 = (bf16[48,16,128]{2,1,0:T(8,128)(2,1)}, bf16[4112,128]{1,0:T(8,128)(2,1)}) custom-call(s32[16]{0:T(128)} %bitcast.17, s32[16]{0:T(128)} %owner_hbm.3, s32[16]{0:T(128)} %lengths_hbm.1, bf16[16,16,128]{2,1,0:T(8,128)(2,1)} %q_ref, bf16[2048,128]{1,0:T(8,128)(2,1)} %bitcast.19, bf16[2048,128]{1,0:T(8,128)(2,1)} %bitcast.20), custom_call_target="tpu_custom_call" | custom-call | bytes 3000000 | tf_op jit(solution)/shard_map/dispatch/pallas_call | solution.py:301
  2.4 5.5 %collective-permute-start.2 = (bf16[4112,128]{1,0:T(8,128)(2,1)}, bf16[4112,128]{1,0:T(8,128)(2,1)S(1)}, u32[]{:S(2)}, u32[]{:S(2)}) collective-permute-start(bf16[4112,128]{1,0:T(8,128)(2,1)} %get-tuple-element.14.refs_0_), channel_id=1, source_target_pairs={{0,24},{8,16},{16,8},{24,0},{1,25},{9,17},{17,9},{25,1},{2,26},{10... | collective-permute-start | bytes 3158024 | tf_op jit(solution)/shard_map/ppermute | solution.py:295
  7.9 14.9 %all-to-all-start = ((bf16[16,3,16,128]{3,2,1,0:T(8,128)(2,1)}), bf16[16,3,16,128]{3,2,1,0:T(8,128)(2,1)S(1)}, u32[]{:S(2)}, u32[]{:S(2)}) async-start(bf16[16,3,16,128]{3,2,1,0:T(8,128)(2,1)} %bitcast.21), calls=%async_computation | async-start | bytes 393216 | tf_op jit(solution)/shard_map/all_to_all | solution.py:328
  22.8 3.1 %collective-permute-start = (bf16[4112,128]{1,0:T(8,128)(2,1)}, bf16[4112,128]{1,0:T(8,128)(2,1)S(1)}, u32[]{:S(2)}, u32[]{:S(2)}) collective-permute-start(bf16[4112,128]{1,0:T(8,128)(2,1)} %get-tuple-element.14.refs_0_), channel_id=1, source_target_pairs={{0,4},{4,0},{1,5},{5,1},{2,6},{6,2},{3,7},{7,3},{8,12},{12,8},{9,1... | collective-permute-start | bytes 3158024 | tf_op jit(solution)/shard_map/ppermute | solution.py:295
  26.0 9.2 %all-to-all-done = bf16[16,3,16,128]{3,2,1,0:T(8,128)(2,1)S(1)} async-done(((bf16[16,3,16,128]{3,2,1,0:T(8,128)(2,1)}), bf16[16,3,16,128]{3,2,1,0:T(8,128)(2,1)S(1)}, u32[]{:S(2)}, u32[]{:S(2)}) %all-to-all-start) | async-done | bytes 196640 | tf_op jit(solution)/shard_map/all_to_all | solution.py:328
  35.2 0.0 collective-permute-done.2.refs_0_.refs_2_
  35.2 7.0 %collective-permute-start.3 = (bf16[4112,128]{1,0:T(8,128)(2,1)S(1)}, bf16[4112,128]{1,0:T(8,128)(2,1)S(1)}, u32[]{:S(2)}, u32[]{:S(2)}) collective-permute-start(bf16[4112,128]{1,0:T(8,128)(2,1)S(1)} %collective-permute-done.2.refs_0_.refs_2_), channel_id=1, source_target_pairs={{0,4},{4,0},{1,5},{5,1},{2,6},{6,2},{3,7},{7,3},{8,12},{12,8},{9,1... | collective-permute-start | bytes 3158024 | tf_op jit(solution)/shard_map/ppermute | solution.py:295
  42.2 1.9 %collective-permute-start.1 = (bf16[48,16,128]{2,1,0:T(8,128)(2,1)S(1)}, bf16[48,16,128]{2,1,0:T(8,128)(2,1)S(1)}, u32[]{:S(2)}, u32[]{:S(2)}) collective-permute-start(bf16[48,16,128]{2,1,0:T(8,128)(2,1)S(1)} %bitcast.14), channel_id=1, source_target_pairs={{0,8},{8,0},{16,24},{24,16},{1,9},{9,1},{17,25},{25,17},{2,10},{10... | collective-permute-start | bytes 589832 | tf_op jit(solution)/shard_map/ppermute | solution.py:295
  44.1 0.0 collective-permute-done.refs_1_
  44.1 0.0 copy-start.7
  44.1 1.2 %copy-done.7 = bf16[4112,128]{1,0:T(8,128)(2,1)S(1)} copy-done((bf16[4112,128]{1,0:T(8,128)(2,1)S(1)}, bf16[4112,128]{1,0:T(8,128)(2,1)}, u32[]{:S(2)}) %copy-start.7) | copy-done | bytes 1052696
  45.3 2.1 %attend.3.a_ref = bf16[51,16,128]{2,1,0:T(8,128)(2,1)S(1)} custom-call(bf16[48,16,128]{2,1,0:T(8,128)(2,1)S(1)} %bitcast.15, bf16[4112,128]{1,0:T(8,128)(2,1)S(1)} %copy-done.7, bf16[4112,128]{1,0:T(8,128)(2,1)S(1)} %collective-permute-done.refs_1_), custom_call_target="tpu_custom_call" | custom-call | flops 1207959552 | bytes 3000000 | tf_op jit(solution)/shard_map/attend/pallas_call | solution.py:338
  47.5 3.1 %collective-permute-done.1.q_ref = bf16[48,16,128]{2,1,0:T(8,128)(2,1)S(1)} collective-permute-done((bf16[48,16,128]{2,1,0:T(8,128)(2,1)S(1)}, bf16[48,16,128]{2,1,0:T(8,128)(2,1)S(1)}, u32[]{:S(2)}, u32[]{:S(2)}) %collective-permute-start.1) | collective-permute-done | bytes 196640 | tf_op jit(solution)/shard_map/ppermute | solution.py:295
  50.6 0.0 collective-permute-done.3.refs_1_.refs_3_
  50.6 4.4 %attend.5 = bf16[51,16,128]{2,1,0:T(8,128)(2,1)S(1)} custom-call(bf16[48,16,128]{2,1,0:T(8,128)(2,1)S(1)} %collective-permute-done.1.q_ref, bf16[4112,128]{1,0:T(8,128)(2,1)S(1)} %copy-done.7, bf16[4112,128]{1,0:T(8,128)(2,1)S(1)} %collective-permute-done.refs_1_, bf16[4112,128]{1,0:T(8,128)(2,1)S(1)} %collective-permute-done.2.refs_0_.refs_2_, ...), custom_call_target="tpu_custom_call" | custom-call | flops 2415919104 | bytes 3000000 | tf_op jit(solution)/shard_map/attend/pallas_call | solution.py:338
  55.0 2.0 %collective-permute-start.4 = (bf16[51,16,128]{2,1,0:T(8,128)(2,1)S(1)}, bf16[51,16,128]{2,1,0:T(8,128)(2,1)S(1)}, u32[]{:S(2)}, u32[]{:S(2)}) collective-permute-start(bf16[51,16,128]{2,1,0:T(8,128)(2,1)S(1)} %attend.5), channel_id=1, source_target_pairs={{0,8},{8,0},{16,24},{24,16},{1,9},{9,1},{17,25},{25,17},{2,10},{10... | collective-permute-start | bytes 626696 | tf_op jit(solution)/shard_map/ppermute | solution.py:295
  57.0 2.1 %attend.4.b_ref = bf16[51,16,128]{2,1,0:T(8,128)(2,1)S(1)} custom-call(bf16[48,16,128]{2,1,0:T(8,128)(2,1)S(1)} %bitcast.16, bf16[4112,128]{1,0:T(8,128)(2,1)S(1)} %collective-permute-done.2.refs_0_.refs_2_, bf16[4112,128]{1,0:T(8,128)(2,1)S(1)} %collective-permute-done.3.refs_1_.refs_3_), custom_call_target="tpu_custom_call" | custom-call | flops 1207959552 | bytes 3000000 | tf_op jit(solution)/shard_map/attend/pallas_call | solution.py:338
  59.1 0.0 copy-start.3
  59.1 0.0 copy-start.6
  59.1 3.6 %collective-permute-done.4.c_ref = bf16[51,16,128]{2,1,0:T(8,128)(2,1)S(1)} collective-permute-done((bf16[51,16,128]{2,1,0:T(8,128)(2,1)S(1)}, bf16[51,16,128]{2,1,0:T(8,128)(2,1)S(1)}, u32[]{:S(2)}, u32[]{:S(2)}) %collective-permute-start.4) | collective-permute-done | bytes 208928 | tf_op jit(solution)/shard_map/ppermute | solution.py:295
  62.8 1.3 %merge.1 = bf16[896,128]{1,0:T(8,128)(2,1)} custom-call(bf16[51,16,128]{2,1,0:T(8,128)(2,1)S(1)} %attend.3.a_ref, bf16[51,16,128]{2,1,0:T(8,128)(2,1)S(1)} %attend.4.b_ref, bf16[51,16,128]{2,1,0:T(8,128)(2,1)S(1)} %collective-permute-done.4.c_ref), custom_call_target="tpu_custom_call" | custom-call | bytes 1000000 | tf_op jit(solution)/shard_map/merge/pallas_call | solution.py:356
  64.0 0.0 copy-start.4
  64.0 0.0 copy-start.5
  64.0 7.0 %all-to-all-start.1 = ((bf16[16,56,128]{2,1,0:T(8,128)(2,1)}), bf16[16,56,128]{2,1,0:T(8,128)(2,1)S(1)}, u32[]{:S(2)}, u32[]{:S(2)}) async-start(bf16[16,56,128]{2,1,0:T(8,128)(2,1)} %bitcast.5), calls=%async_computation.1 | async-start | bytes 458752 | tf_op jit(solution)/shard_map/all_to_all | solution.py:366
  71.1 0.0 copy-done.3
  71.1 0.0 copy-done.6
  71.1 0.0 copy-start.1
  71.1 1.0 copy-done.1
  72.2 0.0 copy-start.2
  72.2 1.0 copy-done.2
  73.2 0.0 copy-start
  73.2 4.4 %suffix.1.suffix_hbm = f32[16,32,128]{2,1,0:T(8,128)S(1)} custom-call(s32[16]{0:T(128)S(1)} %copy-done.6, bf16[16,16,128]{2,1,0:T(8,128)(2,1)S(1)} %copy-done.3, bf16[16,128,128]{2,1,0:T(8,128)(2,1)S(1)} %bitcast.12, bf16[16,128,128]{2,1,0:T(8,128)(2,1)S(1)} %bitcast.13), custom_call_target="tpu_custom_call" | custom-call | flops 16777216 | bytes 2000000 | tf_op jit(solution)/shard_map/suffix/pallas_call | solution.py:374
  77.6 6.1 %all-to-all-done.1 = bf16[16,56,128]{2,1,0:T(8,128)(2,1)S(1)} async-done(((bf16[16,56,128]{2,1,0:T(8,128)(2,1)}), bf16[16,56,128]{2,1,0:T(8,128)(2,1)S(1)}, u32[]{:S(2)}, u32[]{:S(2)}) %all-to-all-start.1) | async-done | bytes 229408 | tf_op jit(solution)/shard_map/all_to_all | solution.py:366
  83.7 0.0 copy-done.4
  83.7 0.0 copy-done.5
  83.7 0.9 combine.1
  84.6 9.4 %all_to_all.20.own_ref = bf16[4,16,2048]{2,1,0:T(8,128)(2,1)S(1)} all-to-all(bf16[4,16,2048]{2,1,0:T(8,128)(2,1)S(1)} %combine.1), channel_id=1, replica_groups=mesh['pool'=16,'y'=4,'core'=2,'head'=4] {'y'}, dimensions={0} | all-to-all | bytes 524288 | tf_op jit(solution)/shard_map/all_to_all | solution.py:410
  94.0 9.3 %collective-permute-start.5 = (bf16[4,16,2048]{2,1,0:T(8,128)(2,1)S(1)}, bf16[4,16,2048]{2,1,0:T(8,128)(2,1)S(1)}, u32[]{:S(2)}, u32[]{:S(2)}) collective-permute-start(bf16[4,16,2048]{2,1,0:T(8,128)(2,1)S(1)} %all_to_all.20.own_ref), channel_id=1, source_target_pairs={{0,4},{4,0},{1,5},{5,1},{2,6},{6,2},{3,7},{7,3},{8,12},{12,8},{9,1... | collective-permute-start | bytes 786440 | tf_op jit(solution)/shard_map/ppermute | solution.py:295
  103.3 1.1 collective-permute-done.5.other_ref
  104.5 0.0 copy-done
  104.5 0.6 project.1
  105.1 8.8 %all_to_all.21 = bf16[4,32,640]{2,1,0:T(8,128)(2,1)S(1)} all-to-all(bf16[4,32,640]{2,1,0:T(8,128)(2,1)S(1)} %bitcast.11), channel_id=1, replica_groups=mesh['pool'=16,'y'=4,'core'=2,'head'=4] {'head'}, dimensions={0} | all-to-all | bytes 327680 | tf_op jit(solution)/shard_map/all_to_all | solution.py:424
  113.9 0.6 reduce_sum.12
Async XLA Ops:
  2.4 32.8 %collective-permute-start.2 = (bf16[4112,128]{1,0:T(8,128)(2,1)}, bf16[4112,128]{1,0:T(8,128)(2,1)S(1)}, u32[]{:S(2)}, u32[]{:S(2)}) collective-permute-start(bf16[4112,128]{1,0:T(8,128)(2,1)} %get-tuple-element.14.refs_0_), channel_id=1, source_target_pairs={{0,24},{8,16},{16,8},{24,0},{1,25},{9,17},{17,9},{25,1},{2,26},{10... | collective-permute-start | bytes 3158024 | tf_op jit(solution)/shard_map/ppermute | solution.py:295
  7.9 27.3 %all-to-all-start = ((bf16[16,3,16,128]{3,2,1,0:T(8,128)(2,1)}), bf16[16,3,16,128]{3,2,1,0:T(8,128)(2,1)S(1)}, u32[]{:S(2)}, u32[]{:S(2)}) async-start(bf16[16,3,16,128]{3,2,1,0:T(8,128)(2,1)} %bitcast.21), calls=%async_computation | async-start | bytes 393216 | tf_op jit(solution)/shard_map/all_to_all | solution.py:328
  22.8 21.3 %collective-permute-start = (bf16[4112,128]{1,0:T(8,128)(2,1)}, bf16[4112,128]{1,0:T(8,128)(2,1)S(1)}, u32[]{:S(2)}, u32[]{:S(2)}) collective-permute-start(bf16[4112,128]{1,0:T(8,128)(2,1)} %get-tuple-element.14.refs_0_), channel_id=1, source_target_pairs={{0,4},{4,0},{1,5},{5,1},{2,6},{6,2},{3,7},{7,3},{8,12},{12,8},{9,1... | collective-permute-start | bytes 3158024 | tf_op jit(solution)/shard_map/ppermute | solution.py:295
  35.2 15.4 %collective-permute-start.3 = (bf16[4112,128]{1,0:T(8,128)(2,1)S(1)}, bf16[4112,128]{1,0:T(8,128)(2,1)S(1)}, u32[]{:S(2)}, u32[]{:S(2)}) collective-permute-start(bf16[4112,128]{1,0:T(8,128)(2,1)S(1)} %collective-permute-done.2.refs_0_.refs_2_), channel_id=1, source_target_pairs={{0,4},{4,0},{1,5},{5,1},{2,6},{6,2},{3,7},{7,3},{8,12},{12,8},{9,1... | collective-permute-start | bytes 3158024 | tf_op jit(solution)/shard_map/ppermute | solution.py:295
  42.2 8.4 %collective-permute-start.1 = (bf16[48,16,128]{2,1,0:T(8,128)(2,1)S(1)}, bf16[48,16,128]{2,1,0:T(8,128)(2,1)S(1)}, u32[]{:S(2)}, u32[]{:S(2)}) collective-permute-start(bf16[48,16,128]{2,1,0:T(8,128)(2,1)S(1)} %bitcast.14), channel_id=1, source_target_pairs={{0,8},{8,0},{16,24},{24,16},{1,9},{9,1},{17,25},{25,17},{2,10},{10... | collective-permute-start | bytes 589832 | tf_op jit(solution)/shard_map/ppermute | solution.py:295
  44.1 1.2 %copy-start.7 = (bf16[4112,128]{1,0:T(8,128)(2,1)S(1)}, bf16[4112,128]{1,0:T(8,128)(2,1)}, u32[]{:S(2)}) copy-start(bf16[4112,128]{1,0:T(8,128)(2,1)} %get-tuple-element.14.refs_0_) | copy-start | bytes 3158020
  55.0 7.8 %collective-permute-start.4 = (bf16[51,16,128]{2,1,0:T(8,128)(2,1)S(1)}, bf16[51,16,128]{2,1,0:T(8,128)(2,1)S(1)}, u32[]{:S(2)}, u32[]{:S(2)}) collective-permute-start(bf16[51,16,128]{2,1,0:T(8,128)(2,1)S(1)} %attend.5), channel_id=1, source_target_pairs={{0,8},{8,0},{16,24},{24,16},{1,9},{9,1},{17,25},{25,17},{2,10},{10... | collective-permute-start | bytes 626696 | tf_op jit(solution)/shard_map/ppermute | solution.py:295
  59.1 12.0 %copy-start.3 = (bf16[16,16,128]{2,1,0:T(8,128)(2,1)S(1)}, bf16[16,16,128]{2,1,0:T(8,128)(2,1)}, u32[]{:S(2)}) copy-start(bf16[16,16,128]{2,1,0:T(8,128)(2,1)} %q_ref) | copy-start | bytes 196612
  59.1 12.0 %copy-start.6 = (s32[16]{0:T(128)S(1)}, s32[16]{0:T(128)}, u32[]{:S(2)}) copy-start(s32[16]{0:T(128)} %length_hbm.1) | copy-start | bytes 196
  64.0 19.7 %copy-start.4 = (s32[16,1]{0,1:T(1,128)S(1)}, s32[16,1]{0,1:T(1,128)}, u32[]{:S(2)}) copy-start(s32[16,1]{0,1:T(1,128)} %param.15) | copy-start | bytes 196
  64.0 19.7 %copy-start.5 = (s32[16]{0:T(128)S(1)}, s32[16]{0:T(128)}, u32[]{:S(2)}) copy-start(s32[16]{0:T(128)} %owner_hbm.3) | copy-start | bytes 196
  64.0 19.7 %all-to-all-start.1 = ((bf16[16,56,128]{2,1,0:T(8,128)(2,1)}), bf16[16,56,128]{2,1,0:T(8,128)(2,1)S(1)}, u32[]{:S(2)}, u32[]{:S(2)}) async-start(bf16[16,56,128]{2,1,0:T(8,128)(2,1)} %bitcast.5), calls=%async_computation.1 | async-start | bytes 458752 | tf_op jit(solution)/shard_map/all_to_all | solution.py:366
  71.1 1.0 copy-start.1
  72.2 1.0 copy-start.2
  73.2 31.3 %copy-start = (bf16[2048,640]{1,0:T(8,128)(2,1)S(1)}, bf16[2048,640]{1,0:T(8,128)(2,1)}, u32[]{:S(2)}) copy-start(bf16[2048,640]{1,0:T(8,128)(2,1)} %w_ref.1) | copy-start | bytes 7864324
  94.0 10.5 %collective-permute-start.5 = (bf16[4,16,2048]{2,1,0:T(8,128)(2,1)S(1)}, bf16[4,16,2048]{2,1,0:T(8,128)(2,1)S(1)}, u32[]{:S(2)}, u32[]{:S(2)}) collective-permute-start(bf16[4,16,2048]{2,1,0:T(8,128)(2,1)S(1)} %all_to_all.20.own_ref), channel_id=1, source_target_pairs={{0,4},{4,0},{1,5},{5,1},{2,6},{6,2},{3,7},{7,3},{8,12},{12,8},{9,1... | collective-permute-start | bytes 786440 | tf_op jit(solution)/shard_map/ppermute | solution.py:295

commit v5 on v4

--- a/solution.py
+++ b/solution.py
@@ -251,23 +251,15 @@
         b = jnp.exp(suffix_lse - highest)
         mixed[r * 16 : (r + 1) * 16, :] = (a * prefix + b * suffix_ref[r, : 2 * GROUP]) / (a + b)
     for h in range(2 * GROUP):
-        piece = mixed[pl.ds(h, rows, stride=16), :].astype(BF16)
-        for n in range(out_ref.shape[0]):
-            out_ref[n, :, h * HD : (h + 1) * HD] = piece
-
-
-def project_kernel(own_ref, other_ref, w_ref, out_ref):
-    count, rows, depth = own_ref.shape
+        out_ref[:, h * HD : (h + 1) * HD] = mixed[pl.ds(h, rows, stride=16), :].astype(BF16)
+
+
+def project_kernel(attended_ref, own_ref, other_ref, out_ref):
     core = lax.axis_index("core")
-    both = jnp.concatenate(
-        [own_ref[...].reshape(count * rows, depth), other_ref[...].reshape(count * rows, depth)],
-        axis=0,
-    )
-    terms = jnp.dot(both, w_ref[...], preferred_element_type=F32).astype(BF16)
-    terms = terms.reshape(2, count, rows, -1)
-    for n in range(count):
-        out_ref[n, core] = terms[0, n]
-        out_ref[n, 1 - core] = terms[1, n]
+    for at, w_ref in ((core, own_ref), (1 - core, other_ref)):
+        out_ref[at] = jnp.dot(
+            attended_ref[...], w_ref[...], preferred_element_type=F32
+        ).astype(BF16)
 
 
 def body(
@@ -362,7 +354,8 @@
         cost_estimate=pl.CostEstimate(flops=0, bytes_accessed=1_000_000, transcendentals=0),
         name="merge",
     )(near_part, far_part, answer)
-    merged, queries_later = lax.optimization_barrier((merged, queries))
+    merged, queries_later, weight = lax.optimization_barrier((merged, queries, out_weight))
+    other_weight = meet(weight, "core", 1)
     returned = lax.all_to_all(
         merged.reshape(pools, CAP * heads + GROUP, hdim),
         "pool",
@@ -371,6 +364,7 @@
         tiled=True,
     ).reshape(-1, hdim)
 
+    returned, other_weight = lax.optimization_barrier((returned, other_weight))
     suffix = pl.pallas_call(
         suffix_kernel,
         out_shape=shape((rows, 2 * heads, hdim), F32),
@@ -391,7 +385,7 @@
 
     attended = pl.pallas_call(
         combine_kernel,
-        out_shape=shape((ring, rows, heads * hdim), BF16),
+        out_shape=shape((rows, heads * hdim), BF16),
         in_specs=[HBM, HBM, VMEM, HBM],
         out_specs=VMEM,
         scratch_shapes=[
@@ -407,28 +401,30 @@
         cost_estimate=pl.CostEstimate(flops=0, bytes_accessed=1_000_000, transcendentals=0),
         name="combine",
     )(row_prefix, owner_map, returned, suffix)
-    gathered = lax.all_to_all(attended, "y", split_axis=0, concat_axis=0, tiled=True)
+    gathered = lax.all_gather(attended, "y", axis=0, tiled=True)
     terms = pl.pallas_call(
         project_kernel,
-        out_shape=shape((ring, 2, rows, columns), BF16),
+        out_shape=shape((2, ring * rows, columns), BF16),
         in_specs=[VMEM] * 3,
         out_specs=VMEM,
         compiler_params=params(16),
         cost_estimate=pl.CostEstimate(
             flops=4 * ring * rows * heads * hdim * columns,
-            bytes_accessed=4_000_000,
+            bytes_accessed=6_000_000,
             transcendentals=0,
         ),
         name="project",
-    )(gathered, meet(gathered, "core", 1), out_weight)
+    )(gathered, out_weight, other_weight)
+    groups = lax.axis_size("head")
     shared = lax.all_to_all(
-        terms.reshape(lax.axis_size("head"), -1, columns),
-        "head",
+        terms.reshape(2 * groups, -1, columns),
+        ("core", "head"),
         split_axis=0,
         concat_axis=0,
         tiled=True,
     )
-    return jnp.sum(shared.astype(F32), axis=0).astype(BF16)
+    shared = shared.reshape(2, groups, -1, columns).astype(F32)
+    return jnp.sum(shared, axis=1).astype(BF16).reshape(-1, columns)
 
 
 def solution(mesh):

time: 116 us -> 120 us (1.034)
  blocking collectives: 18.2 us -> 25.9 us
  starting transfers between devices: 50.8 us -> 45.3 us
  Pallas kernels: 18.2 us -> 20.4 us
  local copies, waits for them, and re-layouts: 3.32 us -> 4.55 us
    all_gather x0 -> x1, blocking collectives: none -> 9.57 us  [body(): gathered = lax.all_gather(attended, 'y', axis=0, tiled=True)]
    ppermute x6, starting transfers between devices: 28.8 us -> 23.5 us  [meet(): return lax.ppermute(value, axis, pairs)]
    ppermute x6, waiting for transfers between devices: 7.9 us -> 5.59 us  [meet(): return lax.ppermute(value, axis, pairs)]
    pallas_call x2, Pallas kernels: 1.45 us -> 3.61 us  [the longest x1 2.76 us: body(): pl.pallas_call(project_kernel, out_shape=shape((2, ring * rows, columns),...]
    all_to_all x2 -> x1, blocking collectives: 18.2 us -> 16.3 us  [body(): lax.all_to_all(terms.reshape(2 * groups, -1, columns), ('core', 'head'),...]
    unnamed x16 -> x20, local copies, waits for them, and re-layouts: 3.32 us -> 4.55 us
    all_to_all x1, waiting for transfers between devices: 6.07 us -> 7.3 us  [body(): lax.all_to_all(merged.reshape(pools, CAP * heads + GROUP, hdim), 'pool',...]
  transfers between devices with their start and end apart: 8 -> 8, of which waited for: 5 -> 4; matrix products, arithmetic and copies ran while one was open for 0% -> 0% of each run, Pallas kernels for 8% -> 7%
where the time goes in v5:
time: 120 us; the launch traced here: 119 us
  starting transfers between devices  45.3 us (38%)
  blocking collectives  25.9 us (22%)
  waiting for transfers between devices  22.1 us (18%)
  Pallas kernels  20.4 us (17%)
  local copies, waits for them, and re-layouts  4.55 us (4%)
    ppermute x6, starting transfers between devices, meet(): return lax.ppermute(value, axis, pairs)  23.5 us
    all_to_all x1, blocking collectives, body(): lax.all_to_all(terms.reshape(2 * groups, -1, columns), ('core', 'head'),...  16.3 us
    all_to_all x1, starting transfers between devices, body(): lax.all_to_all(outgoing.reshape(pools, CAP, heads, hdim), 'pool', split_a...  14.9 us
    all_gather x1, blocking collectives, body(): gathered = lax.all_gather(attended, 'y', axis=0, tiled=True)  9.57 us
    all_to_all x1, waiting for transfers between devices, body(): lax.all_to_all(outgoing.reshape(pools, CAP, heads, hdim), 'pool', split_a...  9.22 us
    pallas_call x3, Pallas kernels, attend(): pl.pallas_call(attend_kernel, out_shape=shape((slots + 3, heads, hdim), B...  8.65 us
    all_to_all x1, waiting for transfers between devices, body(): lax.all_to_all(merged.reshape(pools, CAP * heads + GROUP, hdim), 'pool',...  7.3 us
    all_to_all x1, starting transfers between devices, body(): lax.all_to_all(merged.reshape(pools, CAP * heads + GROUP, hdim), 'pool',...  6.93 us
  transfers between devices with their start and end apart: 8, of which 4 were waited for; matrix products, arithmetic and copies ran while one was open for 0% of the time, Pallas kernels for 7%

profile of v5, /device:TPU:1, one launch (start us, length us, event | category | flops | bytes accessed | tf_op | source)
XLA Modules:
  0.0 119.1 jit_solution(17359156436956280237)
XLA Ops:
  0.0 2.4 %dispatch.1 = (bf16[48,16,128]{2,1,0:T(8,128)(2,1)}, bf16[4112,128]{1,0:T(8,128)(2,1)}) custom-call(s32[16]{0:T(128)} %bitcast.20, s32[16]{0:T(128)} %owner_hbm.3, s32[16]{0:T(128)} %lengths_hbm.1, bf16[16,16,128]{2,1,0:T(8,128)(2,1)} %q_ref, bf16[2048,128]{1,0:T(8,128)(2,1)} %bitcast.22, bf16[2048,128]{1,0:T(8,128)(2,1)} %bitcast.23), custom_call_target="tpu_custom_call" | custom-call | bytes 3000000 | tf_op jit(solution)/shard_map/dispatch/pallas_call | solution.py:293
  2.4 5.5 %collective-permute-start.2 = (bf16[4112,128]{1,0:T(8,128)(2,1)}, bf16[4112,128]{1,0:T(8,128)(2,1)S(1)}, u32[]{:S(2)}, u32[]{:S(2)}) collective-permute-start(bf16[4112,128]{1,0:T(8,128)(2,1)} %get-tuple-element.17.refs_0_), channel_id=1, source_target_pairs={{0,24},{8,16},{16,8},{24,0},{1,25},{9,17},{17,9},{25,1},{2,26},{10... | collective-permute-start | bytes 3158024 | tf_op jit(solution)/shard_map/ppermute | solution.py:287
  7.9 14.9 %all-to-all-start = ((bf16[16,3,16,128]{3,2,1,0:T(8,128)(2,1)}), bf16[16,3,16,128]{3,2,1,0:T(8,128)(2,1)S(1)}, u32[]{:S(2)}, u32[]{:S(2)}) async-start(bf16[16,3,16,128]{3,2,1,0:T(8,128)(2,1)} %bitcast.24), calls=%async_computation | async-start | bytes 393216 | tf_op jit(solution)/shard_map/all_to_all | solution.py:320
  22.8 3.1 %collective-permute-start = (bf16[4112,128]{1,0:T(8,128)(2,1)}, bf16[4112,128]{1,0:T(8,128)(2,1)S(1)}, u32[]{:S(2)}, u32[]{:S(2)}) collective-permute-start(bf16[4112,128]{1,0:T(8,128)(2,1)} %get-tuple-element.17.refs_0_), channel_id=1, source_target_pairs={{0,4},{4,0},{1,5},{5,1},{2,6},{6,2},{3,7},{7,3},{8,12},{12,8},{9,1... | collective-permute-start | bytes 3158024 | tf_op jit(solution)/shard_map/ppermute | solution.py:287
  26.0 9.2 %all-to-all-done = bf16[16,3,16,128]{3,2,1,0:T(8,128)(2,1)S(1)} async-done(((bf16[16,3,16,128]{3,2,1,0:T(8,128)(2,1)}), bf16[16,3,16,128]{3,2,1,0:T(8,128)(2,1)S(1)}, u32[]{:S(2)}, u32[]{:S(2)}) %all-to-all-start) | async-done | bytes 196640 | tf_op jit(solution)/shard_map/all_to_all | solution.py:320
  35.2 0.0 collective-permute-done.2.refs_0_.refs_2_
  35.2 0.0 copy-start.7
  35.2 7.0 %collective-permute-start.3 = (bf16[4112,128]{1,0:T(8,128)(2,1)S(1)}, bf16[4112,128]{1,0:T(8,128)(2,1)S(1)}, u32[]{:S(2)}, u32[]{:S(2)}) collective-permute-start(bf16[4112,128]{1,0:T(8,128)(2,1)S(1)} %collective-permute-done.2.refs_0_.refs_2_), channel_id=1, source_target_pairs={{0,4},{4,0},{1,5},{5,1},{2,6},{6,2},{3,7},{7,3},{8,12},{12,8},{9,1... | collective-permute-start | bytes 3158024 | tf_op jit(solution)/shard_map/ppermute | solution.py:287
  42.2 1.9 %collective-permute-start.1 = (bf16[48,16,128]{2,1,0:T(8,128)(2,1)S(1)}, bf16[48,16,128]{2,1,0:T(8,128)(2,1)S(1)}, u32[]{:S(2)}, u32[]{:S(2)}) collective-permute-start(bf16[48,16,128]{2,1,0:T(8,128)(2,1)S(1)} %bitcast.17), channel_id=1, source_target_pairs={{0,8},{8,0},{16,24},{24,16},{1,9},{9,1},{17,25},{25,17},{2,10},{10... | collective-permute-start | bytes 589832 | tf_op jit(solution)/shard_map/ppermute | solution.py:287
  44.1 0.0 collective-permute-done.refs_1_
  44.1 0.0 copy-start.9
  44.1 1.2 %copy-done.9 = bf16[4112,128]{1,0:T(8,128)(2,1)S(1)} copy-done((bf16[4112,128]{1,0:T(8,128)(2,1)S(1)}, bf16[4112,128]{1,0:T(8,128)(2,1)}, u32[]{:S(2)}) %copy-start.9) | copy-done | bytes 1052696
  45.3 2.1 %attend.3.a_ref = bf16[51,16,128]{2,1,0:T(8,128)(2,1)S(1)} custom-call(bf16[48,16,128]{2,1,0:T(8,128)(2,1)S(1)} %bitcast.18, bf16[4112,128]{1,0:T(8,128)(2,1)S(1)} %copy-done.9, bf16[4112,128]{1,0:T(8,128)(2,1)S(1)} %collective-permute-done.refs_1_), custom_call_target="tpu_custom_call" | custom-call | flops 1207959552 | bytes 3000000 | tf_op jit(solution)/shard_map/attend/pallas_call | solution.py:330
  47.5 3.1 %collective-permute-done.1.q_ref = bf16[48,16,128]{2,1,0:T(8,128)(2,1)S(1)} collective-permute-done((bf16[48,16,128]{2,1,0:T(8,128)(2,1)S(1)}, bf16[48,16,128]{2,1,0:T(8,128)(2,1)S(1)}, u32[]{:S(2)}, u32[]{:S(2)}) %collective-permute-start.1) | collective-permute-done | bytes 196640 | tf_op jit(solution)/shard_map/ppermute | solution.py:287
  50.6 0.0 collective-permute-done.3.refs_1_.refs_3_
  50.6 0.0 copy-done.7
  50.6 4.5 %attend.5 = bf16[51,16,128]{2,1,0:T(8,128)(2,1)S(1)} custom-call(bf16[48,16,128]{2,1,0:T(8,128)(2,1)S(1)} %collective-permute-done.1.q_ref, bf16[4112,128]{1,0:T(8,128)(2,1)S(1)} %copy-done.9, bf16[4112,128]{1,0:T(8,128)(2,1)S(1)} %collective-permute-done.refs_1_, bf16[4112,128]{1,0:T(8,128)(2,1)S(1)} %collective-permute-done.2.refs_0_.refs_2_, ...), custom_call_target="tpu_custom_call" | custom-call | flops 2415919104 | bytes 3000000 | tf_op jit(solution)/shard_map/attend/pallas_call | solution.py:330
  55.1 0.0 copy-start
  55.1 2.3 %collective-permute-start.4 = (bf16[51,16,128]{2,1,0:T(8,128)(2,1)S(1)}, bf16[51,16,128]{2,1,0:T(8,128)(2,1)S(1)}, u32[]{:S(2)}, u32[]{:S(2)}) collective-permute-start(bf16[51,16,128]{2,1,0:T(8,128)(2,1)S(1)} %attend.5), channel_id=1, source_target_pairs={{0,8},{8,0},{16,24},{24,16},{1,9},{9,1},{17,25},{25,17},{2,10},{10... | collective-permute-start | bytes 626696 | tf_op jit(solution)/shard_map/ppermute | solution.py:287
  57.3 0.0 copy-start.8
  57.3 1.2 %copy-done.8 = bf16[4112,128]{1,0:T(8,128)(2,1)S(1)} copy-done((bf16[4112,128]{1,0:T(8,128)(2,1)S(1)}, bf16[4112,128]{1,0:T(8,128)(2,1)}, u32[]{:S(2)}) %copy-start.8) | copy-done | bytes 1052696
  58.6 2.1 %attend.4.b_ref = bf16[51,16,128]{2,1,0:T(8,128)(2,1)S(1)} custom-call(bf16[48,16,128]{2,1,0:T(8,128)(2,1)S(1)} %bitcast.19, bf16[4112,128]{1,0:T(8,128)(2,1)S(1)} %copy-done.8, bf16[4112,128]{1,0:T(8,128)(2,1)S(1)} %collective-permute-done.3.refs_1_.refs_3_), custom_call_target="tpu_custom_call" | custom-call | flops 1207959552 | bytes 3000000 | tf_op jit(solution)/shard_map/attend/pallas_call | solution.py:330
  60.6 0.0 copy-start.3
  60.7 0.0 copy-start.6
  60.7 2.4 %collective-permute-done.4.c_ref = bf16[51,16,128]{2,1,0:T(8,128)(2,1)S(1)} collective-permute-done((bf16[51,16,128]{2,1,0:T(8,128)(2,1)S(1)}, bf16[51,16,128]{2,1,0:T(8,128)(2,1)S(1)}, u32[]{:S(2)}, u32[]{:S(2)}) %collective-permute-start.4) | collective-permute-done | bytes 208928 | tf_op jit(solution)/shard_map/ppermute | solution.py:287
  63.1 1.3 %merge.1 = bf16[896,128]{1,0:T(8,128)(2,1)} custom-call(bf16[51,16,128]{2,1,0:T(8,128)(2,1)S(1)} %attend.3.a_ref, bf16[51,16,128]{2,1,0:T(8,128)(2,1)S(1)} %attend.4.b_ref, bf16[51,16,128]{2,1,0:T(8,128)(2,1)S(1)} %collective-permute-done.4.c_ref), custom_call_target="tpu_custom_call" | custom-call | bytes 1000000 | tf_op jit(solution)/shard_map/merge/pallas_call | solution.py:348
  64.4 0.0 copy-done
  64.4 0.0 copy-start.4
  64.4 0.0 copy-start.5
  64.4 3.7 %collective-permute-start.5 = (bf16[2048,640]{1,0:T(8,128)(2,1)S(1)}, bf16[2048,640]{1,0:T(8,128)(2,1)}, u32[]{:S(2)}, u32[]{:S(2)}) collective-permute-start(bf16[2048,640]{1,0:T(8,128)(2,1)S(1)} %copy-done), channel_id=1, source_target_pairs={{0,4},{4,0},{1,5},{5,1},{2,6},{6,2},{3,7},{7,3},{8,12},{12,8},{9,1... | collective-permute-start | bytes 7864328 | tf_op jit(solution)/shard_map/ppermute | solution.py:287
  68.2 6.9 %all-to-all-start.1 = ((bf16[16,56,128]{2,1,0:T(8,128)(2,1)}), bf16[16,56,128]{2,1,0:T(8,128)(2,1)S(1)}, u32[]{:S(2)}, u32[]{:S(2)}) async-start(bf16[16,56,128]{2,1,0:T(8,128)(2,1)} %bitcast.5), calls=%async_computation.1 | async-start | bytes 458752 | tf_op jit(solution)/shard_map/all_to_all | solution.py:359
  75.1 0.0 copy-done.3
  75.1 0.0 copy-done.6
  75.1 0.0 copy-start.1
  75.1 1.0 copy-done.1
  76.2 0.0 copy-start.2
  76.2 1.0 copy-done.2
  77.2 4.4 %suffix.1.suffix_hbm = f32[16,32,128]{2,1,0:T(8,128)S(1)} custom-call(s32[16]{0:T(128)S(1)} %copy-done.6, bf16[16,16,128]{2,1,0:T(8,128)(2,1)S(1)} %copy-done.3, bf16[16,128,128]{2,1,0:T(8,128)(2,1)S(1)} %bitcast.15, bf16[16,128,128]{2,1,0:T(8,128)(2,1)S(1)} %bitcast.16), custom_call_target="tpu_custom_call" | custom-call | flops 16777216 | bytes 2000000 | tf_op jit(solution)/shard_map/suffix/pallas_call | solution.py:368
  81.6 7.3 %all-to-all-done.1 = bf16[16,56,128]{2,1,0:T(8,128)(2,1)S(1)} async-done(((bf16[16,56,128]{2,1,0:T(8,128)(2,1)}), bf16[16,56,128]{2,1,0:T(8,128)(2,1)S(1)}, u32[]{:S(2)}, u32[]{:S(2)}) %all-to-all-start.1) | async-done | bytes 229408 | tf_op jit(solution)/shard_map/all_to_all | solution.py:359
  88.9 0.0 collective-permute-done.5.other_ref
  88.9 0.0 copy-done.4
  88.9 0.0 copy-done.5
  88.9 0.8 combine.1
  89.8 9.6 %all_gather.3.attended_ref = bf16[64,2048]{1,0:T(8,128)(2,1)S(1)} all-gather(bf16[16,2048]{1,0:T(8,128)(2,1)S(1)} %combine.1), channel_id=1, replica_groups=mesh['pool'=16,'y'=4,'core'=2,'head'=4] {'y'}, dimensions={0}, use_global_device_ids=true | all-gather | bytes 327680 | tf_op jit(solution)/shard_map/all_gather | solution.py:404
  99.4 2.8 %project.1 = bf16[2,64,640]{2,1,0:T(8,128)(2,1)S(1)} custom-call(bf16[64,2048]{1,0:T(8,128)(2,1)S(1)} %all_gather.3.attended_ref, bf16[2048,640]{1,0:T(8,128)(2,1)S(1)} %copy-done, bf16[2048,640]{1,0:T(8,128)(2,1)} %collective-permute-done.5.other_ref), custom_call_target="tpu_custom_call" | custom-call | flops 335544320 | bytes 6000000 | tf_op jit(solution)/shard_map/project/pallas_call | solution.py:405
  102.1 16.3 %all_to_all.15 = bf16[8,16,640]{2,1,0:T(8,128)(2,1)S(1)} all-to-all(bf16[8,16,640]{2,1,0:T(8,128)(2,1)S(1)} %bitcast.14), channel_id=1, replica_groups=mesh['pool'=16,'y'=4,'core'=2,'head'=4] {'core','head'}, dimensions={0} | all-to-all | bytes 327680 | tf_op jit(solution)/shard_map/all_to_all | solution.py:419
  118.4 0.6 bitcast_reduce_fusion
Async XLA Ops:
  2.4 32.8 %collective-permute-start.2 = (bf16[4112,128]{1,0:T(8,128)(2,1)}, bf16[4112,128]{1,0:T(8,128)(2,1)S(1)}, u32[]{:S(2)}, u32[]{:S(2)}) collective-permute-start(bf16[4112,128]{1,0:T(8,128)(2,1)} %get-tuple-element.17.refs_0_), channel_id=1, source_target_pairs={{0,24},{8,16},{16,8},{24,0},{1,25},{9,17},{17,9},{25,1},{2,26},{10... | collective-permute-start | bytes 3158024 | tf_op jit(solution)/shard_map/ppermute | solution.py:287
  7.9 27.3 %all-to-all-start = ((bf16[16,3,16,128]{3,2,1,0:T(8,128)(2,1)}), bf16[16,3,16,128]{3,2,1,0:T(8,128)(2,1)S(1)}, u32[]{:S(2)}, u32[]{:S(2)}) async-start(bf16[16,3,16,128]{3,2,1,0:T(8,128)(2,1)} %bitcast.24), calls=%async_computation | async-start | bytes 393216 | tf_op jit(solution)/shard_map/all_to_all | solution.py:320
  22.8 21.3 %collective-permute-start = (bf16[4112,128]{1,0:T(8,128)(2,1)}, bf16[4112,128]{1,0:T(8,128)(2,1)S(1)}, u32[]{:S(2)}, u32[]{:S(2)}) collective-permute-start(bf16[4112,128]{1,0:T(8,128)(2,1)} %get-tuple-element.17.refs_0_), channel_id=1, source_target_pairs={{0,4},{4,0},{1,5},{5,1},{2,6},{6,2},{3,7},{7,3},{8,12},{12,8},{9,1... | collective-permute-start | bytes 3158024 | tf_op jit(solution)/shard_map/ppermute | solution.py:287
  35.2 15.4 %copy-start.7 = (bf16[4112,128]{1,0:T(8,128)(2,1)}, bf16[4112,128]{1,0:T(8,128)(2,1)S(1)}, u32[]{:S(2)}) copy-start(bf16[4112,128]{1,0:T(8,128)(2,1)S(1)} %collective-permute-done.2.refs_0_.refs_2_) | copy-start | bytes 3158020
  35.2 15.4 %collective-permute-start.3 = (bf16[4112,128]{1,0:T(8,128)(2,1)S(1)}, bf16[4112,128]{1,0:T(8,128)(2,1)S(1)}, u32[]{:S(2)}, u32[]{:S(2)}) collective-permute-start(bf16[4112,128]{1,0:T(8,128)(2,1)S(1)} %collective-permute-done.2.refs_0_.refs_2_), channel_id=1, source_target_pairs={{0,4},{4,0},{1,5},{5,1},{2,6},{6,2},{3,7},{7,3},{8,12},{12,8},{9,1... | collective-permute-start | bytes 3158024 | tf_op jit(solution)/shard_map/ppermute | solution.py:287
  42.2 8.4 %collective-permute-start.1 = (bf16[48,16,128]{2,1,0:T(8,128)(2,1)S(1)}, bf16[48,16,128]{2,1,0:T(8,128)(2,1)S(1)}, u32[]{:S(2)}, u32[]{:S(2)}) collective-permute-start(bf16[48,16,128]{2,1,0:T(8,128)(2,1)S(1)} %bitcast.17), channel_id=1, source_target_pairs={{0,8},{8,0},{16,24},{24,16},{1,9},{9,1},{17,25},{25,17},{2,10},{10... | collective-permute-start | bytes 589832 | tf_op jit(solution)/shard_map/ppermute | solution.py:287
  44.1 1.2 %copy-start.9 = (bf16[4112,128]{1,0:T(8,128)(2,1)S(1)}, bf16[4112,128]{1,0:T(8,128)(2,1)}, u32[]{:S(2)}) copy-start(bf16[4112,128]{1,0:T(8,128)(2,1)} %get-tuple-element.17.refs_0_) | copy-start | bytes 3158020
  55.1 9.4 %copy-start = (bf16[2048,640]{1,0:T(8,128)(2,1)S(1)}, bf16[2048,640]{1,0:T(8,128)(2,1)}, u32[]{:S(2)}) copy-start(bf16[2048,640]{1,0:T(8,128)(2,1)} %own_ref.1) | copy-start | bytes 7864324
  55.1 8.1 %collective-permute-start.4 = (bf16[51,16,128]{2,1,0:T(8,128)(2,1)S(1)}, bf16[51,16,128]{2,1,0:T(8,128)(2,1)S(1)}, u32[]{:S(2)}, u32[]{:S(2)}) collective-permute-start(bf16[51,16,128]{2,1,0:T(8,128)(2,1)S(1)} %attend.5), channel_id=1, source_target_pairs={{0,8},{8,0},{16,24},{24,16},{1,9},{9,1},{17,25},{25,17},{2,10},{10... | collective-permute-start | bytes 626696 | tf_op jit(solution)/shard_map/ppermute | solution.py:287
  57.3 1.2 %copy-start.8 = (bf16[4112,128]{1,0:T(8,128)(2,1)S(1)}, bf16[4112,128]{1,0:T(8,128)(2,1)}, u32[]{:S(2)}) copy-start(bf16[4112,128]{1,0:T(8,128)(2,1)} %copy-done.7) | copy-start | bytes 3158020
  60.6 14.4 %copy-start.3 = (bf16[16,16,128]{2,1,0:T(8,128)(2,1)S(1)}, bf16[16,16,128]{2,1,0:T(8,128)(2,1)}, u32[]{:S(2)}) copy-start(bf16[16,16,128]{2,1,0:T(8,128)(2,1)} %q_ref) | copy-start | bytes 196612
  60.7 14.4 %copy-start.6 = (s32[16]{0:T(128)S(1)}, s32[16]{0:T(128)}, u32[]{:S(2)}) copy-start(s32[16]{0:T(128)} %length_hbm.1) | copy-start | bytes 196
  64.4 24.5 %copy-start.4 = (s32[16,1]{0,1:T(1,128)S(1)}, s32[16,1]{0,1:T(1,128)}, u32[]{:S(2)}) copy-start(s32[16,1]{0,1:T(1,128)} %param.15) | copy-start | bytes 196
  64.4 24.5 %copy-start.5 = (s32[16]{0:T(128)S(1)}, s32[16]{0:T(128)}, u32[]{:S(2)}) copy-start(s32[16]{0:T(128)} %owner_hbm.3) | copy-start | bytes 196
  64.4 24.5 %collective-permute-start.5 = (bf16[2048,640]{1,0:T(8,128)(2,1)S(1)}, bf16[2048,640]{1,0:T(8,128)(2,1)}, u32[]{:S(2)}, u32[]{:S(2)}) collective-permute-start(bf16[2048,640]{1,0:T(8,128)(2,1)S(1)} %copy-done), channel_id=1, source_target_pairs={{0,4},{4,0},{1,5},{5,1},{2,6},{6,2},{3,7},{7,3},{8,12},{12,8},{9,1... | collective-permute-start | bytes 7864328 | tf_op jit(solution)/shard_map/ppermute | solution.py:287
  68.2 20.8 %all-to-all-start.1 = ((bf16[16,56,128]{2,1,0:T(8,128)(2,1)}), bf16[16,56,128]{2,1,0:T(8,128)(2,1)S(1)}, u32[]{:S(2)}, u32[]{:S(2)}) async-start(bf16[16,56,128]{2,1,0:T(8,128)(2,1)} %bitcast.5), calls=%async_computation.1 | async-start | bytes 458752 | tf_op jit(solution)/shard_map/all_to_all | solution.py:359
  75.1 1.0 copy-start.1
  76.2 1.0 copy-start.2

commit v6 on v4

--- a/solution.py
+++ b/solution.py
@@ -88,8 +88,15 @@
             ].astype(BF16)
 
 
-def attend_kernel(q_ref, *refs):
-    blocks, out_ref = refs[:-1], refs[-1]
+def unpack_lse(ref):
+    slots = ref.shape[0] - 3
+    high, middle, low = (ref[slots + i].astype(F32) for i in range(3))
+    return (low + middle) + high
+
+
+def attend_kernel(merging, q_ref, *refs):
+    earlier_ref = refs[0] if merging else None
+    blocks, out_ref = refs[int(merging) : -1], refs[-1]
     slots = q_ref.shape[0]
     step_slots = math.gcd(24, slots)
     length = (blocks[0].shape[0] - TAIL) // 4
@@ -120,6 +127,8 @@
             + biases[n]
         )
 
+    if merging:
+        earlier_lse = unpack_lse(earlier_ref)
     packed = [jnp.zeros((GROUP, 128), F32)] * 2
     kept = {}
     q = query(units[0])
@@ -149,6 +158,20 @@
         kept[g] = (both[:, :HD] / safe).reshape(step_slots, GROUP, HD)
         lse = jnp.where(live, peak * SCALE + jnp.log(safe), LOWEST)
         lse = lse.reshape(step_slots, GROUP, HD)
+        if merging:
+            half = slice(g * GROUP, (g + 1) * GROUP)
+            before = jnp.stack(
+                [
+                    jnp.broadcast_to(earlier_lse[half, s : s + 1], (GROUP, HD))
+                    for s in range(start, start + step_slots)
+                ]
+            )
+            result = earlier_ref[pl.ds(start, step_slots)].astype(F32)[:, half, :]
+            top = jnp.maximum(lse, before)
+            a = jnp.exp(lse - top)
+            b = jnp.exp(before - top)
+            kept[g] = (a * kept[g] + b * result) / (a + b)
+            lse = top + jnp.log(a + b)
         for s in range(step_slots):
             packed[g] = jnp.where(lane == start + s, lse[s], packed[g])
         if g == 1:
@@ -159,14 +182,11 @@
         out_ref[slots + i] = plane.astype(BF16)
 
 
-def merge_kernel(a_ref, b_ref, c_ref, out_ref):
-    blocks = (a_ref, b_ref, c_ref)
+def merge_kernel(a_ref, b_ref, out_ref):
+    blocks = (a_ref, b_ref)
     slots = a_ref.shape[0] - 3
     pools = slots // CAP
-    lses = [
-        (ref[slots + 2].astype(F32) + ref[slots + 1].astype(F32)) + ref[slots].astype(F32)
-        for ref in blocks
-    ]
+    lses = [unpack_lse(ref) for ref in blocks]
     top = functools.reduce(jnp.maximum, lses)
     shares = [jnp.exp(lse - top) for lse in lses]
     total = functools.reduce(jnp.add, shares)
@@ -331,37 +351,40 @@
     asked = meet(arrived, "y", 1)
 
     pair, arrived_later = lax.optimization_barrier((meet(own, "y", 3), arrived))
-    blocks = {(0, 0): own, (0, 1): meet(own, "core", 1), (1, 0): pair, (1, 1): meet(pair, "core", 1)}
-
-    def attend(q, *sources):
+    blocks = {(0, 0): own, (0, 1): meet(own, "core", 1), (1, 0): pair}
+
+    def attend(q, sources, earlier=None, times=1):
         span = len(sources) * length
+        merging = earlier is not None
         return pl.pallas_call(
-            attend_kernel,
+            functools.partial(attend_kernel, merging),
             out_shape=shape((slots + 3, heads, hdim), BF16),
-            in_specs=[VMEM] * (1 + len(sources)),
+            in_specs=[VMEM] * (1 + merging + len(sources)),
             out_specs=VMEM,
             compiler_params=params(30),
             cost_estimate=pl.CostEstimate(
-                flops=6 * slots * heads * span * hdim,
+                flops=6 * times * slots * heads * span * hdim,
                 bytes_accessed=3_000_000,
                 transcendentals=slots * heads * span,
             ),
             name="attend",
-        )(q, *(blocks[source] for source in sources))
+        )(q, *([earlier] if merging else []), *(blocks[source] for source in sources))
 
     near, far = ((0, 0), (0, 1)), ((1, 0), (1, 1))
-    near_part, asked = lax.optimization_barrier((attend(arrived, *near), asked))
-    answer = meet(attend(asked, *near, *far), "y", 1)
-    far_part = attend(arrived_later, *far)
+    first = attend(arrived_later, near[:1])
+    blocks[1, 0], first = lax.optimization_barrier((pair, first))
+    blocks[1, 1] = meet(blocks[1, 0], "core", 1)
+    answer = meet(attend(asked, far, attend(asked, near, times=10)), "y", 1)
+    own_part = attend(arrived_later, near[1:] + far, first)
     merged = pl.pallas_call(
         merge_kernel,
         out_shape=shape((pools * (CAP * heads + GROUP), hdim), BF16),
-        in_specs=[VMEM] * 3,
+        in_specs=[VMEM] * 2,
         out_specs=VMEM,
         compiler_params=params(8),
         cost_estimate=pl.CostEstimate(flops=0, bytes_accessed=1_000_000, transcendentals=0),
         name="merge",
-    )(near_part, far_part, answer)
+    )(own_part, answer)
     merged, queries_later = lax.optimization_barrier((merged, queries))
     returned = lax.all_to_all(
         merged.reshape(pools, CAP * heads + GROUP, hdim),

time: 116 us -> 111 us (0.957)
  blocking collectives: 18.2 us -> 43.2 us
  waiting for transfers between devices: 23.2 us -> 8.24 us
  starting transfers between devices: 50.8 us -> 36.3 us
    all_to_all x0 -> x1, blocking collectives: none -> 25.8 us  [body(): lax.all_to_all(outgoing.reshape(pools, CAP, heads, hdim), 'pool', split_a...]
    all_to_all x1 -> x0, starting transfers between devices: 14.9 us -> none  [body(): lax.all_to_all(outgoing.reshape(pools, CAP, heads, hdim), 'pool', split_a...]
    all_to_all x1 -> x0, waiting for transfers between devices: 9.22 us -> none  [body(): lax.all_to_all(outgoing.reshape(pools, CAP, heads, hdim), 'pool', split_a...]
    ppermute x6, waiting for transfers between devices: 7.9 us -> 2.16 us  [meet(): return lax.ppermute(value, axis, pairs)]
    ppermute x6, starting transfers between devices: 28.8 us -> 30.3 us  [meet(): return lax.ppermute(value, axis, pairs)]
    pallas_call x3 -> x4, Pallas kernels: 8.63 us -> 9.13 us  [attend(): pl.pallas_call(functools.partial(attend_kernel, merging), out_shape=shape...]
  transfers between devices with their start and end apart: 8 -> 7, of which waited for: 5 -> 4; matrix products, arithmetic and copies ran while one was open for 0% -> 0% of each run, Pallas kernels for 8% -> 10%
where the time goes in v6:
time: 111 us; the launch traced here: 110 us
  blocking collectives  43.2 us (39%)
  starting transfers between devices  36.3 us (33%)
  Pallas kernels  18.5 us (17%)
  waiting for transfers between devices  8.24 us (7%)
  local copies, waits for them, and re-layouts  3.32 us (3%)
    ppermute x6, starting transfers between devices, meet(): return lax.ppermute(value, axis, pairs)  30.3 us
    all_to_all x1, blocking collectives, body(): lax.all_to_all(outgoing.reshape(pools, CAP, heads, hdim), 'pool', split_a...  25.8 us
    pallas_call x4, Pallas kernels, attend(): pl.pallas_call(functools.partial(attend_kernel, merging), out_shape=shape...  9.13 us
    all_to_all x1, blocking collectives, body(): lax.all_to_all(terms.reshape(lax.axis_size('head'), -1, columns), 'head',...  8.81 us
    all_to_all x1, blocking collectives, body(): lax.all_to_all(attended, 'y', split_axis=0, concat_axis=0, tiled=True)  8.57 us
    all_to_all x1, waiting for transfers between devices, body(): lax.all_to_all(merged.reshape(pools, CAP * heads + GROUP, hdim), 'pool',...  6.08 us
    all_to_all x1, starting transfers between devices, body(): lax.all_to_all(merged.reshape(pools, CAP * heads + GROUP, hdim), 'pool',...  6.01 us
    pallas_call x1, Pallas kernels, body(): pl.pallas_call(suffix_kernel, out_shape=shape((rows, 2 * heads, hdim), F3...  4.41 us
  transfers between devices with their start and end apart: 7, of which 4 were waited for; matrix products, arithmetic and copies ran while one was open for 0% of the time, Pallas kernels for 10%

profile of v6, /device:TPU:1, one launch (start us, length us, event | category | flops | bytes accessed | tf_op | source)
XLA Modules:
  0.0 110.4 jit_solution(14915765175993499841)
XLA Ops:
  0.0 2.4 %dispatch.1 = (bf16[48,16,128]{2,1,0:T(8,128)(2,1)}, bf16[4112,128]{1,0:T(8,128)(2,1)}) custom-call(s32[16]{0:T(128)} %bitcast.17, s32[16]{0:T(128)} %owner_hbm.3, s32[16]{0:T(128)} %lengths_hbm.1, bf16[16,16,128]{2,1,0:T(8,128)(2,1)} %q_ref, bf16[2048,128]{1,0:T(8,128)(2,1)} %bitcast.19, bf16[2048,128]{1,0:T(8,128)(2,1)} %bitcast.20), custom_call_target="tpu_custom_call" | custom-call | bytes 3000000 | tf_op jit(solution)/shard_map/dispatch/pallas_call | solution.py:321
  2.4 5.5 %collective-permute-start = (bf16[4112,128]{1,0:T(8,128)(2,1)}, bf16[4112,128]{1,0:T(8,128)(2,1)S(1)}, u32[]{:S(2)}, u32[]{:S(2)}) collective-permute-start(bf16[4112,128]{1,0:T(8,128)(2,1)} %get-tuple-element.13.refs_0_), channel_id=1, source_target_pairs={{0,24},{8,16},{16,8},{24,0},{1,25},{9,17},{17,9},{25,1},{2,26},{10... | collective-permute-start | bytes 3158024 | tf_op jit(solution)/shard_map/ppermute | solution.py:315
  7.9 5.2 %collective-permute-start.1 = (bf16[4112,128]{1,0:T(8,128)(2,1)}, bf16[4112,128]{1,0:T(8,128)(2,1)S(1)}, u32[]{:S(2)}, u32[]{:S(2)}) collective-permute-start(bf16[4112,128]{1,0:T(8,128)(2,1)} %get-tuple-element.13.refs_0_), channel_id=1, source_target_pairs={{0,4},{4,0},{1,5},{5,1},{2,6},{6,2},{3,7},{7,3},{8,12},{12,8},{9,1... | collective-permute-start | bytes 3158024 | tf_op jit(solution)/shard_map/ppermute | solution.py:315
  13.1 25.8 %all_to_all.20 = bf16[16,3,16,128]{3,2,1,0:T(8,128)(2,1)S(1)} all-to-all(bf16[16,3,16,128]{3,2,1,0:T(8,128)(2,1)} %bitcast.21), channel_id=1, replica_groups=mesh['pool'=16,'y'=4,'core'=2,'head'=4] {'pool'}, dimensions={0} | all-to-all | bytes 393216 | tf_op jit(solution)/shard_map/all_to_all | solution.py:348
  38.9 1.9 %collective-permute-start.3 = (bf16[48,16,128]{2,1,0:T(8,128)(2,1)S(1)}, bf16[48,16,128]{2,1,0:T(8,128)(2,1)S(1)}, u32[]{:S(2)}, u32[]{:S(2)}) collective-permute-start(bf16[48,16,128]{2,1,0:T(8,128)(2,1)S(1)} %bitcast.14), channel_id=1, source_target_pairs={{0,8},{8,0},{16,24},{24,16},{1,9},{9,1},{17,25},{25,17},{2,10},{10... | collective-permute-start | bytes 589832 | tf_op jit(solution)/shard_map/ppermute | solution.py:315
  40.9 0.0 collective-permute-done.refs_2_.refs_1_
  40.9 0.0 copy-start.7
  40.9 1.2 %copy-done.7 = bf16[4112,128]{1,0:T(8,128)(2,1)S(1)} copy-done((bf16[4112,128]{1,0:T(8,128)(2,1)S(1)}, bf16[4112,128]{1,0:T(8,128)(2,1)}, u32[]{:S(2)}) %copy-start.7) | copy-done | bytes 1052696
  42.1 1.2 %attend.4.refs_0_ = bf16[51,16,128]{2,1,0:T(8,128)(2,1)S(1)} custom-call(bf16[48,16,128]{2,1,0:T(8,128)(2,1)S(1)} %bitcast.15, bf16[4112,128]{1,0:T(8,128)(2,1)S(1)} %copy-done.7), custom_call_target="tpu_custom_call" | custom-call | flops 603979776 | bytes 3000000 | tf_op jit(solution)/shard_map/attend/pallas_call | solution.py:359
  43.3 5.0 %collective-permute-start.2 = (bf16[4112,128]{1,0:T(8,128)(2,1)S(1)}, bf16[4112,128]{1,0:T(8,128)(2,1)S(1)}, u32[]{:S(2)}, u32[]{:S(2)}) collective-permute-start(bf16[4112,128]{1,0:T(8,128)(2,1)S(1)} %collective-permute-done.refs_2_.refs_1_), channel_id=1, source_target_pairs={{0,4},{4,0},{1,5},{5,1},{2,6},{6,2},{3,7},{7,3},{8,12},{12,8},{9,1... | collective-permute-start | bytes 3158024 | tf_op jit(solution)/shard_map/ppermute | solution.py:315
  48.3 0.0 collective-permute-done.3.q_ref
  48.3 0.0 collective-permute-done.1.refs_1_
  48.3 2.1 %attend.6.refs_0_ = bf16[51,16,128]{2,1,0:T(8,128)(2,1)S(1)} custom-call(bf16[48,16,128]{2,1,0:T(8,128)(2,1)S(1)} %collective-permute-done.3.q_ref, bf16[4112,128]{1,0:T(8,128)(2,1)S(1)} %copy-done.7, bf16[4112,128]{1,0:T(8,128)(2,1)S(1)} %collective-permute-done.1.refs_1_), custom_call_target="tpu_custom_call" | custom-call | flops 12079595520 | bytes 3000000 | tf_op jit(solution)/shard_map/attend/pallas_call | solution.py:359
  50.5 0.1 collective-permute-done.2.refs_3_.refs_2_
  50.6 2.4 %attend.7 = bf16[51,16,128]{2,1,0:T(8,128)(2,1)S(1)} custom-call(bf16[48,16,128]{2,1,0:T(8,128)(2,1)S(1)} %collective-permute-done.3.q_ref, bf16[51,16,128]{2,1,0:T(8,128)(2,1)S(1)} %attend.6.refs_0_, bf16[4112,128]{1,0:T(8,128)(2,1)S(1)} %collective-permute-done.refs_2_.refs_1_, bf16[4112,128]{1,0:T(8,128)(2,1)S(1)} %collective-permute-done.2.refs_3_.refs_2_), custom_call_target="tpu_custom_call" | custom-call | flops 1207959552 | bytes 3000000 | tf_op jit(solution)/shard_map/attend/pallas_call | solution.py:359
  53.0 3.5 %collective-permute-start.4 = (bf16[51,16,128]{2,1,0:T(8,128)(2,1)S(1)}, bf16[51,16,128]{2,1,0:T(8,128)(2,1)S(1)}, u32[]{:S(2)}, u32[]{:S(2)}) collective-permute-start(bf16[51,16,128]{2,1,0:T(8,128)(2,1)S(1)} %attend.7), channel_id=1, source_target_pairs={{0,8},{8,0},{16,24},{24,16},{1,9},{9,1},{17,25},{25,17},{2,10},{10... | collective-permute-start | bytes 626696 | tf_op jit(solution)/shard_map/ppermute | solution.py:315
  56.5 3.4 %attend.5.a_ref = bf16[51,16,128]{2,1,0:T(8,128)(2,1)S(1)} custom-call(bf16[48,16,128]{2,1,0:T(8,128)(2,1)S(1)} %bitcast.16, bf16[51,16,128]{2,1,0:T(8,128)(2,1)S(1)} %attend.4.refs_0_, bf16[4112,128]{1,0:T(8,128)(2,1)S(1)} %collective-permute-done.1.refs_1_, bf16[4112,128]{1,0:T(8,128)(2,1)S(1)} %collective-permute-done.refs_2_.refs_1_, ...), custom_call_target="tpu_custom_call" | custom-call | flops 1811939328 | bytes 3000000 | tf_op jit(solution)/shard_map/attend/pallas_call | solution.py:359
  59.9 0.0 copy-start.3
  59.9 0.0 copy-start.6
  59.9 0.9 collective-permute-done.4.b_ref
  60.8 1.2 %merge.1 = bf16[896,128]{1,0:T(8,128)(2,1)} custom-call(bf16[51,16,128]{2,1,0:T(8,128)(2,1)S(1)} %attend.5.a_ref, bf16[51,16,128]{2,1,0:T(8,128)(2,1)S(1)} %collective-permute-done.4.b_ref), custom_call_target="tpu_custom_call" | custom-call | bytes 1000000 | tf_op jit(solution)/shard_map/merge/pallas_call | solution.py:379
  62.0 0.0 copy-start.4
  62.0 0.0 copy-start.5
  62.0 6.0 %all-to-all-start.1 = ((bf16[16,56,128]{2,1,0:T(8,128)(2,1)}), bf16[16,56,128]{2,1,0:T(8,128)(2,1)S(1)}, u32[]{:S(2)}, u32[]{:S(2)}) async-start(bf16[16,56,128]{2,1,0:T(8,128)(2,1)} %bitcast.5), calls=%async_computation.1 | async-start | bytes 458752 | tf_op jit(solution)/shard_map/all_to_all | solution.py:389
  68.0 0.0 copy-done.3
  68.0 0.0 copy-done.6
  68.0 0.0 copy-start.1
  68.0 1.0 copy-done.1
  69.1 0.0 copy-start.2
  69.1 1.0 copy-done.2
  70.1 0.0 copy-start
  70.1 4.4 %suffix.1.suffix_hbm = f32[16,32,128]{2,1,0:T(8,128)S(1)} custom-call(s32[16]{0:T(128)S(1)} %copy-done.6, bf16[16,16,128]{2,1,0:T(8,128)(2,1)S(1)} %copy-done.3, bf16[16,128,128]{2,1,0:T(8,128)(2,1)S(1)} %bitcast.12, bf16[16,128,128]{2,1,0:T(8,128)(2,1)S(1)} %bitcast.13), custom_call_target="tpu_custom_call" | custom-call | flops 16777216 | bytes 2000000 | tf_op jit(solution)/shard_map/suffix/pallas_call | solution.py:397
  74.5 6.1 %all-to-all-done.1 = bf16[16,56,128]{2,1,0:T(8,128)(2,1)S(1)} async-done(((bf16[16,56,128]{2,1,0:T(8,128)(2,1)}), bf16[16,56,128]{2,1,0:T(8,128)(2,1)S(1)}, u32[]{:S(2)}, u32[]{:S(2)}) %all-to-all-start.1) | async-done | bytes 229408 | tf_op jit(solution)/shard_map/all_to_all | solution.py:389
  80.6 0.0 copy-done.4
  80.6 0.0 copy-done.5
  80.6 0.9 combine.1
  81.5 8.6 %all_to_all.21.own_ref = bf16[4,16,2048]{2,1,0:T(8,128)(2,1)S(1)} all-to-all(bf16[4,16,2048]{2,1,0:T(8,128)(2,1)S(1)} %combine.1), channel_id=1, replica_groups=mesh['pool'=16,'y'=4,'core'=2,'head'=4] {'y'}, dimensions={0} | all-to-all | bytes 524288 | tf_op jit(solution)/shard_map/all_to_all | solution.py:433
  90.1 9.2 %collective-permute-start.5 = (bf16[4,16,2048]{2,1,0:T(8,128)(2,1)S(1)}, bf16[4,16,2048]{2,1,0:T(8,128)(2,1)S(1)}, u32[]{:S(2)}, u32[]{:S(2)}) collective-permute-start(bf16[4,16,2048]{2,1,0:T(8,128)(2,1)S(1)} %all_to_all.21.own_ref), channel_id=1, source_target_pairs={{0,4},{4,0},{1,5},{5,1},{2,6},{6,2},{3,7},{7,3},{8,12},{12,8},{9,1... | collective-permute-start | bytes 786440 | tf_op jit(solution)/shard_map/ppermute | solution.py:315
  99.2 1.1 %collective-permute-done.5.other_ref = bf16[4,16,2048]{2,1,0:T(8,128)(2,1)S(1)} collective-permute-done((bf16[4,16,2048]{2,1,0:T(8,128)(2,1)S(1)}, bf16[4,16,2048]{2,1,0:T(8,128)(2,1)S(1)}, u32[]{:S(2)}, u32[]{:S(2)}) %collective-permute-start.5) | collective-permute-done | bytes 262176 | tf_op jit(solution)/shard_map/ppermute | solution.py:315
  100.4 0.0 copy-done
  100.4 0.6 project.1
  101.0 8.8 %all_to_all.22 = bf16[4,32,640]{2,1,0:T(8,128)(2,1)S(1)} all-to-all(bf16[4,32,640]{2,1,0:T(8,128)(2,1)S(1)} %bitcast.11), channel_id=1, replica_groups=mesh['pool'=16,'y'=4,'core'=2,'head'=4] {'head'}, dimensions={0} | all-to-all | bytes 327680 | tf_op jit(solution)/shard_map/all_to_all | solution.py:447
  109.8 0.6 reduce_sum.12
Async XLA Ops:
  2.4 38.5 %collective-permute-start = (bf16[4112,128]{1,0:T(8,128)(2,1)}, bf16[4112,128]{1,0:T(8,128)(2,1)S(1)}, u32[]{:S(2)}, u32[]{:S(2)}) collective-permute-start(bf16[4112,128]{1,0:T(8,128)(2,1)} %get-tuple-element.13.refs_0_), channel_id=1, source_target_pairs={{0,24},{8,16},{16,8},{24,0},{1,25},{9,17},{17,9},{25,1},{2,26},{10... | collective-permute-start | bytes 3158024 | tf_op jit(solution)/shard_map/ppermute | solution.py:315
  7.9 40.4 %collective-permute-start.1 = (bf16[4112,128]{1,0:T(8,128)(2,1)}, bf16[4112,128]{1,0:T(8,128)(2,1)S(1)}, u32[]{:S(2)}, u32[]{:S(2)}) collective-permute-start(bf16[4112,128]{1,0:T(8,128)(2,1)} %get-tuple-element.13.refs_0_), channel_id=1, source_target_pairs={{0,4},{4,0},{1,5},{5,1},{2,6},{6,2},{3,7},{7,3},{8,12},{12,8},{9,1... | collective-permute-start | bytes 3158024 | tf_op jit(solution)/shard_map/ppermute | solution.py:315
  38.9 9.4 %collective-permute-start.3 = (bf16[48,16,128]{2,1,0:T(8,128)(2,1)S(1)}, bf16[48,16,128]{2,1,0:T(8,128)(2,1)S(1)}, u32[]{:S(2)}, u32[]{:S(2)}) collective-permute-start(bf16[48,16,128]{2,1,0:T(8,128)(2,1)S(1)} %bitcast.14), channel_id=1, source_target_pairs={{0,8},{8,0},{16,24},{24,16},{1,9},{9,1},{17,25},{25,17},{2,10},{10... | collective-permute-start | bytes 589832 | tf_op jit(solution)/shard_map/ppermute | solution.py:315
  40.9 1.2 %copy-start.7 = (bf16[4112,128]{1,0:T(8,128)(2,1)S(1)}, bf16[4112,128]{1,0:T(8,128)(2,1)}, u32[]{:S(2)}) copy-start(bf16[4112,128]{1,0:T(8,128)(2,1)} %get-tuple-element.13.refs_0_) | copy-start | bytes 3158020
  43.3 7.3 %collective-permute-start.2 = (bf16[4112,128]{1,0:T(8,128)(2,1)S(1)}, bf16[4112,128]{1,0:T(8,128)(2,1)S(1)}, u32[]{:S(2)}, u32[]{:S(2)}) collective-permute-start(bf16[4112,128]{1,0:T(8,128)(2,1)S(1)} %collective-permute-done.refs_2_.refs_1_), channel_id=1, source_target_pairs={{0,4},{4,0},{1,5},{5,1},{2,6},{6,2},{3,7},{7,3},{8,12},{12,8},{9,1... | collective-permute-start | bytes 3158024 | tf_op jit(solution)/shard_map/ppermute | solution.py:315
  53.0 7.8 %collective-permute-start.4 = (bf16[51,16,128]{2,1,0:T(8,128)(2,1)S(1)}, bf16[51,16,128]{2,1,0:T(8,128)(2,1)S(1)}, u32[]{:S(2)}, u32[]{:S(2)}) collective-permute-start(bf16[51,16,128]{2,1,0:T(8,128)(2,1)S(1)} %attend.7), channel_id=1, source_target_pairs={{0,8},{8,0},{16,24},{24,16},{1,9},{9,1},{17,25},{25,17},{2,10},{10... | collective-permute-start | bytes 626696 | tf_op jit(solution)/shard_map/ppermute | solution.py:315
  59.9 8.1 %copy-start.3 = (bf16[16,16,128]{2,1,0:T(8,128)(2,1)S(1)}, bf16[16,16,128]{2,1,0:T(8,128)(2,1)}, u32[]{:S(2)}) copy-start(bf16[16,16,128]{2,1,0:T(8,128)(2,1)} %q_ref) | copy-start | bytes 196612
  59.9 8.1 %copy-start.6 = (s32[16]{0:T(128)S(1)}, s32[16]{0:T(128)}, u32[]{:S(2)}) copy-start(s32[16]{0:T(128)} %length_hbm.1) | copy-start | bytes 196
  62.0 18.6 %copy-start.4 = (s32[16,1]{0,1:T(1,128)S(1)}, s32[16,1]{0,1:T(1,128)}, u32[]{:S(2)}) copy-start(s32[16,1]{0,1:T(1,128)} %param.15) | copy-start | bytes 196
  62.0 18.6 %copy-start.5 = (s32[16]{0:T(128)S(1)}, s32[16]{0:T(128)}, u32[]{:S(2)}) copy-start(s32[16]{0:T(128)} %owner_hbm.3) | copy-start | bytes 196
  62.0 18.6 %all-to-all-start.1 = ((bf16[16,56,128]{2,1,0:T(8,128)(2,1)}), bf16[16,56,128]{2,1,0:T(8,128)(2,1)S(1)}, u32[]{:S(2)}, u32[]{:S(2)}) async-start(bf16[16,56,128]{2,1,0:T(8,128)(2,1)} %bitcast.5), calls=%async_computation.1 | async-start | bytes 458752 | tf_op jit(solution)/shard_map/all_to_all | solution.py:389
  68.0 1.0 copy-start.1
  69.1 1.0 copy-start.2
  70.1 30.3 %copy-start = (bf16[2048,640]{1,0:T(8,128)(2,1)S(1)}, bf16[2048,640]{1,0:T(8,128)(2,1)}, u32[]{:S(2)}) copy-start(bf16[2048,640]{1,0:T(8,128)(2,1)} %w_ref.1) | copy-start | bytes 7864324
  90.1 10.3 %collective-permute-start.5 = (bf16[4,16,2048]{2,1,0:T(8,128)(2,1)S(1)}, bf16[4,16,2048]{2,1,0:T(8,128)(2,1)S(1)}, u32[]{:S(2)}, u32[]{:S(2)}) collective-permute-start(bf16[4,16,2048]{2,1,0:T(8,128)(2,1)S(1)} %all_to_all.21.own_ref), channel_id=1, source_target_pairs={{0,4},{4,0},{1,5},{5,1},{2,6},{6,2},{3,7},{7,3},{8,12},{12,8},{9,1... | collective-permute-start | bytes 786440 | tf_op jit(solution)/shard_map/ppermute | solution.py:315

commit v7 on v6

--- a/solution.py
+++ b/solution.py
@@ -351,7 +351,7 @@
     asked = meet(arrived, "y", 1)
 
     pair, arrived_later = lax.optimization_barrier((meet(own, "y", 3), arrived))
-    blocks = {(0, 0): own, (0, 1): meet(own, "core", 1), (1, 0): pair}
+    blocks = {(0, 0): own, (1, 0): pair}
 
     def attend(q, sources, earlier=None, times=1):
         span = len(sources) * length
@@ -370,12 +370,12 @@
             name="attend",
         )(q, *([earlier] if merging else []), *(blocks[source] for source in sources))
 
-    near, far = ((0, 0), (0, 1)), ((1, 0), (1, 1))
-    first = attend(arrived_later, near[:1])
-    blocks[1, 0], first = lax.optimization_barrier((pair, first))
-    blocks[1, 1] = meet(blocks[1, 0], "core", 1)
-    answer = meet(attend(asked, far, attend(asked, near, times=10)), "y", 1)
-    own_part = attend(arrived_later, near[1:] + far, first)
+    first = attend(arrived_later, [(0, 0)])
+    mine, pair, first = lax.optimization_barrier((own, pair, first))
+    blocks.update({(0, 1): meet(mine, "core", 1), (1, 1): meet(pair, "core", 1)})
+    direct, swapped = ((0, 0), (1, 0)), ((0, 1), (1, 1))
+    answer = meet(attend(asked, swapped, attend(asked, direct, times=10)), "y", 1)
+    own_part = attend(arrived_later, direct[1:] + swapped, first)
     merged = pl.pallas_call(
         merge_kernel,
         out_shape=shape((pools * (CAP * heads + GROUP), hdim), BF16),

time: 111 us -> 112 us (level)
  starting transfers between devices: 36.3 us -> 33.7 us
  blocking collectives: 43.2 us -> 45.5 us
  waiting for transfers between devices: 8.24 us -> 9.67 us
    all_to_all x1, blocking collectives: 25.8 us -> 27.3 us  [body(): lax.all_to_all(outgoing.reshape(pools, CAP, heads, hdim), 'pool', split_a...]
    ppermute x6, waiting for transfers between devices: 2.16 us -> 3.59 us  [meet(): return lax.ppermute(value, axis, pairs)]
    all_to_all x1, starting transfers between devices: 6.01 us -> 4.71 us  [body(): lax.all_to_all(merged.reshape(pools, CAP * heads + GROUP, hdim), 'pool',...]
    ppermute x6, starting transfers between devices: 30.3 us -> 29 us  [meet(): return lax.ppermute(value, axis, pairs)]
where the time goes in v7:
time: 112 us
  blocking collectives  45.5 us (41%)
  starting transfers between devices  33.7 us (30%)
  Pallas kernels  18.5 us (17%)
  waiting for transfers between devices  9.67 us (9%)
  local copies, waits for them, and re-layouts  3.32 us (3%)
    ppermute x6, starting transfers between devices, meet(): return lax.ppermute(value, axis, pairs)  29 us
    all_to_all x1, blocking collectives, body(): lax.all_to_all(outgoing.reshape(pools, CAP, heads, hdim), 'pool', split_a...  27.3 us
    all_to_all x1, blocking collectives, body(): lax.all_to_all(attended, 'y', split_axis=0, concat_axis=0, tiled=True)  9.37 us
    pallas_call x4, Pallas kernels, attend(): pl.pallas_call(functools.partial(attend_kernel, merging), out_shape=shape...  9.11 us
    all_to_all x1, blocking collectives, body(): lax.all_to_all(terms.reshape(lax.axis_size('head'), -1, columns), 'head',...  8.81 us
    all_to_all x1, waiting for transfers between devices, body(): lax.all_to_all(merged.reshape(pools, CAP * heads + GROUP, hdim), 'pool',...  6.08 us
    all_to_all x1, starting transfers between devices, body(): lax.all_to_all(merged.reshape(pools, CAP * heads + GROUP, hdim), 'pool',...  4.71 us
    pallas_call x1, Pallas kernels, body(): pl.pallas_call(suffix_kernel, out_shape=shape((rows, 2 * heads, hdim), F3...  4.41 us
  transfers between devices with their start and end apart: 7, of which 4 were waited for; matrix products, arithmetic and copies ran while one was open for 0% of the time, Pallas kernels for 10%

profile of v7, /device:TPU:1, one launch (start us, length us, event | category | flops | bytes accessed | tf_op | source)
XLA Modules:
  0.0 111.5 jit_solution(11652759030835781168)
XLA Ops:
  0.0 2.4 %dispatch.1 = (bf16[48,16,128]{2,1,0:T(8,128)(2,1)}, bf16[4112,128]{1,0:T(8,128)(2,1)}) custom-call(s32[16]{0:T(128)} %bitcast.17, s32[16]{0:T(128)} %owner_hbm.3, s32[16]{0:T(128)} %lengths_hbm.1, bf16[16,16,128]{2,1,0:T(8,128)(2,1)} %q_ref, bf16[2048,128]{1,0:T(8,128)(2,1)} %bitcast.19, bf16[2048,128]{1,0:T(8,128)(2,1)} %bitcast.20), custom_call_target="tpu_custom_call" | custom-call | bytes 3000000 | tf_op jit(solution)/shard_map/dispatch/pallas_call | solution.py:321
  2.4 5.5 %collective-permute-start = (bf16[4112,128]{1,0:T(8,128)(2,1)}, bf16[4112,128]{1,0:T(8,128)(2,1)S(1)}, u32[]{:S(2)}, u32[]{:S(2)}) collective-permute-start(bf16[4112,128]{1,0:T(8,128)(2,1)} %get-tuple-element.19.refs_0_), channel_id=1, source_target_pairs={{0,24},{8,16},{16,8},{24,0},{1,25},{9,17},{17,9},{25,1},{2,26},{10... | collective-permute-start | bytes 3158024 | tf_op jit(solution)/shard_map/ppermute | solution.py:315
  7.9 27.3 %all_to_all.20 = bf16[16,3,16,128]{3,2,1,0:T(8,128)(2,1)S(1)} all-to-all(bf16[16,3,16,128]{3,2,1,0:T(8,128)(2,1)} %bitcast.21), channel_id=1, replica_groups=mesh['pool'=16,'y'=4,'core'=2,'head'=4] {'pool'}, dimensions={0} | all-to-all | bytes 393216 | tf_op jit(solution)/shard_map/all_to_all | solution.py:348
  35.2 1.9 %collective-permute-start.3 = (bf16[48,16,128]{2,1,0:T(8,128)(2,1)S(1)}, bf16[48,16,128]{2,1,0:T(8,128)(2,1)S(1)}, u32[]{:S(2)}, u32[]{:S(2)}) collective-permute-start(bf16[48,16,128]{2,1,0:T(8,128)(2,1)S(1)} %bitcast.14), channel_id=1, source_target_pairs={{0,8},{8,0},{16,24},{24,16},{1,9},{9,1},{17,25},{25,17},{2,10},{10... | collective-permute-start | bytes 589832 | tf_op jit(solution)/shard_map/ppermute | solution.py:315
  37.1 0.0 collective-permute-done.refs_1_
  37.1 0.0 copy-start.7
  37.1 1.2 %copy-done.7 = bf16[4112,128]{1,0:T(8,128)(2,1)S(1)} copy-done((bf16[4112,128]{1,0:T(8,128)(2,1)S(1)}, bf16[4112,128]{1,0:T(8,128)(2,1)}, u32[]{:S(2)}) %copy-start.7) | copy-done | bytes 1052696
  38.3 1.2 %attend.4.refs_0_ = bf16[51,16,128]{2,1,0:T(8,128)(2,1)S(1)} custom-call(bf16[48,16,128]{2,1,0:T(8,128)(2,1)S(1)} %bitcast.15, bf16[4112,128]{1,0:T(8,128)(2,1)S(1)} %copy-done.7), custom_call_target="tpu_custom_call" | custom-call | flops 603979776 | bytes 3000000 | tf_op jit(solution)/shard_map/attend/pallas_call | solution.py:359
  39.5 7.1 %collective-permute-start.1 = (bf16[4112,128]{1,0:T(8,128)(2,1)S(1)}, bf16[4112,128]{1,0:T(8,128)(2,1)S(1)}, u32[]{:S(2)}, u32[]{:S(2)}) collective-permute-start(bf16[4112,128]{1,0:T(8,128)(2,1)S(1)} %copy-done.7), channel_id=1, source_target_pairs={{0,4},{4,0},{1,5},{5,1},{2,6},{6,2},{3,7},{7,3},{8,12},{12,8},{9,1... | collective-permute-start | bytes 3158024 | tf_op jit(solution)/shard_map/ppermute | solution.py:315
  46.7 1.9 %collective-permute-start.2 = (bf16[4112,128]{1,0:T(8,128)(2,1)S(1)}, bf16[4112,128]{1,0:T(8,128)(2,1)S(1)}, u32[]{:S(2)}, u32[]{:S(2)}) collective-permute-start(bf16[4112,128]{1,0:T(8,128)(2,1)S(1)} %collective-permute-done.refs_1_), channel_id=1, source_target_pairs={{0,4},{4,0},{1,5},{5,1},{2,6},{6,2},{3,7},{7,3},{8,12},{12,8},{9,1... | collective-permute-start | bytes 3158024 | tf_op jit(solution)/shard_map/ppermute | solution.py:315
  48.6 0.0 collective-permute-done.3.q_ref
  48.6 2.1 %attend.6.refs_0_ = bf16[51,16,128]{2,1,0:T(8,128)(2,1)S(1)} custom-call(bf16[48,16,128]{2,1,0:T(8,128)(2,1)S(1)} %collective-permute-done.3.q_ref, bf16[4112,128]{1,0:T(8,128)(2,1)S(1)} %copy-done.7, bf16[4112,128]{1,0:T(8,128)(2,1)S(1)} %collective-permute-done.refs_1_), custom_call_target="tpu_custom_call" | custom-call | flops 12079595520 | bytes 3000000 | tf_op jit(solution)/shard_map/attend/pallas_call | solution.py:359
  50.7 0.0 collective-permute-done.1.refs_2_.refs_1_
  50.7 0.5 collective-permute-done.2.refs_3_.refs_2_
  51.2 2.5 %attend.7 = bf16[51,16,128]{2,1,0:T(8,128)(2,1)S(1)} custom-call(bf16[48,16,128]{2,1,0:T(8,128)(2,1)S(1)} %collective-permute-done.3.q_ref, bf16[51,16,128]{2,1,0:T(8,128)(2,1)S(1)} %attend.6.refs_0_, bf16[4112,128]{1,0:T(8,128)(2,1)S(1)} %collective-permute-done.1.refs_2_.refs_1_, bf16[4112,128]{1,0:T(8,128)(2,1)S(1)} %collective-permute-done.2.refs_3_.refs_2_), custom_call_target="tpu_custom_call" | custom-call | flops 1207959552 | bytes 3000000 | tf_op jit(solution)/shard_map/attend/pallas_call | solution.py:359
  53.7 3.5 %collective-permute-start.4 = (bf16[51,16,128]{2,1,0:T(8,128)(2,1)S(1)}, bf16[51,16,128]{2,1,0:T(8,128)(2,1)S(1)}, u32[]{:S(2)}, u32[]{:S(2)}) collective-permute-start(bf16[51,16,128]{2,1,0:T(8,128)(2,1)S(1)} %attend.7), channel_id=1, source_target_pairs={{0,8},{8,0},{16,24},{24,16},{1,9},{9,1},{17,25},{25,17},{2,10},{10... | collective-permute-start | bytes 626696 | tf_op jit(solution)/shard_map/ppermute | solution.py:315
  57.2 3.3 %attend.5.a_ref = bf16[51,16,128]{2,1,0:T(8,128)(2,1)S(1)} custom-call(bf16[48,16,128]{2,1,0:T(8,128)(2,1)S(1)} %bitcast.16, bf16[51,16,128]{2,1,0:T(8,128)(2,1)S(1)} %attend.4.refs_0_, bf16[4112,128]{1,0:T(8,128)(2,1)S(1)} %collective-permute-done.refs_1_, bf16[4112,128]{1,0:T(8,128)(2,1)S(1)} %collective-permute-done.1.refs_2_.refs_1_, ...), custom_call_target="tpu_custom_call" | custom-call | flops 1811939328 | bytes 3000000 | tf_op jit(solution)/shard_map/attend/pallas_call | solution.py:359
  60.5 0.0 copy-start.3
  60.6 0.0 copy-start.6
  60.6 2.0 %collective-permute-done.4.b_ref = bf16[51,16,128]{2,1,0:T(8,128)(2,1)S(1)} collective-permute-done((bf16[51,16,128]{2,1,0:T(8,128)(2,1)S(1)}, bf16[51,16,128]{2,1,0:T(8,128)(2,1)S(1)}, u32[]{:S(2)}, u32[]{:S(2)}) %collective-permute-start.4) | collective-permute-done | bytes 208928 | tf_op jit(solution)/shard_map/ppermute | solution.py:315
  62.5 1.2 %merge.1 = bf16[896,128]{1,0:T(8,128)(2,1)} custom-call(bf16[51,16,128]{2,1,0:T(8,128)(2,1)S(1)} %attend.5.a_ref, bf16[51,16,128]{2,1,0:T(8,128)(2,1)S(1)} %collective-permute-done.4.b_ref), custom_call_target="tpu_custom_call" | custom-call | bytes 1000000 | tf_op jit(solution)/shard_map/merge/pallas_call | solution.py:379
  63.7 0.0 copy-start.4
  63.7 0.0 copy-start.5
  63.7 4.7 %all-to-all-start.1 = ((bf16[16,56,128]{2,1,0:T(8,128)(2,1)}), bf16[16,56,128]{2,1,0:T(8,128)(2,1)S(1)}, u32[]{:S(2)}, u32[]{:S(2)}) async-start(bf16[16,56,128]{2,1,0:T(8,128)(2,1)} %bitcast.5), calls=%async_computation.1 | async-start | bytes 458752 | tf_op jit(solution)/shard_map/all_to_all | solution.py:389
  68.4 0.0 copy-done.3
  68.4 0.0 copy-done.6
  68.4 0.0 copy-start.1
  68.4 1.0 copy-done.1
  69.5 0.0 copy-start.2
  69.5 1.0 copy-done.2
  70.5 0.0 copy-start
  70.5 4.4 %suffix.1.suffix_hbm = f32[16,32,128]{2,1,0:T(8,128)S(1)} custom-call(s32[16]{0:T(128)S(1)} %copy-done.6, bf16[16,16,128]{2,1,0:T(8,128)(2,1)S(1)} %copy-done.3, bf16[16,128,128]{2,1,0:T(8,128)(2,1)S(1)} %bitcast.12, bf16[16,128,128]{2,1,0:T(8,128)(2,1)S(1)} %bitcast.13), custom_call_target="tpu_custom_call" | custom-call | flops 16777216 | bytes 2000000 | tf_op jit(solution)/shard_map/suffix/pallas_call | solution.py:397
  74.9 6.1 %all-to-all-done.1 = bf16[16,56,128]{2,1,0:T(8,128)(2,1)S(1)} async-done(((bf16[16,56,128]{2,1,0:T(8,128)(2,1)}), bf16[16,56,128]{2,1,0:T(8,128)(2,1)S(1)}, u32[]{:S(2)}, u32[]{:S(2)}) %all-to-all-start.1) | async-done | bytes 229408 | tf_op jit(solution)/shard_map/all_to_all | solution.py:389
  81.0 0.0 copy-done.4
  81.0 0.0 copy-done.5
  81.0 0.9 combine.1
  81.9 9.4 %all_to_all.21.own_ref = bf16[4,16,2048]{2,1,0:T(8,128)(2,1)S(1)} all-to-all(bf16[4,16,2048]{2,1,0:T(8,128)(2,1)S(1)} %combine.1), channel_id=1, replica_groups=mesh['pool'=16,'y'=4,'core'=2,'head'=4] {'y'}, dimensions={0} | all-to-all | bytes 524288 | tf_op jit(solution)/shard_map/all_to_all | solution.py:433
  91.3 9.1 %collective-permute-start.5 = (bf16[4,16,2048]{2,1,0:T(8,128)(2,1)S(1)}, bf16[4,16,2048]{2,1,0:T(8,128)(2,1)S(1)}, u32[]{:S(2)}, u32[]{:S(2)}) collective-permute-start(bf16[4,16,2048]{2,1,0:T(8,128)(2,1)S(1)} %all_to_all.21.own_ref), channel_id=1, source_target_pairs={{0,4},{4,0},{1,5},{5,1},{2,6},{6,2},{3,7},{7,3},{8,12},{12,8},{9,1... | collective-permute-start | bytes 786440 | tf_op jit(solution)/shard_map/ppermute | solution.py:315
  100.3 1.1 %collective-permute-done.5.other_ref = bf16[4,16,2048]{2,1,0:T(8,128)(2,1)S(1)} collective-permute-done((bf16[4,16,2048]{2,1,0:T(8,128)(2,1)S(1)}, bf16[4,16,2048]{2,1,0:T(8,128)(2,1)S(1)}, u32[]{:S(2)}, u32[]{:S(2)}) %collective-permute-start.5) | collective-permute-done | bytes 262176 | tf_op jit(solution)/shard_map/ppermute | solution.py:315
  101.5 0.0 copy-done
  101.5 0.6 project.1
  102.1 8.8 %all_to_all.22 = bf16[4,32,640]{2,1,0:T(8,128)(2,1)S(1)} all-to-all(bf16[4,32,640]{2,1,0:T(8,128)(2,1)S(1)} %bitcast.11), channel_id=1, replica_groups=mesh['pool'=16,'y'=4,'core'=2,'head'=4] {'head'}, dimensions={0} | all-to-all | bytes 327680 | tf_op jit(solution)/shard_map/all_to_all | solution.py:447
  110.9 0.6 reduce_sum.12
Async XLA Ops:
  2.4 34.7 %collective-permute-start = (bf16[4112,128]{1,0:T(8,128)(2,1)}, bf16[4112,128]{1,0:T(8,128)(2,1)S(1)}, u32[]{:S(2)}, u32[]{:S(2)}) collective-permute-start(bf16[4112,128]{1,0:T(8,128)(2,1)} %get-tuple-element.19.refs_0_), channel_id=1, source_target_pairs={{0,24},{8,16},{16,8},{24,0},{1,25},{9,17},{17,9},{25,1},{2,26},{10... | collective-permute-start | bytes 3158024 | tf_op jit(solution)/shard_map/ppermute | solution.py:315
  35.2 13.4 %collective-permute-start.3 = (bf16[48,16,128]{2,1,0:T(8,128)(2,1)S(1)}, bf16[48,16,128]{2,1,0:T(8,128)(2,1)S(1)}, u32[]{:S(2)}, u32[]{:S(2)}) collective-permute-start(bf16[48,16,128]{2,1,0:T(8,128)(2,1)S(1)} %bitcast.14), channel_id=1, source_target_pairs={{0,8},{8,0},{16,24},{24,16},{1,9},{9,1},{17,25},{25,17},{2,10},{10... | collective-permute-start | bytes 589832 | tf_op jit(solution)/shard_map/ppermute | solution.py:315
  37.1 1.2 %copy-start.7 = (bf16[4112,128]{1,0:T(8,128)(2,1)S(1)}, bf16[4112,128]{1,0:T(8,128)(2,1)}, u32[]{:S(2)}) copy-start(bf16[4112,128]{1,0:T(8,128)(2,1)} %get-tuple-element.19.refs_0_) | copy-start | bytes 3158020
  39.5 11.2 %collective-permute-start.1 = (bf16[4112,128]{1,0:T(8,128)(2,1)S(1)}, bf16[4112,128]{1,0:T(8,128)(2,1)S(1)}, u32[]{:S(2)}, u32[]{:S(2)}) collective-permute-start(bf16[4112,128]{1,0:T(8,128)(2,1)S(1)} %copy-done.7), channel_id=1, source_target_pairs={{0,4},{4,0},{1,5},{5,1},{2,6},{6,2},{3,7},{7,3},{8,12},{12,8},{9,1... | collective-permute-start | bytes 3158024 | tf_op jit(solution)/shard_map/ppermute | solution.py:315
  46.7 4.6 %collective-permute-start.2 = (bf16[4112,128]{1,0:T(8,128)(2,1)S(1)}, bf16[4112,128]{1,0:T(8,128)(2,1)S(1)}, u32[]{:S(2)}, u32[]{:S(2)}) collective-permute-start(bf16[4112,128]{1,0:T(8,128)(2,1)S(1)} %collective-permute-done.refs_1_), channel_id=1, source_target_pairs={{0,4},{4,0},{1,5},{5,1},{2,6},{6,2},{3,7},{7,3},{8,12},{12,8},{9,1... | collective-permute-start | bytes 3158024 | tf_op jit(solution)/shard_map/ppermute | solution.py:315
  53.7 8.8 %collective-permute-start.4 = (bf16[51,16,128]{2,1,0:T(8,128)(2,1)S(1)}, bf16[51,16,128]{2,1,0:T(8,128)(2,1)S(1)}, u32[]{:S(2)}, u32[]{:S(2)}) collective-permute-start(bf16[51,16,128]{2,1,0:T(8,128)(2,1)S(1)} %attend.7), channel_id=1, source_target_pairs={{0,8},{8,0},{16,24},{24,16},{1,9},{9,1},{17,25},{25,17},{2,10},{10... | collective-permute-start | bytes 626696 | tf_op jit(solution)/shard_map/ppermute | solution.py:315
  60.5 7.9 %copy-start.3 = (bf16[16,16,128]{2,1,0:T(8,128)(2,1)S(1)}, bf16[16,16,128]{2,1,0:T(8,128)(2,1)}, u32[]{:S(2)}) copy-start(bf16[16,16,128]{2,1,0:T(8,128)(2,1)} %q_ref) | copy-start | bytes 196612
  60.6 7.9 %copy-start.6 = (s32[16]{0:T(128)S(1)}, s32[16]{0:T(128)}, u32[]{:S(2)}) copy-start(s32[16]{0:T(128)} %length_hbm.1) | copy-start | bytes 196
  63.7 17.3 %copy-start.4 = (s32[16,1]{0,1:T(1,128)S(1)}, s32[16,1]{0,1:T(1,128)}, u32[]{:S(2)}) copy-start(s32[16,1]{0,1:T(1,128)} %param.15) | copy-start | bytes 196
  63.7 17.3 %copy-start.5 = (s32[16]{0:T(128)S(1)}, s32[16]{0:T(128)}, u32[]{:S(2)}) copy-start(s32[16]{0:T(128)} %owner_hbm.3) | copy-start | bytes 196
  63.7 17.3 %all-to-all-start.1 = ((bf16[16,56,128]{2,1,0:T(8,128)(2,1)}), bf16[16,56,128]{2,1,0:T(8,128)(2,1)S(1)}, u32[]{:S(2)}, u32[]{:S(2)}) async-start(bf16[16,56,128]{2,1,0:T(8,128)(2,1)} %bitcast.5), calls=%async_computation.1 | async-start | bytes 458752 | tf_op jit(solution)/shard_map/all_to_all | solution.py:389
  68.4 1.0 copy-start.1
  69.5 1.0 copy-start.2
  70.5 30.9 %copy-start = (bf16[2048,640]{1,0:T(8,128)(2,1)S(1)}, bf16[2048,640]{1,0:T(8,128)(2,1)}, u32[]{:S(2)}) copy-start(bf16[2048,640]{1,0:T(8,128)(2,1)} %w_ref.1) | copy-start | bytes 7864324
  91.3 10.2 %collective-permute-start.5 = (bf16[4,16,2048]{2,1,0:T(8,128)(2,1)S(1)}, bf16[4,16,2048]{2,1,0:T(8,128)(2,1)S(1)}, u32[]{:S(2)}, u32[]{:S(2)}) collective-permute-start(bf16[4,16,2048]{2,1,0:T(8,128)(2,1)S(1)} %all_to_all.21.own_ref), channel_id=1, source_target_pairs={{0,4},{4,0},{1,5},{5,1},{2,6},{6,2},{3,7},{7,3},{8,12},{12,8},{9,1... | collective-permute-start | bytes 786440 | tf_op jit(solution)/shard_map/ppermute | solution.py:315

commit v8 on v7

--- a/solution.py
+++ b/solution.py
@@ -370,12 +370,10 @@
             name="attend",
         )(q, *([earlier] if merging else []), *(blocks[source] for source in sources))
 
-    first = attend(arrived_later, [(0, 0)])
-    mine, pair, first = lax.optimization_barrier((own, pair, first))
-    blocks.update({(0, 1): meet(mine, "core", 1), (1, 1): meet(pair, "core", 1)})
-    direct, swapped = ((0, 0), (1, 0)), ((0, 1), (1, 1))
-    answer = meet(attend(asked, swapped, attend(asked, direct, times=10)), "y", 1)
-    own_part = attend(arrived_later, direct[1:] + swapped, first)
+    blocks.update({(0, 1): meet(own, "core", 1), (1, 1): meet(pair, "core", 1)})
+    others = ((0, 0), (0, 1), (1, 1))
+    answer = meet(attend(asked, others, attend(asked, [(1, 0)], times=20)), "y", 1)
+    own_part = attend(arrived_later, ((1, 0),) + others)
     merged = pl.pallas_call(
         merge_kernel,
         out_shape=shape((pools * (CAP * heads + GROUP), hdim), BF16),

time: 112 us -> 109 us (0.973)
  blocking collectives: 45.5 us -> 44.1 us
  local copies, waits for them, and re-layouts: 3.32 us -> 2.11 us
    all_to_all x1, blocking collectives: 9.37 us -> 8.04 us  [body(): lax.all_to_all(attended, 'y', split_axis=0, concat_axis=0, tiled=True)]
    unnamed x16, local copies, waits for them, and re-layouts: 3.32 us -> 2.11 us
    pallas_call x4 -> x3, Pallas kernels: 9.11 us -> 9.11 us  [attend(): pl.pallas_call(functools.partial(attend_kernel, merging), out_shape=shape...]
  transfers between devices with their start and end apart: 7 -> 7, of which waited for: 4 -> 4; matrix products, arithmetic and copies ran while one was open for 0% -> 0% of each run, Pallas kernels for 10% -> 9%
where the time goes in v8:
time: 109 us
  blocking collectives  44.1 us (40%)
  starting transfers between devices  33.9 us (31%)
  Pallas kernels  18.5 us (17%)
  waiting for transfers between devices  9.24 us (8%)
  local copies, waits for them, and re-layouts  2.11 us (2%)
    ppermute x6, starting transfers between devices, meet(): return lax.ppermute(value, axis, pairs)  29.2 us
    all_to_all x1, blocking collectives, body(): lax.all_to_all(outgoing.reshape(pools, CAP, heads, hdim), 'pool', split_a...  27.3 us
    pallas_call x3, Pallas kernels, attend(): pl.pallas_call(functools.partial(attend_kernel, merging), out_shape=shape...  9.11 us
    all_to_all x1, blocking collectives, body(): lax.all_to_all(terms.reshape(lax.axis_size('head'), -1, columns), 'head',...  8.82 us
    all_to_all x1, blocking collectives, body(): lax.all_to_all(attended, 'y', split_axis=0, concat_axis=0, tiled=True)  8.04 us
    all_to_all x1, waiting for transfers between devices, body(): lax.all_to_all(merged.reshape(pools, CAP * heads + GROUP, hdim), 'pool',...  6.08 us
    all_to_all x1, starting transfers between devices, body(): lax.all_to_all(merged.reshape(pools, CAP * heads + GROUP, hdim), 'pool',...  4.69 us
    pallas_call x1, Pallas kernels, body(): pl.pallas_call(suffix_kernel, out_shape=shape((rows, 2 * heads, hdim), F3...  4.41 us
  transfers between devices with their start and end apart: 7, of which 4 were waited for; matrix products, arithmetic and copies ran while one was open for 0% of the time, Pallas kernels for 9%

profile of v8, /device:TPU:1, one launch (start us, length us, event | category | flops | bytes accessed | tf_op | source)
XLA Modules:
  0.0 108.8 jit_solution(11477028499695498589)
XLA Ops:
  0.0 2.4 %dispatch.1 = (bf16[48,16,128]{2,1,0:T(8,128)(2,1)}, bf16[4112,128]{1,0:T(8,128)(2,1)}) custom-call(s32[16]{0:T(128)} %bitcast.16, s32[16]{0:T(128)} %owner_hbm.3, s32[16]{0:T(128)} %lengths_hbm.1, bf16[16,16,128]{2,1,0:T(8,128)(2,1)} %q_ref, bf16[2048,128]{1,0:T(8,128)(2,1)} %bitcast.18, bf16[2048,128]{1,0:T(8,128)(2,1)} %bitcast.19), custom_call_target="tpu_custom_call" | custom-call | bytes 3000000 | tf_op jit(solution)/shard_map/dispatch/pallas_call | solution.py:321
  2.4 5.5 %collective-permute-start = (bf16[4112,128]{1,0:T(8,128)(2,1)}, bf16[4112,128]{1,0:T(8,128)(2,1)S(1)}, u32[]{:S(2)}, u32[]{:S(2)}) collective-permute-start(bf16[4112,128]{1,0:T(8,128)(2,1)} %get-tuple-element.11.refs_1_), channel_id=1, source_target_pairs={{0,24},{8,16},{16,8},{24,0},{1,25},{9,17},{17,9},{25,1},{2,26},{10... | collective-permute-start | bytes 3158024 | tf_op jit(solution)/shard_map/ppermute | solution.py:315
  7.9 27.3 %all_to_all.20 = bf16[16,3,16,128]{3,2,1,0:T(8,128)(2,1)S(1)} all-to-all(bf16[16,3,16,128]{3,2,1,0:T(8,128)(2,1)} %bitcast.20), channel_id=1, replica_groups=mesh['pool'=16,'y'=4,'core'=2,'head'=4] {'pool'}, dimensions={0} | all-to-all | bytes 393216 | tf_op jit(solution)/shard_map/all_to_all | solution.py:348
  35.2 0.0 copy-start.7
  35.2 2.0 %collective-permute-start.3 = (bf16[48,16,128]{2,1,0:T(8,128)(2,1)S(1)}, bf16[48,16,128]{2,1,0:T(8,128)(2,1)S(1)}, u32[]{:S(2)}, u32[]{:S(2)}) collective-permute-start(bf16[48,16,128]{2,1,0:T(8,128)(2,1)S(1)} %bitcast.14), channel_id=1, source_target_pairs={{0,8},{8,0},{16,24},{24,16},{1,9},{9,1},{17,25},{25,17},{2,10},{10... | collective-permute-start | bytes 589832 | tf_op jit(solution)/shard_map/ppermute | solution.py:315
  37.2 7.1 %collective-permute-start.1 = (bf16[4112,128]{1,0:T(8,128)(2,1)}, bf16[4112,128]{1,0:T(8,128)(2,1)S(1)}, u32[]{:S(2)}, u32[]{:S(2)}) collective-permute-start(bf16[4112,128]{1,0:T(8,128)(2,1)} %get-tuple-element.11.refs_1_), channel_id=1, source_target_pairs={{0,4},{4,0},{1,5},{5,1},{2,6},{6,2},{3,7},{7,3},{8,12},{12,8},{9,1... | collective-permute-start | bytes 3158024 | tf_op jit(solution)/shard_map/ppermute | solution.py:315
  44.4 0.0 collective-permute-done.refs_0_
  44.4 1.9 %collective-permute-start.2 = (bf16[4112,128]{1,0:T(8,128)(2,1)S(1)}, bf16[4112,128]{1,0:T(8,128)(2,1)S(1)}, u32[]{:S(2)}, u32[]{:S(2)}) collective-permute-start(bf16[4112,128]{1,0:T(8,128)(2,1)S(1)} %collective-permute-done.refs_0_), channel_id=1, source_target_pairs={{0,4},{4,0},{1,5},{5,1},{2,6},{6,2},{3,7},{7,3},{8,12},{12,8},{9,1... | collective-permute-start | bytes 3158024 | tf_op jit(solution)/shard_map/ppermute | solution.py:315
  46.3 0.0 collective-permute-done.3.q_ref
  46.3 1.2 %attend.4.refs_0_ = bf16[51,16,128]{2,1,0:T(8,128)(2,1)S(1)} custom-call(bf16[48,16,128]{2,1,0:T(8,128)(2,1)S(1)} %collective-permute-done.3.q_ref, bf16[4112,128]{1,0:T(8,128)(2,1)S(1)} %collective-permute-done.refs_0_), custom_call_target="tpu_custom_call" | custom-call | flops 12079595520 | bytes 3000000 | tf_op jit(solution)/shard_map/attend/pallas_call | solution.py:359
  47.5 0.0 collective-permute-done.1.refs_2_
  47.5 1.4 %collective-permute-done.2.refs_3_ = bf16[4112,128]{1,0:T(8,128)(2,1)S(1)} collective-permute-done((bf16[4112,128]{1,0:T(8,128)(2,1)S(1)}, bf16[4112,128]{1,0:T(8,128)(2,1)S(1)}, u32[]{:S(2)}, u32[]{:S(2)}) %collective-permute-start.2) | collective-permute-done | bytes 1052704 | tf_op jit(solution)/shard_map/ppermute | solution.py:315
  48.9 0.0 copy-done.7
  48.9 3.4 %attend.5 = bf16[51,16,128]{2,1,0:T(8,128)(2,1)S(1)} custom-call(bf16[48,16,128]{2,1,0:T(8,128)(2,1)S(1)} %collective-permute-done.3.q_ref, bf16[51,16,128]{2,1,0:T(8,128)(2,1)S(1)} %attend.4.refs_0_, bf16[4112,128]{1,0:T(8,128)(2,1)S(1)} %copy-done.7, bf16[4112,128]{1,0:T(8,128)(2,1)S(1)} %collective-permute-done.1.refs_2_, ...), custom_call_target="tpu_custom_call" | custom-call | flops 1811939328 | bytes 3000000 | tf_op jit(solution)/shard_map/attend/pallas_call | solution.py:359
  52.3 3.5 %collective-permute-start.4 = (bf16[51,16,128]{2,1,0:T(8,128)(2,1)S(1)}, bf16[51,16,128]{2,1,0:T(8,128)(2,1)S(1)}, u32[]{:S(2)}, u32[]{:S(2)}) collective-permute-start(bf16[51,16,128]{2,1,0:T(8,128)(2,1)S(1)} %attend.5), channel_id=1, source_target_pairs={{0,8},{8,0},{16,24},{24,16},{1,9},{9,1},{17,25},{25,17},{2,10},{10... | collective-permute-start | bytes 626696 | tf_op jit(solution)/shard_map/ppermute | solution.py:315
  55.8 4.5 %attend.3.a_ref = bf16[51,16,128]{2,1,0:T(8,128)(2,1)S(1)} custom-call(bf16[48,16,128]{2,1,0:T(8,128)(2,1)S(1)} %bitcast.15, bf16[4112,128]{1,0:T(8,128)(2,1)S(1)} %collective-permute-done.refs_0_, bf16[4112,128]{1,0:T(8,128)(2,1)S(1)} %copy-done.7, bf16[4112,128]{1,0:T(8,128)(2,1)S(1)} %collective-permute-done.1.refs_2_, ...), custom_call_target="tpu_custom_call" | custom-call | flops 2415919104 | bytes 3000000 | tf_op jit(solution)/shard_map/attend/pallas_call | solution.py:359
  60.3 0.0 copy-start.3
  60.3 0.0 copy-start.6
  60.4 0.6 collective-permute-done.4.b_ref
  61.0 1.2 %merge.1 = bf16[896,128]{1,0:T(8,128)(2,1)} custom-call(bf16[51,16,128]{2,1,0:T(8,128)(2,1)S(1)} %attend.3.a_ref, bf16[51,16,128]{2,1,0:T(8,128)(2,1)S(1)} %collective-permute-done.4.b_ref), custom_call_target="tpu_custom_call" | custom-call | bytes 1000000 | tf_op jit(solution)/shard_map/merge/pallas_call | solution.py:377
  62.2 0.0 copy-start.4
  62.2 0.0 copy-start.5
  62.2 4.7 %all-to-all-start.1 = ((bf16[16,56,128]{2,1,0:T(8,128)(2,1)}), bf16[16,56,128]{2,1,0:T(8,128)(2,1)S(1)}, u32[]{:S(2)}, u32[]{:S(2)}) async-start(bf16[16,56,128]{2,1,0:T(8,128)(2,1)} %bitcast.5), calls=%async_computation.1 | async-start | bytes 458752 | tf_op jit(solution)/shard_map/all_to_all | solution.py:387
  66.9 0.0 copy-done.3
  66.9 0.0 copy-done.6
  66.9 0.0 copy-start.1
  66.9 1.0 copy-done.1
  67.9 0.0 copy-start.2
  67.9 1.0 copy-done.2
  69.0 0.0 copy-start
  69.0 4.4 %suffix.1.suffix_hbm = f32[16,32,128]{2,1,0:T(8,128)S(1)} custom-call(s32[16]{0:T(128)S(1)} %copy-done.6, bf16[16,16,128]{2,1,0:T(8,128)(2,1)S(1)} %copy-done.3, bf16[16,128,128]{2,1,0:T(8,128)(2,1)S(1)} %bitcast.12, bf16[16,128,128]{2,1,0:T(8,128)(2,1)S(1)} %bitcast.13), custom_call_target="tpu_custom_call" | custom-call | flops 16777216 | bytes 2000000 | tf_op jit(solution)/shard_map/suffix/pallas_call | solution.py:395
  73.4 6.1 %all-to-all-done.1 = bf16[16,56,128]{2,1,0:T(8,128)(2,1)S(1)} async-done(((bf16[16,56,128]{2,1,0:T(8,128)(2,1)}), bf16[16,56,128]{2,1,0:T(8,128)(2,1)S(1)}, u32[]{:S(2)}, u32[]{:S(2)}) %all-to-all-start.1) | async-done | bytes 229408 | tf_op jit(solution)/shard_map/all_to_all | solution.py:387
  79.5 0.0 copy-done.4
  79.5 0.0 copy-done.5
  79.5 0.9 combine.1
  80.3 8.0 %all_to_all.21.own_ref = bf16[4,16,2048]{2,1,0:T(8,128)(2,1)S(1)} all-to-all(bf16[4,16,2048]{2,1,0:T(8,128)(2,1)S(1)} %combine.1), channel_id=1, replica_groups=mesh['pool'=16,'y'=4,'core'=2,'head'=4] {'y'}, dimensions={0} | all-to-all | bytes 524288 | tf_op jit(solution)/shard_map/all_to_all | solution.py:431
  88.4 9.2 %collective-permute-start.5 = (bf16[4,16,2048]{2,1,0:T(8,128)(2,1)S(1)}, bf16[4,16,2048]{2,1,0:T(8,128)(2,1)S(1)}, u32[]{:S(2)}, u32[]{:S(2)}) collective-permute-start(bf16[4,16,2048]{2,1,0:T(8,128)(2,1)S(1)} %all_to_all.21.own_ref), channel_id=1, source_target_pairs={{0,4},{4,0},{1,5},{5,1},{2,6},{6,2},{3,7},{7,3},{8,12},{12,8},{9,1... | collective-permute-start | bytes 786440 | tf_op jit(solution)/shard_map/ppermute | solution.py:315
  97.6 1.1 %collective-permute-done.5.other_ref = bf16[4,16,2048]{2,1,0:T(8,128)(2,1)S(1)} collective-permute-done((bf16[4,16,2048]{2,1,0:T(8,128)(2,1)S(1)}, bf16[4,16,2048]{2,1,0:T(8,128)(2,1)S(1)}, u32[]{:S(2)}, u32[]{:S(2)}) %collective-permute-start.5) | collective-permute-done | bytes 262176 | tf_op jit(solution)/shard_map/ppermute | solution.py:315
  98.7 0.0 copy-done
  98.7 0.6 project.1
  99.3 8.8 %all_to_all.22 = bf16[4,32,640]{2,1,0:T(8,128)(2,1)S(1)} all-to-all(bf16[4,32,640]{2,1,0:T(8,128)(2,1)S(1)} %bitcast.11), channel_id=1, replica_groups=mesh['pool'=16,'y'=4,'core'=2,'head'=4] {'head'}, dimensions={0} | all-to-all | bytes 327680 | tf_op jit(solution)/shard_map/all_to_all | solution.py:445
  108.1 0.6 reduce_sum.12
Async XLA Ops:
  2.4 41.9 %collective-permute-start = (bf16[4112,128]{1,0:T(8,128)(2,1)}, bf16[4112,128]{1,0:T(8,128)(2,1)S(1)}, u32[]{:S(2)}, u32[]{:S(2)}) collective-permute-start(bf16[4112,128]{1,0:T(8,128)(2,1)} %get-tuple-element.11.refs_1_), channel_id=1, source_target_pairs={{0,24},{8,16},{16,8},{24,0},{1,25},{9,17},{17,9},{25,1},{2,26},{10... | collective-permute-start | bytes 3158024 | tf_op jit(solution)/shard_map/ppermute | solution.py:315
  35.2 13.7 %copy-start.7 = (bf16[4112,128]{1,0:T(8,128)(2,1)S(1)}, bf16[4112,128]{1,0:T(8,128)(2,1)}, u32[]{:S(2)}) copy-start(bf16[4112,128]{1,0:T(8,128)(2,1)} %get-tuple-element.11.refs_1_) | copy-start | bytes 3158020
  35.2 11.1 %collective-permute-start.3 = (bf16[48,16,128]{2,1,0:T(8,128)(2,1)S(1)}, bf16[48,16,128]{2,1,0:T(8,128)(2,1)S(1)}, u32[]{:S(2)}, u32[]{:S(2)}) collective-permute-start(bf16[48,16,128]{2,1,0:T(8,128)(2,1)S(1)} %bitcast.14), channel_id=1, source_target_pairs={{0,8},{8,0},{16,24},{24,16},{1,9},{9,1},{17,25},{25,17},{2,10},{10... | collective-permute-start | bytes 589832 | tf_op jit(solution)/shard_map/ppermute | solution.py:315
  37.2 10.3 %collective-permute-start.1 = (bf16[4112,128]{1,0:T(8,128)(2,1)}, bf16[4112,128]{1,0:T(8,128)(2,1)S(1)}, u32[]{:S(2)}, u32[]{:S(2)}) collective-permute-start(bf16[4112,128]{1,0:T(8,128)(2,1)} %get-tuple-element.11.refs_1_), channel_id=1, source_target_pairs={{0,4},{4,0},{1,5},{5,1},{2,6},{6,2},{3,7},{7,3},{8,12},{12,8},{9,1... | collective-permute-start | bytes 3158024 | tf_op jit(solution)/shard_map/ppermute | solution.py:315
  44.4 4.6 %collective-permute-start.2 = (bf16[4112,128]{1,0:T(8,128)(2,1)S(1)}, bf16[4112,128]{1,0:T(8,128)(2,1)S(1)}, u32[]{:S(2)}, u32[]{:S(2)}) collective-permute-start(bf16[4112,128]{1,0:T(8,128)(2,1)S(1)} %collective-permute-done.refs_0_), channel_id=1, source_target_pairs={{0,4},{4,0},{1,5},{5,1},{2,6},{6,2},{3,7},{7,3},{8,12},{12,8},{9,1... | collective-permute-start | bytes 3158024 | tf_op jit(solution)/shard_map/ppermute | solution.py:315
  52.3 8.7 %collective-permute-start.4 = (bf16[51,16,128]{2,1,0:T(8,128)(2,1)S(1)}, bf16[51,16,128]{2,1,0:T(8,128)(2,1)S(1)}, u32[]{:S(2)}, u32[]{:S(2)}) collective-permute-start(bf16[51,16,128]{2,1,0:T(8,128)(2,1)S(1)} %attend.5), channel_id=1, source_target_pairs={{0,8},{8,0},{16,24},{24,16},{1,9},{9,1},{17,25},{25,17},{2,10},{10... | collective-permute-start | bytes 626696 | tf_op jit(solution)/shard_map/ppermute | solution.py:315
  60.3 6.5 %copy-start.3 = (bf16[16,16,128]{2,1,0:T(8,128)(2,1)S(1)}, bf16[16,16,128]{2,1,0:T(8,128)(2,1)}, u32[]{:S(2)}) copy-start(bf16[16,16,128]{2,1,0:T(8,128)(2,1)} %q_ref) | copy-start | bytes 196612
  60.3 6.5 %copy-start.6 = (s32[16]{0:T(128)S(1)}, s32[16]{0:T(128)}, u32[]{:S(2)}) copy-start(s32[16]{0:T(128)} %length_hbm.1) | copy-start | bytes 196
  62.2 17.3 %copy-start.4 = (s32[16,1]{0,1:T(1,128)S(1)}, s32[16,1]{0,1:T(1,128)}, u32[]{:S(2)}) copy-start(s32[16,1]{0,1:T(1,128)} %param.15) | copy-start | bytes 196
  62.2 17.3 %copy-start.5 = (s32[16]{0:T(128)S(1)}, s32[16]{0:T(128)}, u32[]{:S(2)}) copy-start(s32[16]{0:T(128)} %owner_hbm.3) | copy-start | bytes 196
  62.2 17.3 %all-to-all-start.1 = ((bf16[16,56,128]{2,1,0:T(8,128)(2,1)}), bf16[16,56,128]{2,1,0:T(8,128)(2,1)S(1)}, u32[]{:S(2)}, u32[]{:S(2)}) async-start(bf16[16,56,128]{2,1,0:T(8,128)(2,1)} %bitcast.5), calls=%async_computation.1 | async-start | bytes 458752 | tf_op jit(solution)/shard_map/all_to_all | solution.py:387
  66.9 1.0 copy-start.1
  67.9 1.0 copy-start.2
  69.0 29.7 %copy-start = (bf16[2048,640]{1,0:T(8,128)(2,1)S(1)}, bf16[2048,640]{1,0:T(8,128)(2,1)}, u32[]{:S(2)}) copy-start(bf16[2048,640]{1,0:T(8,128)(2,1)} %w_ref.1) | copy-start | bytes 7864324
  88.4 10.3 %collective-permute-start.5 = (bf16[4,16,2048]{2,1,0:T(8,128)(2,1)S(1)}, bf16[4,16,2048]{2,1,0:T(8,128)(2,1)S(1)}, u32[]{:S(2)}, u32[]{:S(2)}) collective-permute-start(bf16[4,16,2048]{2,1,0:T(8,128)(2,1)S(1)} %all_to_all.21.own_ref), channel_id=1, source_target_pairs={{0,4},{4,0},{1,5},{5,1},{2,6},{6,2},{3,7},{7,3},{8,12},{12,8},{9,1... | collective-permute-start | bytes 786440 | tf_op jit(solution)/shard_map/ppermute | solution.py:315

commit v9 on v8

--- a/solution.py
+++ b/solution.py
@@ -98,7 +98,7 @@
     earlier_ref = refs[0] if merging else None
     blocks, out_ref = refs[int(merging) : -1], refs[-1]
     slots = q_ref.shape[0]
-    step_slots = math.gcd(24, slots)
+    step_slots = math.gcd(48, slots)
     length = (blocks[0].shape[0] - TAIL) // 4
     width = min(512, length)
     units = [(start, g) for start in range(0, slots, step_slots) for g in range(2)]

time: 109 us -> 109 us (level)
  no operation moved by 1% of the time
where the time goes in v9:
time: 109 us
  blocking collectives  44 us (40%)
  starting transfers between devices  33.8 us (31%)
  Pallas kernels  18.1 us (17%)
  waiting for transfers between devices  9.72 us (9%)
  local copies, waits for them, and re-layouts  2.11 us (2%)
    ppermute x6, starting transfers between devices, meet(): return lax.ppermute(value, axis, pairs)  29.2 us
    all_to_all x1, blocking collectives, body(): lax.all_to_all(outgoing.reshape(pools, CAP, heads, hdim), 'pool', split_a...  27.3 us
    all_to_all x1, blocking collectives, body(): lax.all_to_all(terms.reshape(lax.axis_size('head'), -1, columns), 'head',...  8.82 us
    pallas_call x3, Pallas kernels, attend(): pl.pallas_call(functools.partial(attend_kernel, merging), out_shape=shape...  8.73 us
    all_to_all x1, blocking collectives, body(): lax.all_to_all(attended, 'y', split_axis=0, concat_axis=0, tiled=True)  7.92 us
    all_to_all x1, waiting for transfers between devices, body(): lax.all_to_all(merged.reshape(pools, CAP * heads + GROUP, hdim), 'pool',...  6.23 us
    all_to_all x1, starting transfers between devices, body(): lax.all_to_all(merged.reshape(pools, CAP * heads + GROUP, hdim), 'pool',...  4.69 us
    pallas_call x1, Pallas kernels, body(): pl.pallas_call(suffix_kernel, out_shape=shape((rows, 2 * heads, hdim), F3...  4.41 us
  transfers between devices with their start and end apart: 7, of which 4 were waited for; matrix products, arithmetic and copies ran while one was open for 0% of the time, Pallas kernels for 9%

profile of v9, /device:TPU:1, one launch (start us, length us, event | category | flops | bytes accessed | tf_op | source)
XLA Modules:
  0.0 108.6 jit_solution(2758553778551282030)
XLA Ops:
  0.0 2.4 %dispatch.1 = (bf16[48,16,128]{2,1,0:T(8,128)(2,1)}, bf16[4112,128]{1,0:T(8,128)(2,1)}) custom-call(s32[16]{0:T(128)} %bitcast.16, s32[16]{0:T(128)} %owner_hbm.3, s32[16]{0:T(128)} %lengths_hbm.1, bf16[16,16,128]{2,1,0:T(8,128)(2,1)} %q_ref, bf16[2048,128]{1,0:T(8,128)(2,1)} %bitcast.18, bf16[2048,128]{1,0:T(8,128)(2,1)} %bitcast.19), custom_call_target="tpu_custom_call" | custom-call | bytes 3000000 | tf_op jit(solution)/shard_map/dispatch/pallas_call | solution.py:321
  2.4 5.5 %collective-permute-start = (bf16[4112,128]{1,0:T(8,128)(2,1)}, bf16[4112,128]{1,0:T(8,128)(2,1)S(1)}, u32[]{:S(2)}, u32[]{:S(2)}) collective-permute-start(bf16[4112,128]{1,0:T(8,128)(2,1)} %get-tuple-element.11.refs_1_), channel_id=1, source_target_pairs={{0,24},{8,16},{16,8},{24,0},{1,25},{9,17},{17,9},{25,1},{2,26},{10... | collective-permute-start | bytes 3158024 | tf_op jit(solution)/shard_map/ppermute | solution.py:315
  7.9 27.3 %all_to_all.20 = bf16[16,3,16,128]{3,2,1,0:T(8,128)(2,1)S(1)} all-to-all(bf16[16,3,16,128]{3,2,1,0:T(8,128)(2,1)} %bitcast.20), channel_id=1, replica_groups=mesh['pool'=16,'y'=4,'core'=2,'head'=4] {'pool'}, dimensions={0} | all-to-all | bytes 393216 | tf_op jit(solution)/shard_map/all_to_all | solution.py:348
  35.2 0.0 copy-start.7
  35.2 2.0 %collective-permute-start.3 = (bf16[48,16,128]{2,1,0:T(8,128)(2,1)S(1)}, bf16[48,16,128]{2,1,0:T(8,128)(2,1)S(1)}, u32[]{:S(2)}, u32[]{:S(2)}) collective-permute-start(bf16[48,16,128]{2,1,0:T(8,128)(2,1)S(1)} %bitcast.14), channel_id=1, source_target_pairs={{0,8},{8,0},{16,24},{24,16},{1,9},{9,1},{17,25},{25,17},{2,10},{10... | collective-permute-start | bytes 589832 | tf_op jit(solution)/shard_map/ppermute | solution.py:315
  37.2 7.1 %collective-permute-start.1 = (bf16[4112,128]{1,0:T(8,128)(2,1)}, bf16[4112,128]{1,0:T(8,128)(2,1)S(1)}, u32[]{:S(2)}, u32[]{:S(2)}) collective-permute-start(bf16[4112,128]{1,0:T(8,128)(2,1)} %get-tuple-element.11.refs_1_), channel_id=1, source_target_pairs={{0,4},{4,0},{1,5},{5,1},{2,6},{6,2},{3,7},{7,3},{8,12},{12,8},{9,1... | collective-permute-start | bytes 3158024 | tf_op jit(solution)/shard_map/ppermute | solution.py:315
  44.4 0.0 collective-permute-done.refs_0_
  44.4 1.9 %collective-permute-start.2 = (bf16[4112,128]{1,0:T(8,128)(2,1)S(1)}, bf16[4112,128]{1,0:T(8,128)(2,1)S(1)}, u32[]{:S(2)}, u32[]{:S(2)}) collective-permute-start(bf16[4112,128]{1,0:T(8,128)(2,1)S(1)} %collective-permute-done.refs_0_), channel_id=1, source_target_pairs={{0,4},{4,0},{1,5},{5,1},{2,6},{6,2},{3,7},{7,3},{8,12},{12,8},{9,1... | collective-permute-start | bytes 3158024 | tf_op jit(solution)/shard_map/ppermute | solution.py:315
  46.3 0.0 collective-permute-done.3.q_ref
  46.3 1.2 %attend.4.refs_0_ = bf16[51,16,128]{2,1,0:T(8,128)(2,1)S(1)} custom-call(bf16[48,16,128]{2,1,0:T(8,128)(2,1)S(1)} %collective-permute-done.3.q_ref, bf16[4112,128]{1,0:T(8,128)(2,1)S(1)} %collective-permute-done.refs_0_), custom_call_target="tpu_custom_call" | custom-call | flops 12079595520 | bytes 3000000 | tf_op jit(solution)/shard_map/attend/pallas_call | solution.py:359
  47.5 0.0 collective-permute-done.1.refs_2_
  47.5 1.4 %collective-permute-done.2.refs_3_ = bf16[4112,128]{1,0:T(8,128)(2,1)S(1)} collective-permute-done((bf16[4112,128]{1,0:T(8,128)(2,1)S(1)}, bf16[4112,128]{1,0:T(8,128)(2,1)S(1)}, u32[]{:S(2)}, u32[]{:S(2)}) %collective-permute-start.2) | collective-permute-done | bytes 1052704 | tf_op jit(solution)/shard_map/ppermute | solution.py:315
  48.9 0.0 copy-done.7
  48.9 3.3 %attend.5 = bf16[51,16,128]{2,1,0:T(8,128)(2,1)S(1)} custom-call(bf16[48,16,128]{2,1,0:T(8,128)(2,1)S(1)} %collective-permute-done.3.q_ref, bf16[51,16,128]{2,1,0:T(8,128)(2,1)S(1)} %attend.4.refs_0_, bf16[4112,128]{1,0:T(8,128)(2,1)S(1)} %copy-done.7, bf16[4112,128]{1,0:T(8,128)(2,1)S(1)} %collective-permute-done.1.refs_2_, ...), custom_call_target="tpu_custom_call" | custom-call | flops 1811939328 | bytes 3000000 | tf_op jit(solution)/shard_map/attend/pallas_call | solution.py:359
  52.2 3.5 %collective-permute-start.4 = (bf16[51,16,128]{2,1,0:T(8,128)(2,1)S(1)}, bf16[51,16,128]{2,1,0:T(8,128)(2,1)S(1)}, u32[]{:S(2)}, u32[]{:S(2)}) collective-permute-start(bf16[51,16,128]{2,1,0:T(8,128)(2,1)S(1)} %attend.5), channel_id=1, source_target_pairs={{0,8},{8,0},{16,24},{24,16},{1,9},{9,1},{17,25},{25,17},{2,10},{10... | collective-permute-start | bytes 626696 | tf_op jit(solution)/shard_map/ppermute | solution.py:315
  55.7 4.3 %attend.3.a_ref = bf16[51,16,128]{2,1,0:T(8,128)(2,1)S(1)} custom-call(bf16[48,16,128]{2,1,0:T(8,128)(2,1)S(1)} %bitcast.15, bf16[4112,128]{1,0:T(8,128)(2,1)S(1)} %collective-permute-done.refs_0_, bf16[4112,128]{1,0:T(8,128)(2,1)S(1)} %copy-done.7, bf16[4112,128]{1,0:T(8,128)(2,1)S(1)} %collective-permute-done.1.refs_2_, ...), custom_call_target="tpu_custom_call" | custom-call | flops 2415919104 | bytes 3000000 | tf_op jit(solution)/shard_map/attend/pallas_call | solution.py:359
  60.0 0.0 copy-start.3
  60.0 0.0 copy-start.6
  60.0 0.9 collective-permute-done.4.b_ref
  60.9 1.2 %merge.1 = bf16[896,128]{1,0:T(8,128)(2,1)} custom-call(bf16[51,16,128]{2,1,0:T(8,128)(2,1)S(1)} %attend.3.a_ref, bf16[51,16,128]{2,1,0:T(8,128)(2,1)S(1)} %collective-permute-done.4.b_ref), custom_call_target="tpu_custom_call" | custom-call | bytes 1000000 | tf_op jit(solution)/shard_map/merge/pallas_call | solution.py:377
  62.1 0.0 copy-start.4
  62.1 0.0 copy-start.5
  62.1 4.7 %all-to-all-start.1 = ((bf16[16,56,128]{2,1,0:T(8,128)(2,1)}), bf16[16,56,128]{2,1,0:T(8,128)(2,1)S(1)}, u32[]{:S(2)}, u32[]{:S(2)}) async-start(bf16[16,56,128]{2,1,0:T(8,128)(2,1)} %bitcast.5), calls=%async_computation.1 | async-start | bytes 458752 | tf_op jit(solution)/shard_map/all_to_all | solution.py:387
  66.8 0.0 copy-done.3
  66.8 0.0 copy-done.6
  66.8 0.0 copy-start.1
  66.8 1.0 copy-done.1
  67.9 0.0 copy-start.2
  67.9 1.0 copy-done.2
  68.9 0.0 copy-start
  68.9 4.4 %suffix.1.suffix_hbm = f32[16,32,128]{2,1,0:T(8,128)S(1)} custom-call(s32[16]{0:T(128)S(1)} %copy-done.6, bf16[16,16,128]{2,1,0:T(8,128)(2,1)S(1)} %copy-done.3, bf16[16,128,128]{2,1,0:T(8,128)(2,1)S(1)} %bitcast.12, bf16[16,128,128]{2,1,0:T(8,128)(2,1)S(1)} %bitcast.13), custom_call_target="tpu_custom_call" | custom-call | flops 16777216 | bytes 2000000 | tf_op jit(solution)/shard_map/suffix/pallas_call | solution.py:395
  73.3 6.2 %all-to-all-done.1 = bf16[16,56,128]{2,1,0:T(8,128)(2,1)S(1)} async-done(((bf16[16,56,128]{2,1,0:T(8,128)(2,1)}), bf16[16,56,128]{2,1,0:T(8,128)(2,1)S(1)}, u32[]{:S(2)}, u32[]{:S(2)}) %all-to-all-start.1) | async-done | bytes 229408 | tf_op jit(solution)/shard_map/all_to_all | solution.py:387
  79.6 0.0 copy-done.4
  79.6 0.0 copy-done.5
  79.6 0.9 combine.1
  80.4 7.9 %all_to_all.21.own_ref = bf16[4,16,2048]{2,1,0:T(8,128)(2,1)S(1)} all-to-all(bf16[4,16,2048]{2,1,0:T(8,128)(2,1)S(1)} %combine.1), channel_id=1, replica_groups=mesh['pool'=16,'y'=4,'core'=2,'head'=4] {'y'}, dimensions={0} | all-to-all | bytes 524288 | tf_op jit(solution)/shard_map/all_to_all | solution.py:431
  88.4 9.1 %collective-permute-start.5 = (bf16[4,16,2048]{2,1,0:T(8,128)(2,1)S(1)}, bf16[4,16,2048]{2,1,0:T(8,128)(2,1)S(1)}, u32[]{:S(2)}, u32[]{:S(2)}) collective-permute-start(bf16[4,16,2048]{2,1,0:T(8,128)(2,1)S(1)} %all_to_all.21.own_ref), channel_id=1, source_target_pairs={{0,4},{4,0},{1,5},{5,1},{2,6},{6,2},{3,7},{7,3},{8,12},{12,8},{9,1... | collective-permute-start | bytes 786440 | tf_op jit(solution)/shard_map/ppermute | solution.py:315
  97.5 1.1 %collective-permute-done.5.other_ref = bf16[4,16,2048]{2,1,0:T(8,128)(2,1)S(1)} collective-permute-done((bf16[4,16,2048]{2,1,0:T(8,128)(2,1)S(1)}, bf16[4,16,2048]{2,1,0:T(8,128)(2,1)S(1)}, u32[]{:S(2)}, u32[]{:S(2)}) %collective-permute-start.5) | collective-permute-done | bytes 262176 | tf_op jit(solution)/shard_map/ppermute | solution.py:315
  98.6 0.0 copy-done
  98.6 0.6 project.1
  99.2 8.8 %all_to_all.22 = bf16[4,32,640]{2,1,0:T(8,128)(2,1)S(1)} all-to-all(bf16[4,32,640]{2,1,0:T(8,128)(2,1)S(1)} %bitcast.11), channel_id=1, replica_groups=mesh['pool'=16,'y'=4,'core'=2,'head'=4] {'head'}, dimensions={0} | all-to-all | bytes 327680 | tf_op jit(solution)/shard_map/all_to_all | solution.py:445
  108.0 0.6 reduce_sum.12
Async XLA Ops:
  2.4 41.9 %collective-permute-start = (bf16[4112,128]{1,0:T(8,128)(2,1)}, bf16[4112,128]{1,0:T(8,128)(2,1)S(1)}, u32[]{:S(2)}, u32[]{:S(2)}) collective-permute-start(bf16[4112,128]{1,0:T(8,128)(2,1)} %get-tuple-element.11.refs_1_), channel_id=1, source_target_pairs={{0,24},{8,16},{16,8},{24,0},{1,25},{9,17},{17,9},{25,1},{2,26},{10... | collective-permute-start | bytes 3158024 | tf_op jit(solution)/shard_map/ppermute | solution.py:315
  35.2 13.7 %copy-start.7 = (bf16[4112,128]{1,0:T(8,128)(2,1)S(1)}, bf16[4112,128]{1,0:T(8,128)(2,1)}, u32[]{:S(2)}) copy-start(bf16[4112,128]{1,0:T(8,128)(2,1)} %get-tuple-element.11.refs_1_) | copy-start | bytes 3158020
  35.2 11.1 %collective-permute-start.3 = (bf16[48,16,128]{2,1,0:T(8,128)(2,1)S(1)}, bf16[48,16,128]{2,1,0:T(8,128)(2,1)S(1)}, u32[]{:S(2)}, u32[]{:S(2)}) collective-permute-start(bf16[48,16,128]{2,1,0:T(8,128)(2,1)S(1)} %bitcast.14), channel_id=1, source_target_pairs={{0,8},{8,0},{16,24},{24,16},{1,9},{9,1},{17,25},{25,17},{2,10},{10... | collective-permute-start | bytes 589832 | tf_op jit(solution)/shard_map/ppermute | solution.py:315
  37.2 10.3 %collective-permute-start.1 = (bf16[4112,128]{1,0:T(8,128)(2,1)}, bf16[4112,128]{1,0:T(8,128)(2,1)S(1)}, u32[]{:S(2)}, u32[]{:S(2)}) collective-permute-start(bf16[4112,128]{1,0:T(8,128)(2,1)} %get-tuple-element.11.refs_1_), channel_id=1, source_target_pairs={{0,4},{4,0},{1,5},{5,1},{2,6},{6,2},{3,7},{7,3},{8,12},{12,8},{9,1... | collective-permute-start | bytes 3158024 | tf_op jit(solution)/shard_map/ppermute | solution.py:315
  44.4 4.6 %collective-permute-start.2 = (bf16[4112,128]{1,0:T(8,128)(2,1)S(1)}, bf16[4112,128]{1,0:T(8,128)(2,1)S(1)}, u32[]{:S(2)}, u32[]{:S(2)}) collective-permute-start(bf16[4112,128]{1,0:T(8,128)(2,1)S(1)} %collective-permute-done.refs_0_), channel_id=1, source_target_pairs={{0,4},{4,0},{1,5},{5,1},{2,6},{6,2},{3,7},{7,3},{8,12},{12,8},{9,1... | collective-permute-start | bytes 3158024 | tf_op jit(solution)/shard_map/ppermute | solution.py:315
  52.2 8.8 %collective-permute-start.4 = (bf16[51,16,128]{2,1,0:T(8,128)(2,1)S(1)}, bf16[51,16,128]{2,1,0:T(8,128)(2,1)S(1)}, u32[]{:S(2)}, u32[]{:S(2)}) collective-permute-start(bf16[51,16,128]{2,1,0:T(8,128)(2,1)S(1)} %attend.5), channel_id=1, source_target_pairs={{0,8},{8,0},{16,24},{24,16},{1,9},{9,1},{17,25},{25,17},{2,10},{10... | collective-permute-start | bytes 626696 | tf_op jit(solution)/shard_map/ppermute | solution.py:315
  60.0 6.8 %copy-start.3 = (bf16[16,16,128]{2,1,0:T(8,128)(2,1)S(1)}, bf16[16,16,128]{2,1,0:T(8,128)(2,1)}, u32[]{:S(2)}) copy-start(bf16[16,16,128]{2,1,0:T(8,128)(2,1)} %q_ref) | copy-start | bytes 196612
  60.0 6.8 %copy-start.6 = (s32[16]{0:T(128)S(1)}, s32[16]{0:T(128)}, u32[]{:S(2)}) copy-start(s32[16]{0:T(128)} %length_hbm.1) | copy-start | bytes 196
  62.1 17.5 %copy-start.4 = (s32[16,1]{0,1:T(1,128)S(1)}, s32[16,1]{0,1:T(1,128)}, u32[]{:S(2)}) copy-start(s32[16,1]{0,1:T(1,128)} %param.15) | copy-start | bytes 196
  62.1 17.5 %copy-start.5 = (s32[16]{0:T(128)S(1)}, s32[16]{0:T(128)}, u32[]{:S(2)}) copy-start(s32[16]{0:T(128)} %owner_hbm.3) | copy-start | bytes 196
  62.1 17.4 %all-to-all-start.1 = ((bf16[16,56,128]{2,1,0:T(8,128)(2,1)}), bf16[16,56,128]{2,1,0:T(8,128)(2,1)S(1)}, u32[]{:S(2)}, u32[]{:S(2)}) async-start(bf16[16,56,128]{2,1,0:T(8,128)(2,1)} %bitcast.5), calls=%async_computation.1 | async-start | bytes 458752 | tf_op jit(solution)/shard_map/all_to_all | solution.py:387
  66.8 1.0 copy-start.1
  67.9 1.0 copy-start.2
  68.9 29.7 %copy-start = (bf16[2048,640]{1,0:T(8,128)(2,1)S(1)}, bf16[2048,640]{1,0:T(8,128)(2,1)}, u32[]{:S(2)}) copy-start(bf16[2048,640]{1,0:T(8,128)(2,1)} %w_ref.1) | copy-start | bytes 7864324
  88.4 10.2 %collective-permute-start.5 = (bf16[4,16,2048]{2,1,0:T(8,128)(2,1)S(1)}, bf16[4,16,2048]{2,1,0:T(8,128)(2,1)S(1)}, u32[]{:S(2)}, u32[]{:S(2)}) collective-permute-start(bf16[4,16,2048]{2,1,0:T(8,128)(2,1)S(1)} %all_to_all.21.own_ref), channel_id=1, source_target_pairs={{0,4},{4,0},{1,5},{5,1},{2,6},{6,2},{3,7},{7,3},{8,12},{12,8},{9,1... | collective-permute-start | bytes 786440 | tf_op jit(solution)/shard_map/ppermute | solution.py:315
